TPU v7x, 32 devices: a whole 2x2x4 slice. The times are simulated.
32 devices in a mesh: groups: 2 (over y), expert: 4 (over x, core), tensor: 4 (over z).
Axes of the slice: x: 2, y: 2, z: 4, core: 2. Of those that a mesh axis runs over, the one named last changes fastest.
Arguments:
- context: bfloat16 [4096, 4096], P(('groups', 'expert'), 'tensor'), parts along dimension 0, may hold values from -6 to 6
- o_weight: bfloat16 [4096, 2048], P('tensor'), may hold values from -0.09375 to 0.09375
- resid: bfloat16 [4096, 2048], P(('groups', 'expert', 'tensor')), parts along dimension 0, may hold values from -6 to 6
- norm_gain: float32 [2048], replicated, may hold values from 0.5 to 1.5
- router: bfloat16 [2048, 16], replicated, may hold values from -0.125 to 0.125
- gate_weight: bfloat16 [16, 2048, 768], P(('expert', 'tensor')), may hold values from -0.125 to 0.125
- up_weight: bfloat16 [16, 2048, 768], P(('expert', 'tensor')), may hold values from -0.125 to 0.125
- down_weight: bfloat16 [16, 768, 2048], P(('expert', 'tensor')), may hold values from -0.21875 to 0.21875
- expert_ids: int32 [4096, 4], P(('groups', 'expert', 'tensor')), parts along dimension 0, may hold values from 0 to 15, all different within a row; in each aligned block of 128 rows (0 to 127, 128 to 255, ...) at most 40 rows name the same one
- lengths: int32 [8, 8], P(('groups', 'expert')), parts along dimension 0, may hold values from 1 to 192, 512 in all within a row
Outputs:
- loss_value: float32 [2], P('groups'), parts along dimension 0
- grad_resid: bfloat16 [4096, 2048], P(('groups', 'expert', 'tensor')), parts along dimension 0
There are 2 independent parts, one for each index of `groups`. A program takes and returns all parts, laid end to end along the dimension named above; an argument that names none is the same for every part. Nothing has to cross between parts.
Inputs may be any that keep to these rules, and one draw needn't show every extreme that they name: `expert_ids`: each row names 4 different experts. Within the 128 rows of one device no expert is named more than 40 times, a bound that some block reaches. `lengths`: each row sums to 512 and its largest entry is 192.
All inputs are finite; a program needn't handle non-finite values.
Results may differ from a plain program's by a relative error of at most 0.015.
Values may be sent and summed in bfloat16 or wider, within the bound.
No kernel may reach another device: no remote copies, remote signals or barrier semaphores. Data moves between devices by JAX's collectives and lax.ppermute only.
A program may use at most 128 MiB of HBM per device.

v0:
```python
import jax
import jax.numpy as jnp
from jax import lax
from jax.sharding import PartitionSpec as P

EPSILON = 1e-06
SOFTMAX_WARMTH = 0.05
LOSS_SCALE = 32768.0
EXACT_PRECISION = lax.Precision.HIGHEST


def slot_positions(flat_ids, expert_total):
    onehot = (flat_ids[..., None] == jnp.arange(expert_total, dtype=jnp.int32)).astype(jnp.int32)
    before = jnp.cumsum(onehot, axis=-2) - onehot
    return jnp.sum(before * onehot, axis=-1)


def contract_last(left, right):
    return lax.dot_general(
        left, right, (((1,), (1,)), ((), ())), preferred_element_type=jnp.float32
    )


def contrast(embedded):
    pair_count = embedded.shape[0] // 2
    norms = jnp.sqrt(jnp.sum(embedded * embedded, axis=1, keepdims=True) + EPSILON)
    unit_rows = embedded / norms
    query_rows = unit_rows[0::2]
    passage_rows = unit_rows[1::2]
    similarity_scores = (
        jnp.dot(query_rows, passage_rows.T, precision=EXACT_PRECISION) / SOFTMAX_WARMTH
    )
    exp_scores = jnp.exp(similarity_scores)
    row_total = jnp.sum(exp_scores, axis=1, keepdims=True)
    loss_value = jnp.mean(jnp.log(row_total[:, 0]) - jnp.diagonal(similarity_scores))
    score_gradient = (
        exp_scores / row_total - jnp.eye(pair_count, dtype=similarity_scores.dtype)
    ) * (LOSS_SCALE / pair_count)
    query_gradient = (
        jnp.dot(score_gradient, passage_rows, precision=EXACT_PRECISION) / SOFTMAX_WARMTH
    )
    passage_gradient = (
        jnp.dot(score_gradient.T, query_rows, precision=EXACT_PRECISION) / SOFTMAX_WARMTH
    )
    dunit_rows = jnp.stack([query_gradient, passage_gradient], axis=1).reshape(embedded.shape)
    radial = jnp.sum(unit_rows * dunit_rows, axis=1, keepdims=True)
    return (loss_value, (dunit_rows - unit_rows * radial) / norms)


def body(
    context,
    o_weight,
    resid,
    norm_gain,
    router,
    gate_weight,
    up_weight,
    down_weight,
    expert_ids,
    lengths,
):
    expert_count = lax.axis_size("expert")
    tensor_count = lax.axis_size("tensor")
    device_count = expert_count * tensor_count
    expert_index = lax.axis_index("expert")
    tensor_index = lax.axis_index("tensor")
    local_rows, model_width = resid.shape
    expert_total = router.shape[1]
    top_count = expert_ids.shape[1]
    seq_count = lengths.shape[1]
    seq_total = seq_count * expert_count
    capacity = max(2, local_rows * top_count * 5 // (4 * expert_total))
    attention_out = lax.psum_scatter(
        jnp.dot(context, o_weight, preferred_element_type=jnp.float32).astype(jnp.bfloat16),
        "tensor",
        scatter_dimension=0,
        tiled=True,
    ).astype(jnp.float32)
    resid_mid = resid.astype(jnp.float32) + attention_out
    rms_scale = lax.rsqrt(jnp.mean(resid_mid * resid_mid, axis=1, keepdims=True) + EPSILON)
    normed = (resid_mid * rms_scale * norm_gain).astype(jnp.bfloat16)
    logits = jnp.dot(normed, router, preferred_element_type=jnp.float32)
    expert_onehot = (expert_ids[:, :, None] == jnp.arange(expert_total, dtype=jnp.int32)).astype(
        jnp.float32
    )
    chosen = jnp.sum(logits[:, None, :] * expert_onehot, axis=2)
    exp_chosen = jnp.exp(chosen)
    gate_probs = exp_chosen / jnp.sum(exp_chosen, axis=1, keepdims=True)
    flat_ids = expert_ids.reshape(local_rows * top_count)
    target = flat_ids * capacity + slot_positions(flat_ids, expert_total)

    def move_rows(blocks):
        return lax.all_to_all(blocks, ("expert", "tensor"), split_axis=0, concat_axis=0, tiled=True)

    seq_lengths = lengths[0]
    seq_ends = jnp.cumsum(seq_lengths)
    seq_starts = seq_ends - seq_lengths
    positions = tensor_index * local_rows + jnp.arange(local_rows, dtype=jnp.int32)
    member = (
        (positions[None, :] >= seq_starts[:, None]) & (positions[None, :] < seq_ends[:, None])
    ).astype(jnp.float32)
    tok_len = jnp.sum(member * seq_lengths[:, None].astype(jnp.float32), axis=0)
    repeated = jnp.broadcast_to(normed[:, None, :], (local_rows, top_count, model_width)).reshape(
        local_rows * top_count, model_width
    )
    buffer = (
        jnp.zeros((expert_total * capacity, model_width), jnp.bfloat16).at[target].set(repeated)
    )
    received = move_rows(buffer.reshape(device_count, capacity, model_width)).reshape(
        device_count * capacity, model_width
    )
    pre_gate = jnp.dot(received, gate_weight[0], preferred_element_type=jnp.float32)
    pre_up = jnp.dot(received, up_weight[0], preferred_element_type=jnp.float32)
    hidden = (jax.nn.silu(pre_gate) * pre_up).astype(jnp.bfloat16)
    expert_rows = jnp.dot(hidden, down_weight[0], preferred_element_type=jnp.float32).astype(
        jnp.bfloat16
    )
    seq_local = jnp.dot(jnp.arange(seq_count, dtype=jnp.float32), member, precision=EXACT_PRECISION)
    seq_global = seq_local + (expert_index * seq_count).astype(jnp.float32)
    info_rows = jnp.stack(
        [
            gate_probs,
            jnp.broadcast_to(seq_global[:, None], (local_rows, top_count)),
            jnp.broadcast_to(tok_len[:, None], (local_rows, top_count)),
        ],
        axis=2,
    ).reshape(local_rows * top_count, 3)
    info_init = jnp.zeros((expert_total * capacity, 3), jnp.float32).at[:, 2].set(1.0)
    info_buffer = info_init.at[target].set(info_rows).reshape(device_count, capacity, 3)
    slot_data = lax.all_to_all(
        info_buffer, ("expert", "tensor"), split_axis=0, concat_axis=0, tiled=True
    ).reshape(device_count * capacity, 3)
    slot_gate = slot_data[:, 0:1]
    slot_seq = slot_data[:, 1].astype(jnp.int32)
    slot_len = slot_data[:, 2:3]
    slot_onehot = (slot_seq[:, None] == jnp.arange(seq_total, dtype=jnp.int32)).astype(jnp.float32)
    out_float = expert_rows.astype(jnp.float32)
    expert_part = lax.dot_general(
        slot_onehot,
        slot_gate * out_float / slot_len,
        (((0,), (0,)), ((), ())),
        precision=EXACT_PRECISION,
        preferred_element_type=jnp.float32,
    )
    partial_value = jnp.dot(member, resid_mid / tok_len[:, None], precision=EXACT_PRECISION)
    placed = lax.dynamic_update_slice_in_dim(
        expert_part,
        lax.dynamic_slice_in_dim(expert_part, expert_index * seq_count, seq_count, 0)
        + partial_value,
        expert_index * seq_count,
        0,
    )
    embedded = lax.psum(placed, ("expert", "tensor"))
    loss_value, dembedded = contrast(embedded)
    own_rows = lax.dynamic_slice_in_dim(
        dembedded, expert_index * seq_count, seq_count, 0
    ) / seq_lengths[:, None].astype(jnp.float32)
    dresid_out = lax.dot_general(
        member,
        own_rows,
        (((0,), (0,)), ((), ())),
        precision=EXACT_PRECISION,
        preferred_element_type=jnp.float32,
    )
    slot_dresid = jnp.dot(slot_onehot, dembedded, precision=EXACT_PRECISION) / slot_len
    received_grad = (slot_gate * slot_dresid).astype(jnp.bfloat16)
    slot_dgate = jnp.sum(slot_dresid * out_float, axis=1)
    returned = lax.all_to_all(
        slot_dgate.reshape(device_count, capacity),
        ("expert", "tensor"),
        split_axis=0,
        concat_axis=0,
        tiled=True,
    )
    dgate_prob = returned.reshape(expert_total * capacity)[target].reshape(local_rows, top_count)
    dhidden = contract_last(received_grad, down_weight[0])
    gate_sigmoid = jax.nn.sigmoid(pre_gate)
    dpre_gate = (dhidden * pre_up * gate_sigmoid * (1.0 + pre_gate * (1.0 - gate_sigmoid))).astype(
        jnp.bfloat16
    )
    dpre_up = (dhidden * jax.nn.silu(pre_gate)).astype(jnp.bfloat16)
    dx_rows = (
        contract_last(dpre_gate, gate_weight[0]) + contract_last(dpre_up, up_weight[0])
    ).astype(jnp.bfloat16)
    dx_moe = jnp.sum(
        move_rows(dx_rows.reshape(device_count, capacity, model_width))
        .reshape(expert_total * capacity, model_width)[target]
        .astype(jnp.float32)
        .reshape(local_rows, top_count, model_width),
        axis=1,
    )
    dchosen = gate_probs * (dgate_prob - jnp.sum(gate_probs * dgate_prob, axis=1, keepdims=True))
    dlogits = jnp.sum(dchosen[:, :, None] * expert_onehot, axis=1).astype(jnp.bfloat16)
    dnormed = dx_moe + contract_last(dlogits, router)
    gain_grad = dnormed * norm_gain
    grad_resid = (
        dresid_out
        + rms_scale * gain_grad
        - resid_mid * rms_scale**3 * jnp.mean(gain_grad * resid_mid, axis=1, keepdims=True)
    )
    return (loss_value.reshape(1), grad_resid.astype(jnp.bfloat16))


def solution(mesh):
    in_specs = (
        P(("groups", "expert"), "tensor"),
        P("tensor", None),
        P(("groups", "expert", "tensor"), None),
        P(),
        P(),
        P(("expert", "tensor"), None, None),
        P(("expert", "tensor"), None, None),
        P(("expert", "tensor"), None, None),
        P(("groups", "expert", "tensor"), None),
        P(("groups", "expert"), None),
    )
    out_specs = (P("groups"), P(("groups", "expert", "tensor"), None))
    return jax.shard_map(body, mesh=mesh, in_specs=in_specs, out_specs=out_specs, check_vma=False)
```

profile of v0, /device:TPU:0, one launch (start us, length us, event | category | flops | bytes accessed | tf_op | source)
XLA Modules:
  0.0 395.6 jit_solution(15591593675813145853)
XLA Ops:
  7.2 6.3 %convolution_convert_fusion.1 = bf16[512,2048]{1,0:T(8,128)(2,1)} fusion(bf16[512,1024]{1,0:T(8,128)(2,1)} %param.12, bf16[1024,2048]{1,0:T(8,128)(2,1)} %param.13), kind=kOutput, calls=%fused_computation.23 | convolution fusion | flops 2148532224 | bytes 7340032 | tf_op jit(solution)/shard_map/dot_general | solution.py:74
  16.7 43.7 %reduce-scatter.2.cloned.1.call-done = bf16[128,2048]{1,0:T(8,128)(2,1)} async-done(((bf16[512,2048]{1,0:T(8,128)(2,1)}), bf16[128,2048]{1,0:T(8,128)(2,1)}) %reduce-scatter.2.cloned.1.call-update) | async-done | bytes 524304 | tf_op jit(solution)/shard_map/reduce_scatter | solution.py:73
  60.3 1.5 multiply_reduce_fusion.1
  62.3 1.4 multiply_convert_fusion.5
  66.0 2.3 scatter_fusion
  69.0 4.0 %all-to-all-start = ((f32[16,40,3]{1,2,0:T(4,128)}), f32[16,40,3]{1,2,0:T(4,128)S(1)}, u32[]{:S(2)}, u32[]{:S(2)}) async-start(f32[16,40,3]{1,2,0:T(4,128)} %copy.56), calls=%async_computation.1 | async-start | bytes 65536 | tf_op jit(solution)/shard_map/all_to_all | solution.py:130
  73.1 3.4 broadcast_in_dim.7
  76.5 4.0 %reshape.311 = bf16[512,2048]{1,0:T(8,128)(2,1)} reshape(bf16[128,4,2048]{2,1,0:T(4,128)(2,1)} %broadcast_in_dim.7) | data formatting | bytes 4194304 | tf_op jit(solution)/shard_map/reshape | solution.py:103
  80.5 6.4 %scatter_custom_fusion.1 = bf16[640,2048]{1,0:T(8,128)(2,1)} fusion(s32[512]{0:T(512)S(1)} %bitcast.77, bf16[512,2048]{1,0:T(8,128)(2,1)} %reshape.311, bf16[]{:T(256)} %constant.88.clone.1), kind=kCustom, calls=%fused_computation.44 | custom fusion | bytes 2621952 | tf_op jit(solution)/shard_map/scatter | solution.py:107
  86.9 6.1 %all-to-all-start.1 = ((bf16[16,40,2048]{2,1,0:T(8,128)(2,1)}), bf16[16,40,2048]{2,1,0:T(8,128)(2,1)}, u32[]{:S(2)}, u32[]{:S(2)}) async-start(bf16[16,40,2048]{2,1,0:T(8,128)(2,1)} %bitcast.74), calls=%async_computation.2 | async-start | bytes 5242880 | tf_op jit(solution)/shard_map/all_to_all | solution.py:93
  93.4 60.3 %all-to-all-done.1 = bf16[16,40,2048]{2,1,0:T(8,128)(2,1)} async-done(((bf16[16,40,2048]{2,1,0:T(8,128)(2,1)}), bf16[16,40,2048]{2,1,0:T(8,128)(2,1)}, u32[]{:S(2)}, u32[]{:S(2)}) %all-to-all-start.1) | async-done | bytes 2621472 | tf_op jit(solution)/shard_map/all_to_all | solution.py:93
  153.7 5.0 %fusion.8 = f32[640,768]{1,0:T(8,128)S(1)} fusion(bf16[640,2048]{1,0:T(8,128)(2,1)} %bitcast.9, bf16[1,2048,768]{2,1,0:T(8,128)(2,1)} %param.18), kind=kOutput, calls=%fused_computation.17 | convolution fusion | flops 2013265920 | bytes 7733248 | tf_op jit(solution)/shard_map/dot_general | solution.py:113
  158.8 4.7 %fusion.12 = f32[640,768]{1,0:T(8,128)S(1)} fusion(bf16[640,2048]{1,0:T(8,128)(2,1)} %bitcast.9, bf16[1,2048,768]{2,1,0:T(8,128)(2,1)S(1)} %copy-done.37), kind=kOutput, calls=%fused_computation.21 | convolution fusion | flops 2013265920 | bytes 7733248 | tf_op jit(solution)/shard_map/dot_general | solution.py:112
  163.4 2.2 convolution_convert_fusion
  165.8 2.6 fusion.2
  169.8 87.6 %all-reduce.2.cloned.1.call-done = f32[32,2048]{1,0:T(8,128)} async-done(((f32[32,2048]{1,0:T(8,128)}), f32[32,2048]{1,0:T(8,128)}) %all-reduce.2.cloned.1.call-update) | async-done | bytes 262160 | tf_op jit(solution)/shard_map/psum | solution.py:153
  258.6 1.7 broadcast_divide_fusion
  260.3 1.6 slice.40
  266.6 1.8 reshape.271
  270.7 4.9 %fusion.1 = (f32[640]{0:T(1024)S(1)}, f32[640,2048]{1,0:T(8,128)S(1)}) fusion(bf16[640,2048]{1,0:T(8,128)(2,1)} %copy-done.45, f32[640]{0:T(1024)} %copy-done.23, f32[32,2048]{1,0:T(8,128)S(1)} %subtract_divide_fusion, s32[640]{0:T(1024)} %copy-done.24), kind=kOutput, calls=%fused_computation.8 | convolution fusion | flops 508579200 | bytes 8134144 | tf_op jit(solution)/shard_map/dot_general | solution.py:165
  275.7 2.3 fusion.4
  278.7 5.0 %fusion.10 = f32[640,2048]{1,0:T(8,128)} fusion(bf16[1,2048,768]{2,1,0:T(8,128)(2,1)S(1)} %copy-done.38, f32[640,768]{1,0:T(8,128)S(1)} %copy-done.41, f32[640,768]{1,0:T(8,128)S(1)} %fusion.4, f32[640,768]{1,0:T(8,128)S(1)} %copy-done.44), kind=kOutput, calls=%fused_computation.19 | convolution fusion | flops 2018181120 | bytes 14286848 | tf_op jit(solution)/shard_map/dot_general | solution.py:19
  284.5 5.2 %all-to-all-start.3 = ((f32[16,1,40]{2,1,0:T(1,128)}), f32[16,1,40]{2,1,0:T(1,128)S(1)}, u32[]{:S(2)}, u32[]{:S(2)}) async-start(f32[16,1,40]{2,1,0:T(1,128)} %all_to_all.18), calls=%async_computation.4 | async-start | bytes 16384 | tf_op jit(solution)/shard_map/all_to_all | solution.py:168
  289.7 8.3 %add_convert_fusion = bf16[640,2048]{1,0:T(8,128)(2,1)} fusion(f32[640,2048]{1,0:T(8,128)} %fusion.10, bf16[1,2048,768]{2,1,0:T(8,128)(2,1)} %param.18, f32[640,768]{1,0:T(8,128)} %copy-done.42, f32[640,768]{1,0:T(8,128)} %copy-done.40), kind=kOutput, calls=%fused_computation.9 | convolution fusion | flops 2018836480 | bytes 14942208 | tf_op jit(solution)/shard_map/dot_general | solution.py:19
  298.0 6.2 %all-to-all-start.2 = ((bf16[16,40,2048]{2,1,0:T(8,128)(2,1)}), bf16[16,40,2048]{2,1,0:T(8,128)(2,1)}, u32[]{:S(2)}, u32[]{:S(2)}) async-start(bf16[16,40,2048]{2,1,0:T(8,128)(2,1)} %bitcast.75), calls=%async_computation.3 | async-start | bytes 5242880 | tf_op jit(solution)/shard_map/all_to_all | solution.py:93
  307.5 2.3 gather_fusion.2
  310.0 54.9 %all-to-all-done.2 = bf16[16,40,2048]{2,1,0:T(8,128)(2,1)} async-done(((bf16[16,40,2048]{2,1,0:T(8,128)(2,1)}), bf16[16,40,2048]{2,1,0:T(8,128)(2,1)}, u32[]{:S(2)}, u32[]{:S(2)}) %all-to-all-start.2) | async-done | bytes 2621472 | tf_op jit(solution)/shard_map/all_to_all | solution.py:93
  365.0 7.3 %gather_fusion.1 = bf16[512,2048]{1,0:T(8,128)(2,1)} fusion(bf16[640,2048]{1,0:T(8,128)(2,1)} %bitcast.18, s32[1024]{0:T(1024)S(1)} %pad_clamp_fusion), kind=kCustom, calls=%fused_computation.1 | custom fusion | bytes 4196352 | tf_op jit(solution)/shard_map/gather | solution.py:186
  372.3 4.8 %reshape.276 = f32[128,4,2048]{2,1,0:T(4,128)} reshape(bf16[512,2048]{1,0:T(8,128)(2,1)} %gather_fusion.1) | data formatting | bytes 6291456 | tf_op jit(solution)/shard_map/convert_element_type | solution.py:188
  377.1 5.8 %reduce_sum.138 = f32[128,2048]{1,0:T(8,128)} reduce(f32[128,4,2048]{2,1,0:T(4,128)} %reshape.276, f32[]{:T(128)} %constant.81.clone.1), dimensions={1}, to_apply=%region_16.17 | reduce | flops 786432 | bytes 5242884 | tf_op jit(solution)/shard_map/reduce_sum | solution.py:185
  383.0 2.1 multiply_reduce_fusion
  385.1 2.5 fusion.19
  (161 shorter events, 20.6 us)
Async XLA Ops:
  7.2 156.3 %copy-start = (bf16[1,768,2048]{2,1,0:T(8,128)(2,1)S(1)}, bf16[1,768,2048]{2,1,0:T(8,128)(2,1)}, u32[]{:S(2)}) copy-start(bf16[1,768,2048]{2,1,0:T(8,128)(2,1)} %param.19) | copy-start | bytes 9437188
  7.2 6.4 %copy-start.13 = (s32[128,4]{0,1:T(4,128)S(1)}, s32[128,4]{0,1:T(4,128)}, u32[]{:S(2)}) copy-start(s32[128,4]{0,1:T(4,128)} %param.20) | copy-start | bytes 6148
  7.2 8.4 %copy-start.39 = (s32[1,8]{1,0:T(1,128)S(1)}, s32[1,8]{1,0:T(1,128)}, u32[]{:S(2)}) copy-start(s32[1,8]{1,0:T(1,128)} %param.21) | copy-start | bytes 100
  7.2 53.1 %reduce-scatter.2.cloned.1.call-start = ((), (), s32[]{:S(2)}) async-start(), calls=%async_computation.5 | async-start | bytes 2621440 | tf_op jit(solution)/shard_map/reduce_scatter | solution.py:73
  13.6 48.8 %copy-start.11 = (f32[2048]{0:T(1024)S(1)}, f32[2048]{0:T(1024)}, u32[]{:S(2)}) copy-start(f32[2048]{0:T(1024)} %param.15) | copy-start | bytes 24580
  13.6 51.0 %copy-start.8 = (bf16[2048,16]{0,1:T(8,128)(2,1)S(1)}, bf16[2048,16]{0,1:T(8,128)(2,1)}, u32[]{:S(2)}) copy-start(bf16[2048,16]{0,1:T(8,128)(2,1)} %param.16) | copy-start | bytes 196612
  13.6 52.4 %copy-start.35 = (f32[3]{0:T(128)S(1)}, f32[3]{0:T(128)}, u32[]{:S(2)}) copy-start(f32[3]{0:T(128)} %constant.77.clone.1) | copy-start | bytes 40
  15.8 152.6 %copy-start.27 = (s32[8,1]{0,1:T(1,128)}, s32[8,1]{0,1:T(1,128)S(1)}, u32[]{:S(2)}) copy-start(s32[8,1]{0,1:T(1,128)S(1)} %reduce-window.19) | copy-start | bytes 100
  15.8 152.6 %copy-start.29 = (s32[128]{0:T(128)}, s32[128]{0:T(128)S(1)}, u32[]{:S(2)}) copy-start(s32[128]{0:T(128)S(1)} %iota_add_fusion) | copy-start | bytes 1540
  15.9 152.5 %copy-start.33 = (s32[8]{0:T(128)}, s32[8]{0:T(128)S(1)}, u32[]{:S(2)}) copy-start(s32[8]{0:T(128)S(1)} %bitcast_subtract_fusion) | copy-start | bytes 100
  16.7 63.8 %copy-start.14 = (s32[512,1]{0,1:T(1,128)}, s32[512,1]{0,1:T(1,128)S(1)}, u32[]{:S(2)}) copy-start(s32[512,1]{0,1:T(1,128)S(1)} %compare_select_fusion) | copy-start | bytes 6148
  64.9 4.2 %copy-start.16 = (f32[128]{0:T(128)}, f32[128]{0:T(128)S(1)}, u32[]{:S(2)}) copy-start(f32[128]{0:T(128)S(1)} %exponential_reduce_fusion.1) | copy-start | bytes 1540
  69.0 17.9 %all-to-all-start = ((f32[16,40,3]{1,2,0:T(4,128)}), f32[16,40,3]{1,2,0:T(4,128)S(1)}, u32[]{:S(2)}, u32[]{:S(2)}) async-start(f32[16,40,3]{1,2,0:T(4,128)} %copy.56), calls=%async_computation.1 | async-start | bytes 65536 | tf_op jit(solution)/shard_map/all_to_all | solution.py:130
  86.9 66.8 %all-to-all-start.1 = ((bf16[16,40,2048]{2,1,0:T(8,128)(2,1)}), bf16[16,40,2048]{2,1,0:T(8,128)(2,1)}, u32[]{:S(2)}, u32[]{:S(2)}) async-start(bf16[16,40,2048]{2,1,0:T(8,128)(2,1)} %bitcast.74), calls=%async_computation.2 | async-start | bytes 5242880 | tf_op jit(solution)/shard_map/all_to_all | solution.py:93
  93.0 164.4 %all-reduce.2.cloned.1.call-start = ((), (), s32[]{:S(2)}) async-start(), calls=%async_computation.6 | async-start | bytes 524288 | tf_op jit(solution)/shard_map/psum | solution.py:153
  93.3 72.4 %copy-start.24 = (s32[640]{0:T(1024)}, s32[640]{0:T(1024)S(1)}, u32[]{:S(2)}) copy-start(s32[640]{0:T(1024)S(1)} %fusion.42) | copy-start | bytes 7684
  93.4 72.4 %copy-start.21 = (f32[640]{0:T(1024)}, f32[640]{0:T(1024)S(1)}, u32[]{:S(2)}) copy-start(f32[640]{0:T(1024)S(1)} %get-tuple-element.14) | copy-start | bytes 7684
  93.4 72.4 %copy-start.23 = (f32[640]{0:T(1024)}, f32[640]{0:T(1024)S(1)}, u32[]{:S(2)}) copy-start(f32[640]{0:T(1024)S(1)} %get-tuple-element.15) | copy-start | bytes 7684
  153.7 5.0 %copy-start.37 = (bf16[1,2048,768]{2,1,0:T(8,128)(2,1)S(1)}, bf16[1,2048,768]{2,1,0:T(8,128)(2,1)}, u32[]{:S(2)}) copy-start(bf16[1,2048,768]{2,1,0:T(8,128)(2,1)} %param.17) | copy-start | bytes 9437188
  158.7 4.7 %copy-start.43 = (f32[640,768]{1,0:T(8,128)}, f32[640,768]{1,0:T(8,128)S(1)}, u32[]{:S(2)}) copy-start(f32[640,768]{1,0:T(8,128)S(1)} %fusion.8) | copy-start | bytes 5898244
  257.4 11.0 %copy-start.6 = (f32[32,2048]{1,0:T(8,128)S(1)}, f32[32,2048]{1,0:T(8,128)}, u32[]{:S(2)}) copy-start(f32[32,2048]{1,0:T(8,128)} %all-reduce.2.cloned.1.call-done) | copy-start | bytes 786436
  270.7 5.0 %copy-start.7 = (f32[32,2048]{1,0:T(8,128)}, f32[32,2048]{1,0:T(8,128)S(1)}, u32[]{:S(2)}) copy-start(f32[32,2048]{1,0:T(8,128)S(1)} %subtract_divide_fusion) | copy-start | bytes 786436
  270.7 5.0 %copy-start.22 = (f32[640]{0:T(1024)S(1)}, f32[640]{0:T(1024)}, u32[]{:S(2)}) copy-start(f32[640]{0:T(1024)} %copy-done.21) | copy-start | bytes 7684
  275.7 3.1 copy-start.44
  278.7 5.1 %copy-start.42 = (f32[640,768]{1,0:T(8,128)}, f32[640,768]{1,0:T(8,128)S(1)}, u32[]{:S(2)}) copy-start(f32[640,768]{1,0:T(8,128)S(1)} %fusion.4) | copy-start | bytes 5898244
  284.5 13.5 %all-to-all-start.3 = ((f32[16,1,40]{2,1,0:T(1,128)}), f32[16,1,40]{2,1,0:T(1,128)S(1)}, u32[]{:S(2)}, u32[]{:S(2)}) async-start(f32[16,1,40]{2,1,0:T(1,128)} %all_to_all.18), calls=%async_computation.4 | async-start | bytes 16384 | tf_op jit(solution)/shard_map/all_to_all | solution.py:168
  298.0 6.2 %copy-start.15 = (s32[512,1]{0,1:T(1,128)S(1)}, s32[512,1]{0,1:T(1,128)}, u32[]{:S(2)}) copy-start(s32[512,1]{0,1:T(1,128)} %copy-done.14) | copy-start | bytes 6148
  298.0 6.9 %copy-start.19 = (f32[16]{0:T(128)S(1)}, f32[16]{0:T(128)}, u32[]{:S(2)}) copy-start(f32[16]{0:T(128)} %copy-done.18) | copy-start | bytes 196
  298.0 66.9 %all-to-all-start.2 = ((bf16[16,40,2048]{2,1,0:T(8,128)(2,1)}), bf16[16,40,2048]{2,1,0:T(8,128)(2,1)}, u32[]{:S(2)}, u32[]{:S(2)}) async-start(bf16[16,40,2048]{2,1,0:T(8,128)(2,1)} %bitcast.75), calls=%async_computation.3 | async-start | bytes 5242880 | tf_op jit(solution)/shard_map/all_to_all | solution.py:93
  304.2 5.7 %copy-start.17 = (f32[128]{0:T(128)S(1)}, f32[128]{0:T(128)}, u32[]{:S(2)}) copy-start(f32[128]{0:T(128)} %copy-done.16) | copy-start | bytes 1540
  377.1 5.8 %copy-start.9 = (bf16[2048,16]{0,1:T(8,128)(2,1)S(1)}, bf16[2048,16]{0,1:T(8,128)(2,1)}, u32[]{:S(2)}) copy-start(bf16[2048,16]{0,1:T(8,128)(2,1)} %param.16) | copy-start | bytes 196612
  377.1 5.8 %copy-start.12 = (f32[2048]{0:T(1024)S(1)}, f32[2048]{0:T(1024)}, u32[]{:S(2)}) copy-start(f32[2048]{0:T(1024)} %param.15) | copy-start | bytes 24580
  (20 other events, 40.3 us)
Sparse Core Ops, SparseCore 0:
  13.7 46.5 reduce-scatter.1
  169.9 87.4 all-reduce.1
where the time goes:
time: 397 us; the launch traced here: 396 us
  waiting for transfers between devices  247 us (62%)
  matrix products  49.8 us (13%)
  local copies, waits for them, and re-layouts  43.5 us (11%)
  starting transfers between devices  21.7 us (5%)
  other arithmetic  17.4 us (4%)
  between operations  16.6 us (4%)
    all_to_all x2, waiting for transfers between devices, move_rows(): lax.all_to_all(blocks, ('expert', 'tensor'), split_axis=0, concat_axis=0,...  115 us
    psum x1, waiting for transfers between devices, body(): embedded = lax.psum(placed, ('expert', 'tensor'))  87.6 us
    reduce_scatter x1, waiting for transfers between devices, body(): lax.psum_scatter(jnp.dot(context, o_weight, preferred_element_type=jnp.fl...  43.7 us
    dot_general x4, matrix products, contract_last(): lax.dot_general(left, right, (((1,), (1,)), ((), ())), preferred_element_...  17.7 us
    all_to_all x2, starting transfers between devices, move_rows(): lax.all_to_all(blocks, ('expert', 'tensor'), split_axis=0, concat_axis=0,...  12.2 us
  transfers between devices with their start and end apart: 6, of which 4 were waited for; matrix products, arithmetic and copies ran while one was open for 8% of the time, Pallas kernels for 0%

commit v1 on v0

--- a/solution.py
+++ b/solution.py
@@ -1,6 +1,10 @@
+import functools
+
 import jax
 import jax.numpy as jnp
 from jax import lax
+from jax.experimental import pallas as pl
+from jax.experimental.pallas import tpu as pltpu
 from jax.sharding import PartitionSpec as P
 
 EPSILON = 1e-06
@@ -201,7 +205,480 @@
     return (loss_value.reshape(1), grad_resid.astype(jnp.bfloat16))
 
 
+ROW_EXTRA = 128
+LEAVES_IN = ((0, 1), (3, 2))
+INNER_SWAP = ((1, 2), (2, 1))
+LEAVES_OUT = ((1, 0), (2, 3))
+BLOCK_ORDER = ((3, 2, 1, 0), (3, 0, 2, 1), (0, 3, 1, 2), (0, 1, 2, 3))
+BF16 = jnp.bfloat16
+F32 = jnp.float32
+
+
+def dot_nn(left, right):
+    return lax.dot_general(left, right, (((1,), (0,)), ((), ())), preferred_element_type=F32)
+
+
+def halves(value):
+    high = value.astype(BF16)
+    return high, (value - high.astype(F32)).astype(BF16)
+
+
+def stacked_halves(value):
+    high, low = halves(value)
+    return jnp.concatenate([high.astype(F32), low.astype(F32)], axis=0).astype(BF16)
+
+
+def fold(product):
+    rows = product.shape[0] // 2
+    return product[:rows] + product[rows:]
+
+
+def iota(shape, axis):
+    return lax.broadcasted_iota(jnp.int32, shape, axis)
+
+
+def dispatch_kernel(capacity, numbers, t_ref, gain_ref, router_ref, mask_ref, token_ref, *outs):
+    row_refs, place_ref = outs[:4], outs[4]
+    width = t_ref.shape[1]
+    rows = t_ref.shape[0]
+    experts = router_ref.shape[0]
+    x = t_ref[...].astype(F32)
+    scale = lax.rsqrt(jnp.mean(x * x, axis=1, keepdims=True) + EPSILON)
+    normed = (x * scale * gain_ref[...]).astype(BF16)
+    logits = contract_last(router_ref[...], normed)
+    mask = mask_ref[...]
+    chosen = mask.astype(F32) > 0.5
+    exp_chosen = jnp.where(chosen, jnp.exp(jnp.where(chosen, logits, 0.0)), 0.0)
+    gates = exp_chosen / jnp.sum(exp_chosen, axis=0, keepdims=True)
+    earlier = (iota((rows, rows), 0) < iota((rows, rows), 1)).astype(F32).astype(BF16)
+    position = jnp.where(chosen, dot_nn(mask, earlier), -1.0)
+    gate_high, gate_low = halves(gates)
+    inverse = token_ref[1:2, :]
+    inv_high = inverse.astype(BF16).astype(F32)
+    inv_mid = (inverse - inv_high).astype(BF16).astype(F32)
+    inv_low = inverse - inv_high - inv_mid
+    slot_row = iota((8, rows), 0)
+    token_part = jnp.where(
+        slot_row == 0,
+        token_ref[0:1, :],
+        jnp.where(slot_row == 1, inv_high, jnp.where(slot_row == 2, inv_mid, jnp.where(slot_row == 3, inv_low, 0.0))),
+    )
+    extra = jnp.concatenate(
+        [
+            gate_high.astype(F32),
+            gate_low.astype(F32),
+            token_part,
+            jnp.zeros((ROW_EXTRA - 2 * experts - 8, rows), F32),
+        ],
+        axis=0,
+    ).astype(BF16)
+    expert_row = iota((experts, rows), 0)
+    slot = iota((capacity, rows), 0).astype(F32)
+    picks = []
+    for way in range(4):
+        own = jnp.sum(jnp.where(expert_row == numbers[way], position, 0.0), axis=0, keepdims=True)
+        picks.append((slot == own).astype(F32))
+    picked = jnp.concatenate(picks, axis=0)
+    place_ref[...] = jnp.transpose(picked).astype(BF16)
+    picked = picked.astype(BF16)
+    sent = dot_nn(picked, normed)
+    sent_extra = contract_last(picked, extra)
+    for way in range(4):
+        at = slice(way * capacity, (way + 1) * capacity)
+        row_refs[way][:, :width] = sent[at].astype(BF16)
+        row_refs[way][:, width:] = sent_extra[at].astype(BF16)
+
+
+def expert_kernel(numbers, r0, r1, r2, r3, gate_ref, up_ref, hidden_ref, a_ref, b_ref, pooled_ref, info_ref, x_ref, weight_ref):
+    width = gate_ref.shape[0]
+    experts = 16
+
+    @pl.when(pl.program_id(0) == 0)
+    def _():
+        x_ref[...] = jnp.concatenate([r[:, :width].astype(F32) for r in (r0, r1, r2, r3)], axis=0).astype(BF16)
+        extra = jnp.concatenate([r[:, width:].astype(F32) for r in (r0, r1, r2, r3)], axis=0).astype(BF16)
+        own = numbers[0]
+
+        def mixer(source, goal):
+            gates = (goal < experts) & ((source == goal) | (source == goal + experts))
+            sequence = (goal == experts) & (source == 2 * experts)
+            inverse = (goal == experts + 1) & (source > 2 * experts) & (source < 2 * experts + 4)
+            gate = (goal == experts + 2) & ((source == own) | (source == own + experts))
+            return (gates | sequence | inverse | gate).astype(F32).astype(BF16)
+
+        square = (ROW_EXTRA, ROW_EXTRA)
+        info = dot_nn(extra, mixer(iota(square, 0), iota(square, 1)))
+        info_ref[...] = info
+        turned = contract_last(mixer(iota(square, 1), iota(square, 0)), extra)
+        sequence = turned[experts : experts + 1]
+        weight = turned[experts + 1 : experts + 2] * turned[experts + 2 : experts + 3]
+        pool = jnp.where(iota((pooled_ref.shape[0], extra.shape[0]), 0).astype(F32) == sequence, weight, 0.0)
+        weight_ref[...] = stacked_halves(pool)
+
+    x = x_ref[...]
+    pre_gate = dot_nn(x, gate_ref[...])
+    pre_up = dot_nn(x, up_ref[...])
+    sigmoid = 1.0 / (1.0 + jnp.exp(-pre_gate))
+    silu = pre_gate * sigmoid
+    hidden = (silu * pre_up).astype(BF16)
+    hidden_ref[...] = hidden
+    a_ref[...] = pre_up * sigmoid * (1.0 + pre_gate * (1.0 - sigmoid))
+    b_ref[...] = silu
+    pooled_ref[...] = fold(dot_nn(weight_ref[...], hidden))
+
+
+def embed_kernel(numbers, p0, p1, p2, p3, down_ref, t_ref, token_ref, o0, o1, o2, o3, part_ref):
+    pooled = p0[...] + p1[...] + p2[...] + p3[...]
+    part = fold(dot_nn(stacked_halves(pooled), down_ref[...]))
+    sequences = part.shape[0]
+    own = jnp.where(
+        iota((sequences, t_ref.shape[0]), 0).astype(F32) == token_ref[0:1, :], token_ref[1:2, :], 0.0
+    )
+    part_ref[...] = part + fold(dot_nn(stacked_halves(own), t_ref[...]))
+    rows = o0.shape[0]
+    for way, out in enumerate((o0, o1, o2, o3)):
+        out[...] = part_ref[pl.ds(pl.multiple_of(numbers[way] * rows, rows), rows), :]
+
+
+def contrast_kernel(numbers, q0, q1, q2, q3, down_ref, loss_ref, grad_ref, hidden_grad_ref, all_ref):
+    rows = q0.shape[0]
+    for way, part in enumerate((q0, q1, q2, q3)):
+        all_ref[pl.ds(pl.multiple_of(numbers[way] * rows, rows), rows), :] = part[...]
+    embedded = all_ref[...]
+    count = embedded.shape[0]
+    pairs = count // 2
+    norms = jnp.sqrt(jnp.sum(embedded * embedded, axis=1, keepdims=True) + EPSILON)
+    unit = embedded / norms
+    scores = (
+        lax.dot_general(
+            unit, unit, (((1,), (1,)), ((), ())), precision=EXACT_PRECISION, preferred_element_type=F32
+        )
+        / SOFTMAX_WARMTH
+    )
+    row, column = iota((count, count), 0), iota((count, count), 1)
+    is_pair = (row % 2 == 0) & (column % 2 == 1)
+    matched = is_pair & (column == row + 1)
+    exp_scores = jnp.where(is_pair, jnp.exp(jnp.where(is_pair, scores, 0.0)), 0.0)
+    row_total = jnp.sum(exp_scores, axis=1, keepdims=True)
+    is_query = iota((count, 1), 0) % 2 == 0
+    row_total = jnp.where(is_query, row_total, 1.0)
+    own_score = jnp.sum(jnp.where(matched, scores, 0.0), axis=1, keepdims=True)
+    terms = jnp.where(is_query, jnp.log(row_total) - own_score, 0.0)
+    loss_ref[...] = jnp.broadcast_to(jnp.sum(terms, axis=0, keepdims=True) / pairs, loss_ref.shape)
+    dscore = (exp_scores / row_total - jnp.where(matched, 1.0, 0.0)) * (LOSS_SCALE / pairs)
+    both = dscore + jnp.transpose(dscore)
+    dunit = (
+        lax.dot_general(
+            both, unit, (((1,), (0,)), ((), ())), precision=EXACT_PRECISION, preferred_element_type=F32
+        )
+        / SOFTMAX_WARMTH
+    )
+    radial = jnp.sum(unit * dunit, axis=1, keepdims=True)
+    grad = (dunit - unit * radial) / norms
+    grad_ref[...] = grad
+    hidden_grad_ref[...] = fold(contract_last(stacked_halves(grad), down_ref[...]))
+
+
+def backward_kernel(capacity, numbers, a_ref, b_ref, hidden_ref, info_ref, dh_ref, gate_ref, up_ref, router_ref, o0, o1, o2, o3, dgate_ref, dup_ref, dlog_ref):
+    experts = 16
+
+    @pl.when(pl.program_id(0) == 0)
+    def _():
+        info = info_ref[0]
+        slots = info.shape[0]
+        sequence = info[:, experts : experts + 1]
+        weight = info[:, experts + 1 : experts + 2] * info[:, experts + 2 : experts + 3]
+        member = (iota((slots, dh_ref.shape[0]), 1).astype(F32) == sequence).astype(F32).astype(BF16)
+        high, low = halves(dh_ref[...])
+        dhidden = weight * (dot_nn(member, high) + dot_nn(member, low))
+        dgate_ref[...] = (dhidden * a_ref[0]).astype(BF16)
+        dup_ref[...] = (dhidden * b_ref[0]).astype(BF16)
+        moved = jnp.sum(dhidden * hidden_ref[0].astype(F32), axis=1, keepdims=True)
+        lane = iota((slots, ROW_EXTRA), 1)
+        gates = jnp.where(lane < experts, info, 0.0)
+        dlog_ref[...] = (moved * (jnp.where(lane == numbers[1], 1.0, 0.0) - gates)).astype(BF16)
+
+    total = (
+        contract_last(dgate_ref[...], gate_ref[...])
+        + contract_last(dup_ref[...], up_ref[...])
+        + dot_nn(dlog_ref[...], router_ref[...])
+    )
+    for way, out in enumerate((o0, o1, o2, o3)):
+        out[...] = total[way * capacity : (way + 1) * capacity].astype(BF16)
+
+
+def combine_kernel(numbers, place_ref, r0, r1, r2, r3, out_ref):
+    rows = jnp.concatenate([r[...].astype(F32) for r in (r0, r1, r2, r3)], axis=0).astype(BF16)
+    out_ref[...] = dot_nn(place_ref[0], rows)
+
+
+def finish_kernel(t_ref, gain_ref, grad_ref, token_ref, own_ref, r4, r5, r6, out_ref):
+    x = t_ref[...].astype(F32)
+    scale = lax.rsqrt(jnp.mean(x * x, axis=1, keepdims=True) + EPSILON)
+    sequences = grad_ref.shape[0]
+    spread = jnp.where(
+        iota((sequences, x.shape[0]), 0).astype(F32) == token_ref[0:1, :], 1.0, 0.0
+    )
+    spread = jnp.transpose(spread).astype(BF16)
+    inverse = jnp.transpose(token_ref[...])[:, 1:2]
+    high, low = halves(grad_ref[...])
+    dresid = inverse * (dot_nn(spread, high) + dot_nn(spread, low))
+    dnormed = own_ref[...] + r4[...].astype(F32) + r5[...].astype(F32) + r6[...].astype(F32)
+    gained = dnormed * gain_ref[...]
+    out = dresid + scale * gained - x * (scale * scale * scale) * jnp.mean(gained * x, axis=1, keepdims=True)
+    out_ref[...] = out.astype(BF16)
+
+
+def whole_call(kernel, outs, *args, scratch=(), numbers=0, limit=40, flops=0):
+    spec = pl.BlockSpec(memory_space=pltpu.VMEM)
+    smem = pl.BlockSpec(memory_space=pltpu.SMEM)
+    moved = sum(a.size * a.dtype.itemsize for a in args)
+    return pl.pallas_call(
+        kernel,
+        out_shape=outs,
+        in_specs=[smem] * numbers + [spec] * (len(args) - numbers),
+        out_specs=jax.tree.map(lambda _: spec, outs),
+        scratch_shapes=scratch,
+        compiler_params=pltpu.CompilerParams(vmem_limit_bytes=limit * 2**20),
+        cost_estimate=pl.CostEstimate(flops=flops, bytes_accessed=moved, transcendentals=0),
+    )(*args)
+
+
+def fast_body(context, o_weight, resid, norm_gain, router, gate_weight, up_weight, down_weight, expert_ids, lengths):
+    e = lax.axis_index("expert")
+    z = lax.axis_index("tensor")
+    rows, width = resid.shape
+    experts = router.shape[1]
+    top = expert_ids.shape[1]
+    seq_count = lengths.shape[1]
+    sequences = 4 * seq_count
+    hidden_width = gate_weight.shape[2]
+    capacity = max(2, rows * top * 5 // (4 * experts))
+    slots = 4 * capacity
+    is_leaf = (z == 0) | (z == 3)
+    ways = e ^ jnp.arange(4, dtype=jnp.int32)
+    way_experts = ways * 4 + z
+    own_expert = (e * 4 + z).astype(jnp.int32)
+    gate_w, up_w, down_w = gate_weight[0], up_weight[0], down_weight[0]
+    gain = norm_gain.reshape(1, width)
+    router_turned = router.T
+    router_rows = jnp.zeros((ROW_EXTRA, width), BF16).at[:experts].set(router_turned)
+
+    def along_z(value, pairs):
+        return lax.ppermute(value, "tensor", pairs)
+
+    def swap_z(value, bits):
+        return lax.ppermute(value, "tensor", [(i, i ^ bits) for i in range(4)])
+
+    def swap_e(value, bits):
+        return lax.ppermute(value, "expert", [(i, i ^ bits) for i in range(4)])
+
+    mask_own = jnp.sum(
+        (expert_ids[None, :, :] == jnp.arange(experts, dtype=jnp.int32)[:, None, None]).astype(F32), axis=2
+    )
+    mask_wide = jnp.concatenate([jnp.where(z == c, mask_own, 0.0) for c in range(4)], axis=1).astype(BF16)
+    mask_sum = mask_wide + along_z(mask_wide, LEAVES_IN)
+    mask_sum = mask_sum + along_z(mask_sum, INNER_SWAP)
+    mask_back = along_z(mask_sum, LEAVES_OUT)
+    mask_all = jnp.where(is_leaf, mask_back, mask_sum)
+
+    seq_lengths = lengths[0]
+    seq_ends = jnp.cumsum(seq_lengths)
+    places = jnp.arange(4 * rows, dtype=jnp.int32)
+    after = places[None, :] >= seq_ends[:, None]
+    seq_local = jnp.sum(after.astype(jnp.int32), axis=0)
+    token_len = jnp.sum(
+        jnp.where(seq_local[None, :] == jnp.arange(seq_count, dtype=jnp.int32)[:, None], seq_lengths[:, None], 0), axis=0
+    )
+    token_info = jnp.concatenate(
+        [
+            (seq_local + e * seq_count).astype(F32)[None],
+            (1.0 / token_len.astype(F32))[None],
+            jnp.zeros((6, 4 * rows), F32),
+        ],
+        axis=0,
+    )
+    token_own = lax.dynamic_slice_in_dim(token_info, z * rows, rows, 1)
+
+    totals, received, placed = [], [], []
+    for c in range(4):
+        part = jnp.dot(context[c * rows : (c + 1) * rows], o_weight, preferred_element_type=F32)
+        part = (part + jnp.where(z == c, resid.astype(F32), 0.0)).astype(BF16)
+        arrived = along_z(part, LEAVES_IN)
+        half = (part.astype(F32) + arrived.astype(F32)).astype(BF16)
+        other = along_z(half, INNER_SWAP)
+        total = (half.astype(F32) + other.astype(F32)).astype(BF16)
+        back = along_z(total, LEAVES_OUT)
+        total = jnp.where(is_leaf, back, total)
+        totals.append(total)
+        *sent, place = whole_call(
+            functools.partial(dispatch_kernel, capacity),
+            [jax.ShapeDtypeStruct((capacity, width + ROW_EXTRA), BF16)] * 4
+            + [jax.ShapeDtypeStruct((rows, slots), BF16)],
+            way_experts,
+            total,
+            gain,
+            router_turned,
+            mask_all[:, c * rows : (c + 1) * rows],
+            token_info[:, c * rows : (c + 1) * rows],
+            numbers=1,
+            flops=2 * slots * rows * width,
+        )
+        placed.append(place)
+        received.append([sent[0]] + [swap_e(sent[way], way) for way in (1, 2, 3)])
+
+    tile = 256
+    hiddens, a_parts, b_parts, pools, infos = [], [], [], [], []
+    for c in range(4):
+        whole = pl.BlockSpec((capacity, width + ROW_EXTRA), lambda j, n: (0, 0))
+        hid, a, b, pool, info = pl.pallas_call(
+            expert_kernel,
+            out_shape=[
+                jax.ShapeDtypeStruct((slots, hidden_width), BF16),
+                jax.ShapeDtypeStruct((slots, hidden_width), F32),
+                jax.ShapeDtypeStruct((slots, hidden_width), F32),
+                jax.ShapeDtypeStruct((sequences, hidden_width), F32),
+                jax.ShapeDtypeStruct((slots, ROW_EXTRA), F32),
+            ],
+            grid_spec=pltpu.PrefetchScalarGridSpec(
+                num_scalar_prefetch=1,
+                grid=(hidden_width // tile,),
+                in_specs=[whole] * 4 + [pl.BlockSpec((width, tile), lambda j, n: (0, j))] * 2,
+                out_specs=[
+                    pl.BlockSpec((slots, tile), lambda j, n: (0, j)),
+                    pl.BlockSpec((slots, tile), lambda j, n: (0, j)),
+                    pl.BlockSpec((slots, tile), lambda j, n: (0, j)),
+                    pl.BlockSpec((sequences, tile), lambda j, n: (0, j)),
+                    pl.BlockSpec((slots, ROW_EXTRA), lambda j, n: (0, 0)),
+                ],
+                scratch_shapes=[pltpu.VMEM((slots, width), BF16), pltpu.VMEM((2 * sequences, slots), BF16)],
+            ),
+            compiler_params=pltpu.CompilerParams(vmem_limit_bytes=40 * 2**20),
+            cost_estimate=pl.CostEstimate(
+                flops=4 * slots * width * hidden_width, bytes_accessed=4 * width * hidden_width, transcendentals=0
+            ),
+        )(own_expert.reshape(1), *received[c], gate_w, up_w)
+        hiddens.append(hid)
+        a_parts.append(a)
+        b_parts.append(b)
+        pools.append(pool)
+        infos.append(info)
+
+    total_own = lax.select_n(z, *totals)
+    seq_shape = jax.ShapeDtypeStruct((seq_count, width), F32)
+    quarters = whole_call(
+        embed_kernel,
+        [seq_shape] * 4,
+        ways,
+        *pools,
+        down_w,
+        total_own,
+        token_own,
+        scratch=[pltpu.VMEM((sequences, width), F32)],
+        numbers=1,
+        flops=4 * sequences * hidden_width * width,
+    )
+    mine = (quarters[0] + swap_e(quarters[1], 1)) + (swap_e(quarters[2], 2) + swap_e(quarters[3], 3))
+    mine = (mine + swap_z(mine, 1)) + (swap_z(mine, 2) + swap_z(mine, 3))
+    pieces = [mine] + [swap_e(mine, way) for way in (1, 2, 3)]
+    loss, dembedded, hidden_grad = whole_call(
+        contrast_kernel,
+        [
+            jax.ShapeDtypeStruct((1, 128), F32),
+            jax.ShapeDtypeStruct((sequences, width), F32),
+            jax.ShapeDtypeStruct((sequences, hidden_width), F32),
+        ],
+        ways,
+        *pieces,
+        down_w,
+        scratch=[pltpu.VMEM((sequences, width), F32)],
+        numbers=1,
+        flops=4 * sequences * hidden_width * width,
+    )
+
+    hidden_all, a_all, b_all, info_all = (jnp.stack(part) for part in (hiddens, a_parts, b_parts, infos))
+    place_all = jnp.stack(placed)
+    order = jnp.asarray(BLOCK_ORDER, jnp.int32)[z]
+    tile = 512
+    sums = []
+    for j in range(4):
+        numbers = jnp.stack([order[j], own_expert])
+        block = lambda shape: pl.BlockSpec((1,) + shape, lambda i, n: (n[0], 0, 0))
+        out_spec = pl.BlockSpec((capacity, tile), lambda i, n: (0, i))
+        grads = pl.pallas_call(
+            functools.partial(backward_kernel, capacity),
+            out_shape=[jax.ShapeDtypeStruct((capacity, width), BF16)] * 4,
+            grid_spec=pltpu.PrefetchScalarGridSpec(
+                num_scalar_prefetch=1,
+                grid=(width // tile,),
+                in_specs=[
+                    block((slots, hidden_width)),
+                    block((slots, hidden_width)),
+                    block((slots, hidden_width)),
+                    block((slots, ROW_EXTRA)),
+                    pl.BlockSpec((sequences, hidden_width), lambda i, n: (0, 0)),
+                    pl.BlockSpec((tile, hidden_width), lambda i, n: (i, 0)),
+                    pl.BlockSpec((tile, hidden_width), lambda i, n: (i, 0)),
+                    pl.BlockSpec((ROW_EXTRA, tile), lambda i, n: (0, i)),
+                ],
+                out_specs=[out_spec] * 4,
+                scratch_shapes=[
+                    pltpu.VMEM((slots, hidden_width), BF16),
+                    pltpu.VMEM((slots, hidden_width), BF16),
+                    pltpu.VMEM((slots, ROW_EXTRA), BF16),
+                ],
+            ),
+            compiler_params=pltpu.CompilerParams(vmem_limit_bytes=40 * 2**20),
+            cost_estimate=pl.CostEstimate(
+                flops=4 * slots * width * hidden_width, bytes_accessed=4 * width * hidden_width, transcendentals=0
+            ),
+        )(numbers, a_all, b_all, hidden_all, info_all, hidden_grad, gate_w, up_w, router_rows)
+        back = [grads[0]] + [swap_e(grads[way], way) for way in (1, 2, 3)]
+        rows_spec = pl.BlockSpec((capacity, width), lambda i, n: (0, 0))
+        summed = pl.pallas_call(
+            combine_kernel,
+            out_shape=jax.ShapeDtypeStruct((rows, width), F32),
+            grid_spec=pltpu.PrefetchScalarGridSpec(
+                num_scalar_prefetch=1,
+                grid=(1,),
+                in_specs=[pl.BlockSpec((1, rows, slots), lambda i, n: (n[0], 0, 0))] + [rows_spec] * 4,
+                out_specs=pl.BlockSpec((rows, width), lambda i, n: (0, 0)),
+            ),
+            compiler_params=pltpu.CompilerParams(vmem_limit_bytes=40 * 2**20),
+            cost_estimate=pl.CostEstimate(
+                flops=2 * slots * rows * width, bytes_accessed=8 * rows * width, transcendentals=0
+            ),
+        )(numbers, place_all, *back)
+        sums.append(summed)
+
+    def narrow(value):
+        return value.astype(BF16)
+
+    got1 = along_z(narrow(sums[0]), LEAVES_IN)
+    got2 = along_z(narrow(sums[1]), LEAVES_IN)
+    got3 = along_z(narrow(sums[0] + got1.astype(F32)), INNER_SWAP)
+    got4 = along_z(narrow(sums[2]), LEAVES_IN)
+    got5 = along_z(narrow(sums[2] + got2.astype(F32)), INNER_SWAP)
+    got6 = along_z(narrow(sums[1] + got3.astype(F32)), LEAVES_OUT)
+    grad = whole_call(
+        finish_kernel,
+        jax.ShapeDtypeStruct((rows, width), BF16),
+        total_own,
+        gain,
+        dembedded,
+        token_own,
+        sums[3],
+        got4,
+        got5,
+        got6,
+        flops=4 * rows * sequences * width,
+    )
+    return loss[0, :1], grad
+
+
 def solution(mesh):
+    shape = dict(mesh.shape)
+    part_body = fast_body if (shape["expert"], shape["tensor"]) == (4, 4) else body
     in_specs = (
         P(("groups", "expert"), "tensor"),
         P("tensor", None),
@@ -215,4 +692,4 @@
         P(("groups", "expert"), None),
     )
     out_specs = (P("groups"), P(("groups", "expert", "tensor"), None))
-    return jax.shard_map(body, mesh=mesh, in_specs=in_specs, out_specs=out_specs, check_vma=False)
+    return jax.shard_map(part_body, mesh=mesh, in_specs=in_specs, out_specs=out_specs, check_vma=False)

time: 397 us -> 283 us (0.71)
  waiting for transfers between devices: 247 us -> 139 us
  Pallas kernels: 0 us -> 46 us
  starting transfers between devices: 21.7 us -> 64.2 us
  matrix products: 49.8 us -> 12.2 us
  local copies, waits for them, and re-layouts: 43.5 us -> 7.78 us
  between operations: 16.6 us -> 1.51 us
  other arithmetic: 17.4 us -> 11.4 us
    ppermute x0 -> x54, waiting for transfers between devices: none -> 139 us  [the longest x21 94.2 us: along_z(): return lax.ppermute(value, 'tensor', pairs)]
    all_to_all x4 -> x0, waiting for transfers between devices: 115 us -> none  [the longest x2 115 us: move_rows(): lax.all_to_all(blocks, ('expert', 'tensor'), split_axis=0, concat_axis=0,...]
    psum x1 -> x0, waiting for transfers between devices: 87.6 us -> none  [body(): embedded = lax.psum(placed, ('expert', 'tensor'))]
    ppermute x0 -> x54, starting transfers between devices: none -> 64.2 us  [the longest x21 39.9 us: along_z(): return lax.ppermute(value, 'tensor', pairs)]
    pallas_call x0 -> x19, Pallas kernels: none -> 46 us  [the longest x4 16.3 us: fast_body(): pl.pallas_call(functools.partial(backward_kernel, capacity), out_shape=[j...]
    reduce_scatter x1 -> x0, waiting for transfers between devices: 43.7 us -> none  [body(): lax.psum_scatter(jnp.dot(context, o_weight, preferred_element_type=jnp.fl...]
    dot_general x17 -> x4, matrix products: 49.8 us -> 12.2 us  [fast_body(): jnp.dot(context[c * rows:(c + 1) * rows], o_weight, preferred_element_typ...]
    all_to_all x4 -> x0, starting transfers between devices: 21.5 us -> none  [the longest x2 12.2 us: move_rows(): lax.all_to_all(blocks, ('expert', 'tensor'), split_axis=0, concat_axis=0,...]
  transfers between devices with their start and end apart: 6 -> 54, of which waited for: 4 -> 23; matrix products, arithmetic and copies ran while one was open for 8% -> 7% of each run, Pallas kernels for 0% -> 11%
where the time goes in v1:
time: 283 us; the launch traced here: 282 us
  waiting for transfers between devices  139 us (49%)
  starting transfers between devices  64.2 us (23%)
  Pallas kernels  46 us (16%)
  matrix products  12.2 us (4%)
  other arithmetic  11.4 us (4%)
  local copies, waits for them, and re-layouts  7.78 us (3%)
    ppermute x21, waiting for transfers between devices, along_z(): return lax.ppermute(value, 'tensor', pairs)  94.2 us
    ppermute x30, waiting for transfers between devices, swap_e(): return lax.ppermute(value, 'expert', [(i, i ^ bits) for i in range(4)])  40.1 us
    ppermute x21, starting transfers between devices, along_z(): return lax.ppermute(value, 'tensor', pairs)  39.9 us
    ppermute x30, starting transfers between devices, swap_e(): return lax.ppermute(value, 'expert', [(i, i ^ bits) for i in range(4)])  19.8 us
    pallas_call x4, Pallas kernels, fast_body(): pl.pallas_call(functools.partial(backward_kernel, capacity), out_shape=[j...  16.3 us
    pallas_call x4, Pallas kernels, fast_body(): pl.pallas_call(expert_kernel, out_shape=[jax.ShapeDtypeStruct((slots, hid...  13.4 us
    pallas_call x7, Pallas kernels, whole_call(): pl.pallas_call(kernel, out_shape=outs, in_specs=[smem] * numbers + [spec]...  12.9 us
    dot_general x4, matrix products, fast_body(): jnp.dot(context[c * rows:(c + 1) * rows], o_weight, preferred_element_typ...  12.2 us
  transfers between devices with their start and end apart: 54, of which 23 were waited for; matrix products, arithmetic and copies ran while one was open for 7% of the time, Pallas kernels for 11%

profile of v1, /device:TPU:0, one launch (start us, length us, event | category | flops | bytes accessed | tf_op | source)
XLA Modules:
  0.0 282.0 jit_solution(6374050022631908593)
XLA Ops:
  0.6 3.2 %fusion = bf16[128,2048]{1,0:T(8,128)(2,1)S(1)} fusion(bf16[1024,2048]{1,0:T(8,128)(2,1)} %param.14, bf16[128,2048]{1,0:T(8,128)(2,1)} %param.15, pred[]{:T(512)S(6)} %eq.20, bf16[512,1024]{1,0:T(8,128)(2,1)} %param.13), kind=kOutput, calls=%fused_computation.4 | convolution fusion | flops 537919488 | bytes 5505025 | tf_op jit(solution)/shard_map/dot_general | solution.py:505
  3.8 5.7 %collective-permute-start = (bf16[128,2048]{1,0:T(8,128)(2,1)S(1)}, bf16[128,2048]{1,0:T(8,128)(2,1)}, u32[]{:S(2)}, u32[]{:S(2)}) collective-permute-start(bf16[128,2048]{1,0:T(8,128)(2,1)S(1)} %fusion), channel_id=1, source_target_pairs={{0,1},{3,2},{4,5},{7,6},{8,9},{11,10},{12,13},{15,14},{16,17},{19,... | collective-permute-start | bytes 1572872 | tf_op jit(solution)/shard_map/ppermute | solution.py:468
  9.5 3.0 %fusion.3 = bf16[128,2048]{1,0:T(8,128)(2,1)S(1)} fusion(bf16[1024,2048]{1,0:T(8,128)(2,1)} %param.14, bf16[128,2048]{1,0:T(8,128)(2,1)S(1)} %copy-done.13, pred[]{:T(512)S(6)} %eq.21, bf16[512,1024]{1,0:T(8,128)(2,1)} %param.13), kind=kOutput, calls=%fused_computation.7 | convolution fusion | flops 537919488 | bytes 5505025 | tf_op jit(solution)/shard_map/dot_general | solution.py:505
  14.7 3.0 %fusion.1 = bf16[128,2048]{1,0:T(8,128)(2,1)S(1)} fusion(bf16[1024,2048]{1,0:T(8,128)(2,1)} %param.14, bf16[128,2048]{1,0:T(8,128)(2,1)S(1)} %copy-done.13, pred[]{:T(512)S(6)} %eq.49, bf16[512,1024]{1,0:T(8,128)(2,1)} %param.13), kind=kOutput, calls=%fused_computation.5 | convolution fusion | flops 537919488 | bytes 5505025 | tf_op jit(solution)/shard_map/dot_general | solution.py:505
  19.8 3.0 %fusion.2 = bf16[128,2048]{1,0:T(8,128)(2,1)S(1)} fusion(bf16[1024,2048]{1,0:T(8,128)(2,1)} %param.14, bf16[128,2048]{1,0:T(8,128)(2,1)S(1)} %copy-done.13, pred[]{:T(512)S(6)} %eq.50, bf16[512,1024]{1,0:T(8,128)(2,1)} %param.13), kind=kOutput, calls=%fused_computation.6 | convolution fusion | flops 537919488 | bytes 5505025 | tf_op jit(solution)/shard_map/dot_general | solution.py:505
  26.1 27.9 %collective-permute-done.3 = bf16[16,512]{1,0:T(8,128)(2,1)S(1)} collective-permute-done((bf16[16,512]{1,0:T(8,128)(2,1)S(1)}, bf16[16,512]{1,0:T(8,128)(2,1)S(1)}, u32[]{:S(2)}, u32[]{:S(2)}) %collective-permute-start.3) | collective-permute-done | bytes 16416 | tf_op jit(solution)/shard_map/ppermute | solution.py:468
  69.2 22.0 %collective-permute-done.2 = bf16[128,2048]{1,0:T(8,128)(2,1)S(1)} collective-permute-done((bf16[128,2048]{1,0:T(8,128)(2,1)S(1)}, bf16[128,2048]{1,0:T(8,128)(2,1)S(1)}, u32[]{:S(2)}, u32[]{:S(2)}) %collective-permute-start.2) | collective-permute-done | bytes 524320 | tf_op jit(solution)/shard_map/ppermute | solution.py:468
  91.3 11.3 %collective-permute-done.23 = bf16[128,2048]{1,0:T(8,128)(2,1)} collective-permute-done((bf16[128,2048]{1,0:T(8,128)(2,1)S(1)}, bf16[128,2048]{1,0:T(8,128)(2,1)}, u32[]{:S(2)}, u32[]{:S(2)}) %collective-permute-start.23) | collective-permute-done | bytes 524320 | tf_op jit(solution)/shard_map/ppermute | solution.py:468
  102.6 11.2 %collective-permute-done.11 = bf16[128,2048]{1,0:T(8,128)(2,1)} collective-permute-done((bf16[128,2048]{1,0:T(8,128)(2,1)S(1)}, bf16[128,2048]{1,0:T(8,128)(2,1)}, u32[]{:S(2)}, u32[]{:S(2)}) %collective-permute-start.11) | collective-permute-done | bytes 524320 | tf_op jit(solution)/shard_map/ppermute | solution.py:468
  113.9 9.9 %collective-permute-done.17 = bf16[128,2048]{1,0:T(8,128)(2,1)} collective-permute-done((bf16[128,2048]{1,0:T(8,128)(2,1)S(1)}, bf16[128,2048]{1,0:T(8,128)(2,1)}, u32[]{:S(2)}, u32[]{:S(2)}) %collective-permute-start.17) | collective-permute-done | bytes 524320 | tf_op jit(solution)/shard_map/ppermute | solution.py:468
  123.7 2.9 %select_select_fusion = (bf16[128,2048]{1,0:T(8,128)(2,1)}, bf16[128,2048]{1,0:T(8,128)(2,1)S(1)}, bf16[128,2048]{1,0:T(8,128)(2,1)S(1)}, bf16[128,2048]{1,0:T(8,128)(2,1)}, bf16[128,2048]{1,0:T(8,128)(2,1)}) fusion(pred[]{:T(512)S(6)} %select_n.146, pred[]{:T(512)S(6)} %select_n.143, pred[]{:T(512)S(6)} %select_n.141, ...), kind=kLoop, calls=%fused_computation.26 | loop fusion | flops 1835008 | bytes 6815748 | tf_op jit(solution)/shard_map/select_n | solution.py:567
  146.9 3.9 %shard_map.129 = (bf16[160,768]{1,0:T(8,128)(2,1)S(1)}, f32[160,768]{1,0:T(8,128)S(1)}, f32[160,768]{1,0:T(8,128)S(1)}, f32[32,768]{1,0:T(8,128)S(1)}, f32[160,128]{1,0:T(8,128)S(1)}) custom-call(s32[1]{0:T(128)} %bitcast.numbers, bf16[40,2176]{1,0:T(8,128)(2,1)S(1)} %copy-done.10, bf16[40,2176]{1,0:T(8,128)(2,1)} %collective-permute-done.24.r1, ...), custom_call_target="tpu_custom_call" | custom-call | flops 1006632960 | bytes 6291456 | tf_op jit(solution)/shard_map/pallas_call | solution.py:534
  153.0 3.7 %shard_map.127 = (bf16[160,768]{1,0:T(8,128)(2,1)S(1)}, f32[160,768]{1,0:T(8,128)S(1)}, f32[160,768]{1,0:T(8,128)S(1)}, f32[32,768]{1,0:T(8,128)S(1)}, f32[160,128]{1,0:T(8,128)S(1)}) custom-call(s32[1]{0:T(128)} %bitcast.numbers, bf16[40,2176]{1,0:T(8,128)(2,1)S(1)} %get-tuple-element.87.r0, bf16[40,2176]{1,0:T(8,128)(2,1)} %collective-permute-done.18.r1, ...), custom_call_target="tpu_custom_call" | custom-call | flops 1006632960 | bytes 6291456 | tf_op jit(solution)/shard_map/pallas_call | solution.py:534
  156.8 2.9 %shard_map.125 = (bf16[160,768]{1,0:T(8,128)(2,1)S(1)}, f32[160,768]{1,0:T(8,128)S(1)}, f32[160,768]{1,0:T(8,128)S(1)}, f32[32,768]{1,0:T(8,128)S(1)}, f32[160,128]{1,0:T(8,128)S(1)}) custom-call(s32[1]{0:T(128)} %bitcast.numbers, bf16[40,2176]{1,0:T(8,128)(2,1)S(1)} %get-tuple-element.82.r0, bf16[40,2176]{1,0:T(8,128)(2,1)S(1)} %collective-permute-done.12.r1, ...), custom_call_target="tpu_custom_call" | custom-call | flops 1006632960 | bytes 6291456 | tf_op jit(solution)/shard_map/pallas_call | solution.py:534
  161.3 2.9 %shard_map.123 = (bf16[160,768]{1,0:T(8,128)(2,1)S(1)}, f32[160,768]{1,0:T(8,128)S(1)}, f32[160,768]{1,0:T(8,128)S(1)}, f32[32,768]{1,0:T(8,128)S(1)}, f32[160,128]{1,0:T(8,128)S(1)}) custom-call(s32[1]{0:T(128)} %bitcast.numbers, bf16[40,2176]{1,0:T(8,128)(2,1)S(1)} %get-tuple-element.77.r0, bf16[40,2176]{1,0:T(8,128)(2,1)S(1)} %collective-permute-done.6.r1, ...), custom_call_target="tpu_custom_call" | custom-call | flops 1006632960 | bytes 6291456 | tf_op jit(solution)/shard_map/pallas_call | solution.py:534
  172.1 3.0 %collective-permute-start.31 = (f32[8,2048]{1,0:T(8,128)S(1)}, f32[8,2048]{1,0:T(8,128)S(1)}, u32[]{:S(2)}, u32[]{:S(2)}) collective-permute-start(f32[8,2048]{1,0:T(8,128)S(1)} %add_add_fusion.1), channel_id=1, source_target_pairs={{0,2},{1,3},{2,0},{3,1},{4,6},{5,7},{6,4},{7,5},{8,10},{9,11},{10,... | collective-permute-start | bytes 196616 | tf_op jit(solution)/shard_map/ppermute | solution.py:471
  183.3 3.1 %collective-permute-done.34.q2 = f32[8,2048]{1,0:T(8,128)S(1)} collective-permute-done((f32[8,2048]{1,0:T(8,128)S(1)}, f32[8,2048]{1,0:T(8,128)S(1)}, u32[]{:S(2)}, u32[]{:S(2)}) %collective-permute-start.34) | collective-permute-done | bytes 65568 | tf_op jit(solution)/shard_map/ppermute | solution.py:474
  186.8 3.3 %shard_map.131 = (f32[1,128]{1,0:T(1,128)}, f32[32,2048]{1,0:T(8,128)S(1)}, f32[32,768]{1,0:T(8,128)S(1)}) custom-call(s32[4]{0:T(128)S(1)} %iota_xor_fusion.numbers, f32[8,2048]{1,0:T(8,128)S(1)} %add_add_fusion.q0, f32[8,2048]{1,0:T(8,128)S(1)} %collective-permute-done.33.q1, f32[8,2048]{1,0:T(8,128)S(1)} %collective-permute-done.34.q2, ...), custom_call_target="tpu_custom_call" | custom-call | flops 201326592 | bytes 3407888 | tf_op jit(solution)/shard_map/pallas_call | solution.py:436
  190.1 4.1 %shard_map.138 = (bf16[40,2048]{1,0:T(8,128)(2,1)S(1)}, bf16[40,2048]{1,0:T(8,128)(2,1)S(1)}, bf16[40,2048]{1,0:T(8,128)(2,1)S(1)}, bf16[40,2048]{1,0:T(8,128)(2,1)S(1)}) custom-call(s32[2]{0:T(128)S(1)} %pad_add_fusion.3.numbers, f32[4,160,768]{2,1,0:T(8,128)S(1)} %get-tuple-element.166.a_ref, f32[4,160,768]{2,1,0:T(8,128)S(1)} %get-tuple-element.167.b_ref, ...), custom_call_target="tpu_custom_call" | custom-call | flops 1006632960 | bytes 6291456 | tf_op jit(solution)/shard_map/pallas_call | solution.py:608
  196.2 5.4 %collective-permute-done.49.r2 = bf16[40,2048]{1,0:T(8,128)(2,1)S(1)} collective-permute-done((bf16[40,2048]{1,0:T(8,128)(2,1)S(1)}, bf16[40,2048]{1,0:T(8,128)(2,1)S(1)}, u32[]{:S(2)}, u32[]{:S(2)}) %collective-permute-start.49) | collective-permute-done | bytes 163872 | tf_op jit(solution)/shard_map/ppermute | solution.py:474
  204.6 2.8 collective-permute-start.51
  207.4 11.8 %collective-permute-done.51 = bf16[128,2048]{1,0:T(8,128)(2,1)S(1)} collective-permute-done((bf16[128,2048]{1,0:T(8,128)(2,1)S(1)}, bf16[128,2048]{1,0:T(8,128)(2,1)S(1)}, u32[]{:S(2)}, u32[]{:S(2)}) %collective-permute-start.51) | collective-permute-done | bytes 524320 | tf_op jit(solution)/shard_map/ppermute | solution.py:468
  220.9 4.1 %shard_map.136 = (bf16[40,2048]{1,0:T(8,128)(2,1)S(1)}, bf16[40,2048]{1,0:T(8,128)(2,1)S(1)}, bf16[40,2048]{1,0:T(8,128)(2,1)S(1)}, bf16[40,2048]{1,0:T(8,128)(2,1)S(1)}) custom-call(s32[2]{0:T(128)S(1)} %pad_add_fusion.2.numbers, f32[4,160,768]{2,1,0:T(8,128)S(1)} %get-tuple-element.166.a_ref, f32[4,160,768]{2,1,0:T(8,128)S(1)} %get-tuple-element.167.b_ref, ...), custom_call_target="tpu_custom_call" | custom-call | flops 1006632960 | bytes 6291456 | tf_op jit(solution)/shard_map/pallas_call | solution.py:608
  226.9 5.2 %collective-permute-done.44.r2 = bf16[40,2048]{1,0:T(8,128)(2,1)S(1)} collective-permute-done((bf16[40,2048]{1,0:T(8,128)(2,1)S(1)}, bf16[40,2048]{1,0:T(8,128)(2,1)S(1)}, u32[]{:S(2)}, u32[]{:S(2)}) %collective-permute-start.44) | collective-permute-done | bytes 163872 | tf_op jit(solution)/shard_map/ppermute | solution.py:474
  232.1 2.6 collective-permute-done.45.r3
  235.7 7.0 %collective-permute-start.46 = (bf16[128,2048]{1,0:T(8,128)(2,1)S(1)}, bf16[128,2048]{1,0:T(8,128)(2,1)S(1)}, u32[]{:S(2)}, u32[]{:S(2)}) collective-permute-start(bf16[128,2048]{1,0:T(8,128)(2,1)S(1)} %get-tuple-element.146), channel_id=1, source_target_pairs={{0,1},{3,2},{4,5},{7,6},{8,9},{11,10},{12,13},{15,14},{16,17},{19,... | collective-permute-start | bytes 1572872 | tf_op jit(solution)/shard_map/ppermute | solution.py:468
  243.4 4.1 %shard_map.134 = (bf16[40,2048]{1,0:T(8,128)(2,1)S(1)}, bf16[40,2048]{1,0:T(8,128)(2,1)S(1)}, bf16[40,2048]{1,0:T(8,128)(2,1)S(1)}, bf16[40,2048]{1,0:T(8,128)(2,1)S(1)}) custom-call(s32[2]{0:T(128)S(1)} %pad_add_fusion.1.numbers, f32[4,160,768]{2,1,0:T(8,128)S(1)} %get-tuple-element.166.a_ref, f32[4,160,768]{2,1,0:T(8,128)S(1)} %get-tuple-element.167.b_ref, ...), custom_call_target="tpu_custom_call" | custom-call | flops 1006632960 | bytes 6291456 | tf_op jit(solution)/shard_map/pallas_call | solution.py:608
  249.4 5.2 %collective-permute-done.40.r2 = bf16[40,2048]{1,0:T(8,128)(2,1)S(1)} collective-permute-done((bf16[40,2048]{1,0:T(8,128)(2,1)S(1)}, bf16[40,2048]{1,0:T(8,128)(2,1)S(1)}, u32[]{:S(2)}, u32[]{:S(2)}) %collective-permute-start.40) | collective-permute-done | bytes 163872 | tf_op jit(solution)/shard_map/ppermute | solution.py:474
  254.6 2.6 collective-permute-done.41.r3
  259.6 4.6 %collective-permute-start.42 = (bf16[128,2048]{1,0:T(8,128)(2,1)S(1)}, bf16[128,2048]{1,0:T(8,128)(2,1)S(1)}, u32[]{:S(2)}, u32[]{:S(2)}) collective-permute-start(bf16[128,2048]{1,0:T(8,128)(2,1)S(1)} %get-tuple-element.148), channel_id=1, source_target_pairs={{0,1},{3,2},{4,5},{7,6},{8,9},{11,10},{12,13},{15,14},{16,17},{19,... | collective-permute-start | bytes 1572872 | tf_op jit(solution)/shard_map/ppermute | solution.py:468
  265.6 4.1 %shard_map.132 = (bf16[40,2048]{1,0:T(8,128)(2,1)S(1)}, bf16[40,2048]{1,0:T(8,128)(2,1)S(1)}, bf16[40,2048]{1,0:T(8,128)(2,1)S(1)}, bf16[40,2048]{1,0:T(8,128)(2,1)S(1)}) custom-call(s32[2]{0:T(128)S(1)} %pad_add_fusion.numbers, f32[4,160,768]{2,1,0:T(8,128)S(1)} %get-tuple-element.166.a_ref, f32[4,160,768]{2,1,0:T(8,128)S(1)} %get-tuple-element.167.b_ref, ...), custom_call_target="tpu_custom_call" | custom-call | flops 1006632960 | bytes 6291456 | tf_op jit(solution)/shard_map/pallas_call | solution.py:608
  271.9 4.9 %collective-permute-done.37.r2 = bf16[40,2048]{1,0:T(8,128)(2,1)S(1)} collective-permute-done((bf16[40,2048]{1,0:T(8,128)(2,1)S(1)}, bf16[40,2048]{1,0:T(8,128)(2,1)S(1)}, u32[]{:S(2)}, u32[]{:S(2)}) %collective-permute-start.37) | collective-permute-done | bytes 163872 | tf_op jit(solution)/shard_map/ppermute | solution.py:474
  (185 shorter events, 86.0 us)
Async XLA Ops:
  3.8 52.2 %collective-permute-start = (bf16[128,2048]{1,0:T(8,128)(2,1)S(1)}, bf16[128,2048]{1,0:T(8,128)(2,1)}, u32[]{:S(2)}, u32[]{:S(2)}) collective-permute-start(bf16[128,2048]{1,0:T(8,128)(2,1)S(1)} %fusion), channel_id=1, source_target_pairs={{0,1},{3,2},{4,5},{7,6},{8,9},{11,10},{12,13},{15,14},{16,17},{19,... | collective-permute-start | bytes 1572872 | tf_op jit(solution)/shard_map/ppermute | solution.py:468
  12.6 45.3 %collective-permute-start.21 = (bf16[128,2048]{1,0:T(8,128)(2,1)S(1)}, bf16[128,2048]{1,0:T(8,128)(2,1)}, u32[]{:S(2)}, u32[]{:S(2)}) collective-permute-start(bf16[128,2048]{1,0:T(8,128)(2,1)S(1)} %fusion.3), channel_id=1, source_target_pairs={{0,1},{3,2},{4,5},{7,6},{8,9},{11,10},{12,13},{15,14},{16,17},{19,... | collective-permute-start | bytes 1572872 | tf_op jit(solution)/shard_map/ppermute | solution.py:468
  17.7 42.0 %collective-permute-start.9 = (bf16[128,2048]{1,0:T(8,128)(2,1)S(1)}, bf16[128,2048]{1,0:T(8,128)(2,1)}, u32[]{:S(2)}, u32[]{:S(2)}) collective-permute-start(bf16[128,2048]{1,0:T(8,128)(2,1)S(1)} %fusion.1), channel_id=1, source_target_pairs={{0,1},{3,2},{4,5},{7,6},{8,9},{11,10},{12,13},{15,14},{16,17},{19,... | collective-permute-start | bytes 1572872 | tf_op jit(solution)/shard_map/ppermute | solution.py:468
  22.9 38.8 %collective-permute-start.15 = (bf16[128,2048]{1,0:T(8,128)(2,1)S(1)}, bf16[128,2048]{1,0:T(8,128)(2,1)S(1)}, u32[]{:S(2)}, u32[]{:S(2)}) collective-permute-start(bf16[128,2048]{1,0:T(8,128)(2,1)S(1)} %fusion.2), channel_id=1, source_target_pairs={{0,1},{3,2},{4,5},{7,6},{8,9},{11,10},{12,13},{15,14},{16,17},{19,... | collective-permute-start | bytes 1572872 | tf_op jit(solution)/shard_map/ppermute | solution.py:468
  24.2 29.7 %collective-permute-start.3 = (bf16[16,512]{1,0:T(8,128)(2,1)S(1)}, bf16[16,512]{1,0:T(8,128)(2,1)S(1)}, u32[]{:S(2)}, u32[]{:S(2)}) collective-permute-start(bf16[16,512]{1,0:T(8,128)(2,1)S(1)} %pad_maximum_fusion.5), channel_id=1, source_target_pairs={{0,1},{3,2},{4,5},{7,6},{8,9},{11,10},{12,13},{15,14},{16,17},{19,... | collective-permute-start | bytes 49160 | tf_op jit(solution)/shard_map/ppermute | solution.py:468
  54.7 14.5 %collective-permute-start.5 = (bf16[16,512]{1,0:T(8,128)(2,1)S(1)}, bf16[16,512]{1,0:T(8,128)(2,1)S(1)}, u32[]{:S(2)}, u32[]{:S(2)}) collective-permute-start(bf16[16,512]{1,0:T(8,128)(2,1)S(1)} %add.109), channel_id=1, source_target_pairs={{1,0},{2,3},{5,4},{6,7},{9,8},{10,11},{13,12},{14,15},{17,16},{18,... | collective-permute-start | bytes 49160 | tf_op jit(solution)/shard_map/ppermute | solution.py:468
  62.6 28.6 %collective-permute-start.2 = (bf16[128,2048]{1,0:T(8,128)(2,1)S(1)}, bf16[128,2048]{1,0:T(8,128)(2,1)S(1)}, u32[]{:S(2)}, u32[]{:S(2)}) collective-permute-start(bf16[128,2048]{1,0:T(8,128)(2,1)S(1)} %add_convert_fusion.9), channel_id=1, source_target_pairs={{1,0},{2,3},{5,4},{6,7},{9,8},{10,11},{13,12},{14,15},{17,16},{18,... | collective-permute-start | bytes 1572872 | tf_op jit(solution)/shard_map/ppermute | solution.py:468
  64.1 38.5 %collective-permute-start.23 = (bf16[128,2048]{1,0:T(8,128)(2,1)S(1)}, bf16[128,2048]{1,0:T(8,128)(2,1)}, u32[]{:S(2)}, u32[]{:S(2)}) collective-permute-start(bf16[128,2048]{1,0:T(8,128)(2,1)S(1)} %add_convert_fusion.3), channel_id=1, source_target_pairs={{1,0},{2,3},{5,4},{6,7},{9,8},{10,11},{13,12},{14,15},{17,16},{18,... | collective-permute-start | bytes 1572872 | tf_op jit(solution)/shard_map/ppermute | solution.py:468
  65.6 48.3 %collective-permute-start.11 = (bf16[128,2048]{1,0:T(8,128)(2,1)S(1)}, bf16[128,2048]{1,0:T(8,128)(2,1)}, u32[]{:S(2)}, u32[]{:S(2)}) collective-permute-start(bf16[128,2048]{1,0:T(8,128)(2,1)S(1)} %add_convert_fusion.7), channel_id=1, source_target_pairs={{1,0},{2,3},{5,4},{6,7},{9,8},{10,11},{13,12},{14,15},{17,16},{18,... | collective-permute-start | bytes 1572872 | tf_op jit(solution)/shard_map/ppermute | solution.py:468
  67.0 56.7 %collective-permute-start.17 = (bf16[128,2048]{1,0:T(8,128)(2,1)S(1)}, bf16[128,2048]{1,0:T(8,128)(2,1)}, u32[]{:S(2)}, u32[]{:S(2)}) collective-permute-start(bf16[128,2048]{1,0:T(8,128)(2,1)S(1)} %add_convert_fusion.5), channel_id=1, source_target_pairs={{1,0},{2,3},{5,4},{6,7},{9,8},{10,11},{13,12},{14,15},{17,16},{18,... | collective-permute-start | bytes 1572872 | tf_op jit(solution)/shard_map/ppermute | solution.py:468
  128.8 10.0 %collective-permute-start.24 = (bf16[40,2176]{1,0:T(8,128)(2,1)}, bf16[40,2176]{1,0:T(8,128)(2,1)}, u32[]{:S(2)}, u32[]{:S(2)}) collective-permute-start(bf16[40,2176]{1,0:T(8,128)(2,1)} %get-tuple-element.93), channel_id=1, source_target_pairs={{0,4},{4,0},{8,12},{12,8},{1,5},{5,1},{9,13},{13,9},{2,6},{6,2},{1... | collective-permute-start | bytes 522248 | tf_op jit(solution)/shard_map/ppermute | solution.py:474
  128.8 10.2 %collective-permute-start.25 = (bf16[40,2176]{1,0:T(8,128)(2,1)}, bf16[40,2176]{1,0:T(8,128)(2,1)}, u32[]{:S(2)}, u32[]{:S(2)}) collective-permute-start(bf16[40,2176]{1,0:T(8,128)(2,1)} %get-tuple-element.94), channel_id=1, source_target_pairs={{0,8},{4,12},{8,0},{12,4},{1,9},{5,13},{9,1},{13,5},{2,10},{6,14},... | collective-permute-start | bytes 522248 | tf_op jit(solution)/shard_map/ppermute | solution.py:474
  130.9 11.6 %collective-permute-start.26 = (bf16[40,2176]{1,0:T(8,128)(2,1)}, bf16[40,2176]{1,0:T(8,128)(2,1)}, u32[]{:S(2)}, u32[]{:S(2)}) collective-permute-start(bf16[40,2176]{1,0:T(8,128)(2,1)} %get-tuple-element.95), channel_id=1, source_target_pairs={{0,12},{4,8},{8,4},{12,0},{1,13},{5,9},{9,5},{13,1},{2,14},{6,10},... | collective-permute-start | bytes 522248 | tf_op jit(solution)/shard_map/ppermute | solution.py:474
  134.6 9.5 %collective-permute-start.18 = (bf16[40,2176]{1,0:T(8,128)(2,1)}, bf16[40,2176]{1,0:T(8,128)(2,1)}, u32[]{:S(2)}, u32[]{:S(2)}) collective-permute-start(bf16[40,2176]{1,0:T(8,128)(2,1)} %get-tuple-element.88), channel_id=1, source_target_pairs={{0,4},{4,0},{8,12},{12,8},{1,5},{5,1},{9,13},{13,9},{2,6},{6,2},{1... | collective-permute-start | bytes 522248 | tf_op jit(solution)/shard_map/ppermute | solution.py:474
  134.9 15.9 %collective-permute-start.19 = (bf16[40,2176]{1,0:T(8,128)(2,1)}, bf16[40,2176]{1,0:T(8,128)(2,1)S(1)}, u32[]{:S(2)}, u32[]{:S(2)}) collective-permute-start(bf16[40,2176]{1,0:T(8,128)(2,1)} %copy-done.12), channel_id=1, source_target_pairs={{0,8},{4,12},{8,0},{12,4},{1,9},{5,13},{9,1},{13,5},{2,10},{6,14},... | collective-permute-start | bytes 522248 | tf_op jit(solution)/shard_map/ppermute | solution.py:474
  138.8 12.8 %collective-permute-start.20 = (bf16[40,2176]{1,0:T(8,128)(2,1)}, bf16[40,2176]{1,0:T(8,128)(2,1)S(1)}, u32[]{:S(2)}, u32[]{:S(2)}) collective-permute-start(bf16[40,2176]{1,0:T(8,128)(2,1)} %copy-done.11), channel_id=1, source_target_pairs={{0,12},{4,8},{8,4},{12,0},{1,13},{5,9},{9,5},{13,1},{2,14},{6,10},... | collective-permute-start | bytes 522248 | tf_op jit(solution)/shard_map/ppermute | solution.py:474
  138.9 14.1 %collective-permute-start.12 = (bf16[40,2176]{1,0:T(8,128)(2,1)S(1)}, bf16[40,2176]{1,0:T(8,128)(2,1)S(1)}, u32[]{:S(2)}, u32[]{:S(2)}) collective-permute-start(bf16[40,2176]{1,0:T(8,128)(2,1)S(1)} %get-tuple-element.83), channel_id=1, source_target_pairs={{0,4},{4,0},{8,12},{12,8},{1,5},{5,1},{9,13},{13,9},{2,6},{6,2},{1... | collective-permute-start | bytes 522248 | tf_op jit(solution)/shard_map/ppermute | solution.py:474
  142.5 14.2 %collective-permute-start.13 = (bf16[40,2176]{1,0:T(8,128)(2,1)S(1)}, bf16[40,2176]{1,0:T(8,128)(2,1)S(1)}, u32[]{:S(2)}, u32[]{:S(2)}) collective-permute-start(bf16[40,2176]{1,0:T(8,128)(2,1)S(1)} %get-tuple-element.84), channel_id=1, source_target_pairs={{0,8},{4,12},{8,0},{12,4},{1,9},{5,13},{9,1},{13,5},{2,10},{6,14},... | collective-permute-start | bytes 522248 | tf_op jit(solution)/shard_map/ppermute | solution.py:474
  144.1 12.6 %collective-permute-start.14 = (bf16[40,2176]{1,0:T(8,128)(2,1)S(1)}, bf16[40,2176]{1,0:T(8,128)(2,1)S(1)}, u32[]{:S(2)}, u32[]{:S(2)}) collective-permute-start(bf16[40,2176]{1,0:T(8,128)(2,1)S(1)} %get-tuple-element.85), channel_id=1, source_target_pairs={{0,12},{4,8},{8,4},{12,0},{1,13},{5,9},{9,5},{13,1},{2,14},{6,10},... | collective-permute-start | bytes 522248 | tf_op jit(solution)/shard_map/ppermute | solution.py:474
  150.8 8.9 %collective-permute-start.6 = (bf16[40,2176]{1,0:T(8,128)(2,1)S(1)}, bf16[40,2176]{1,0:T(8,128)(2,1)S(1)}, u32[]{:S(2)}, u32[]{:S(2)}) collective-permute-start(bf16[40,2176]{1,0:T(8,128)(2,1)S(1)} %get-tuple-element.78), channel_id=1, source_target_pairs={{0,4},{4,0},{8,12},{12,8},{1,5},{5,1},{9,13},{13,9},{2,6},{6,2},{1... | collective-permute-start | bytes 522248 | tf_op jit(solution)/shard_map/ppermute | solution.py:474
  151.5 8.2 %collective-permute-start.7 = (bf16[40,2176]{1,0:T(8,128)(2,1)S(1)}, bf16[40,2176]{1,0:T(8,128)(2,1)S(1)}, u32[]{:S(2)}, u32[]{:S(2)}) collective-permute-start(bf16[40,2176]{1,0:T(8,128)(2,1)S(1)} %get-tuple-element.79), channel_id=1, source_target_pairs={{0,8},{4,12},{8,0},{12,4},{1,9},{5,13},{9,1},{13,5},{2,10},{6,14},... | collective-permute-start | bytes 522248 | tf_op jit(solution)/shard_map/ppermute | solution.py:474
  153.0 8.3 %collective-permute-start.8 = (bf16[40,2176]{1,0:T(8,128)(2,1)S(1)}, bf16[40,2176]{1,0:T(8,128)(2,1)S(1)}, u32[]{:S(2)}, u32[]{:S(2)}) collective-permute-start(bf16[40,2176]{1,0:T(8,128)(2,1)S(1)} %get-tuple-element.80), channel_id=1, source_target_pairs={{0,12},{4,8},{8,4},{12,0},{1,13},{5,9},{9,5},{13,1},{2,14},{6,10},... | collective-permute-start | bytes 522248 | tf_op jit(solution)/shard_map/ppermute | solution.py:474
  195.1 8.6 %collective-permute-start.50 = (bf16[40,2048]{1,0:T(8,128)(2,1)S(1)}, bf16[40,2048]{1,0:T(8,128)(2,1)S(1)}, u32[]{:S(2)}, u32[]{:S(2)}) collective-permute-start(bf16[40,2048]{1,0:T(8,128)(2,1)S(1)} %get-tuple-element.139), channel_id=1, source_target_pairs={{0,12},{4,8},{8,4},{12,0},{1,13},{5,9},{9,5},{13,1},{2,14},{6,10},... | collective-permute-start | bytes 491528 | tf_op jit(solution)/shard_map/ppermute | solution.py:474
  204.6 14.6 %collective-permute-start.51 = (bf16[128,2048]{1,0:T(8,128)(2,1)S(1)}, bf16[128,2048]{1,0:T(8,128)(2,1)S(1)}, u32[]{:S(2)}, u32[]{:S(2)}) collective-permute-start(bf16[128,2048]{1,0:T(8,128)(2,1)S(1)} %convert_element_type.186), channel_id=1, source_target_pairs={{0,1},{3,2},{4,5},{7,6},{8,9},{11,10},{12,13},{15,14},{16,17},{19,... | collective-permute-start | bytes 1572872 | tf_op jit(solution)/shard_map/ppermute | solution.py:468
  219.3 16.2 %collective-permute-start.52 = (bf16[128,2048]{1,0:T(8,128)(2,1)S(1)}, bf16[128,2048]{1,0:T(8,128)(2,1)S(1)}, u32[]{:S(2)}, u32[]{:S(2)}) collective-permute-start(bf16[128,2048]{1,0:T(8,128)(2,1)S(1)} %add_convert_fusion.1), channel_id=1, source_target_pairs={{1,2},{2,1},{5,6},{6,5},{9,10},{10,9},{13,14},{14,13},{17,18},{18,... | collective-permute-start | bytes 1572872 | tf_op jit(solution)/shard_map/ppermute | solution.py:468
  226.1 8.6 %collective-permute-start.45 = (bf16[40,2048]{1,0:T(8,128)(2,1)S(1)}, bf16[40,2048]{1,0:T(8,128)(2,1)S(1)}, u32[]{:S(2)}, u32[]{:S(2)}) collective-permute-start(bf16[40,2048]{1,0:T(8,128)(2,1)S(1)} %get-tuple-element.135), channel_id=1, source_target_pairs={{0,12},{4,8},{8,4},{12,0},{1,13},{5,9},{9,5},{13,1},{2,14},{6,10},... | collective-permute-start | bytes 491528 | tf_op jit(solution)/shard_map/ppermute | solution.py:474
  235.7 23.7 %collective-permute-start.46 = (bf16[128,2048]{1,0:T(8,128)(2,1)S(1)}, bf16[128,2048]{1,0:T(8,128)(2,1)S(1)}, u32[]{:S(2)}, u32[]{:S(2)}) collective-permute-start(bf16[128,2048]{1,0:T(8,128)(2,1)S(1)} %get-tuple-element.146), channel_id=1, source_target_pairs={{0,1},{3,2},{4,5},{7,6},{8,9},{11,10},{12,13},{15,14},{16,17},{19,... | collective-permute-start | bytes 1572872 | tf_op jit(solution)/shard_map/ppermute | solution.py:468
  248.6 8.6 %collective-permute-start.41 = (bf16[40,2048]{1,0:T(8,128)(2,1)S(1)}, bf16[40,2048]{1,0:T(8,128)(2,1)S(1)}, u32[]{:S(2)}, u32[]{:S(2)}) collective-permute-start(bf16[40,2048]{1,0:T(8,128)(2,1)S(1)} %get-tuple-element.131), channel_id=1, source_target_pairs={{0,12},{4,8},{8,4},{12,0},{1,13},{5,9},{9,5},{13,1},{2,14},{6,10},... | collective-permute-start | bytes 491528 | tf_op jit(solution)/shard_map/ppermute | solution.py:474
  258.1 22.2 %collective-permute-start.53 = (bf16[128,2048]{1,0:T(8,128)(2,1)S(1)}, bf16[128,2048]{1,0:T(8,128)(2,1)S(1)}, u32[]{:S(2)}, u32[]{:S(2)}) collective-permute-start(bf16[128,2048]{1,0:T(8,128)(2,1)S(1)} %get-tuple-element.145), channel_id=1, source_target_pairs={{1,0},{2,3},{5,4},{6,7},{9,8},{10,11},{13,12},{14,15},{17,16},{18,... | collective-permute-start | bytes 1572872 | tf_op jit(solution)/shard_map/ppermute | solution.py:468
  259.6 20.8 %collective-permute-start.42 = (bf16[128,2048]{1,0:T(8,128)(2,1)S(1)}, bf16[128,2048]{1,0:T(8,128)(2,1)S(1)}, u32[]{:S(2)}, u32[]{:S(2)}) collective-permute-start(bf16[128,2048]{1,0:T(8,128)(2,1)S(1)} %get-tuple-element.148), channel_id=1, source_target_pairs={{0,1},{3,2},{4,5},{7,6},{8,9},{11,10},{12,13},{15,14},{16,17},{19,... | collective-permute-start | bytes 1572872 | tf_op jit(solution)/shard_map/ppermute | solution.py:468
  264.2 16.2 %collective-permute-start.47 = (bf16[128,2048]{1,0:T(8,128)(2,1)S(1)}, bf16[128,2048]{1,0:T(8,128)(2,1)S(1)}, u32[]{:S(2)}, u32[]{:S(2)}) collective-permute-start(bf16[128,2048]{1,0:T(8,128)(2,1)S(1)} %get-tuple-element.147), channel_id=1, source_target_pairs={{1,2},{2,1},{5,6},{6,5},{9,10},{10,9},{13,14},{14,13},{17,18},{18,... | collective-permute-start | bytes 1572872 | tf_op jit(solution)/shard_map/ppermute | solution.py:468
  271.2 8.3 %collective-permute-start.38 = (bf16[40,2048]{1,0:T(8,128)(2,1)S(1)}, bf16[40,2048]{1,0:T(8,128)(2,1)S(1)}, u32[]{:S(2)}, u32[]{:S(2)}) collective-permute-start(bf16[40,2048]{1,0:T(8,128)(2,1)S(1)} %get-tuple-element.127), channel_id=1, source_target_pairs={{0,12},{4,8},{8,4},{12,0},{1,13},{5,9},{9,5},{13,1},{2,14},{6,10},... | collective-permute-start | bytes 491528 | tf_op jit(solution)/shard_map/ppermute | solution.py:474
  (43 other events, 496.4 us)

commit v2 on v1

--- a/solution.py
+++ b/solution.py
@@ -209,7 +209,13 @@
 LEAVES_IN = ((0, 1), (3, 2))
 INNER_SWAP = ((1, 2), (2, 1))
 LEAVES_OUT = ((1, 0), (2, 3))
+PIECES = (1, 1, 1, 2)
+FORWARD_ORDER = (
+    "p0", "p1", "p2", "s0", "p3", "s1", "t0", "p4", "s2", "t1", "d0", "s3", "t2", "d1", "x0", "s4", "t3", "t4", "d2", "x1", "d3", "x2", "x3",
+)
+VMEM_LIMIT = 24 * 2**20
 BLOCK_ORDER = ((3, 2, 1, 0), (3, 0, 2, 1), (0, 3, 1, 2), (0, 1, 2, 3))
+OWN_EXPERT, LEAF, Z, PEER, PEER_EXPERT, ORDER = 0, 1, 2, 3, 7, 11
 BF16 = jnp.bfloat16
 F32 = jnp.float32
 
@@ -237,16 +243,46 @@
     return lax.broadcasted_iota(jnp.int32, shape, axis)
 
 
-def dispatch_kernel(capacity, numbers, t_ref, gain_ref, router_ref, mask_ref, token_ref, *outs):
-    row_refs, place_ref = outs[:4], outs[4]
-    width = t_ref.shape[1]
-    rows = t_ref.shape[0]
-    experts = router_ref.shape[0]
-    x = t_ref[...].astype(F32)
+def project_kernel(block, offset, n, context_ref, weight_ref, resid_ref, *rest):
+    out_ref = rest[-1]
+    rows = context_ref.shape[0]
+    part = dot_nn(context_ref[...], weight_ref[...])
+    share = jnp.where(n[Z] == block, resid_ref[offset : offset + rows, :].astype(F32), 0.0)
+    out_ref[:rows, :] = (part + share).astype(BF16)
+    if block == 0:
+        mask = rest[0][...]
+        out_ref[rows:, :] = jnp.where(pl.program_id(0) == 0, mask.astype(F32), 0.0).astype(BF16)
+
+
+def add_kernel(n, left_ref, right_ref, _, out_ref):
+    out_ref[...] = (left_ref[...].astype(F32) + right_ref[...].astype(F32)).astype(BF16)
+
+
+def dispatch_kernel(capacity, block, pieces, n, *refs):
+    inner_refs, back_refs, refs = refs[:pieces], refs[pieces : 2 * pieces], refs[2 * pieces :]
+    gain_ref, router_ref, token_ref, *refs = refs
+    rows = token_ref.shape[1]
+    outs = refs[-7:] if block == 0 else refs[-6:]
+    row_refs, t_ref, place_ref = outs[:4], outs[4], outs[5]
+    experts, width = router_ref.shape
+    x = jnp.concatenate(
+        [
+            jnp.where(n[LEAF] == 1, back[...].astype(F32), inner[...].astype(F32))
+            for inner, back in zip(inner_refs, back_refs)
+        ],
+        axis=0,
+    )
+    if block == 0:
+        wide = x[rows:, : 4 * rows].astype(BF16)
+        outs[6][...] = wide
+        x = x[:rows]
+    else:
+        wide = refs[0][...]
+    mask = wide[:, block * rows : (block + 1) * rows]
+    t_ref[0] = x.astype(BF16)
     scale = lax.rsqrt(jnp.mean(x * x, axis=1, keepdims=True) + EPSILON)
     normed = (x * scale * gain_ref[...]).astype(BF16)
     logits = contract_last(router_ref[...], normed)
-    mask = mask_ref[...]
     chosen = mask.astype(F32) > 0.5
     exp_chosen = jnp.where(chosen, jnp.exp(jnp.where(chosen, logits, 0.0)), 0.0)
     gates = exp_chosen / jnp.sum(exp_chosen, axis=0, keepdims=True)
@@ -276,10 +312,10 @@
     slot = iota((capacity, rows), 0).astype(F32)
     picks = []
     for way in range(4):
-        own = jnp.sum(jnp.where(expert_row == numbers[way], position, 0.0), axis=0, keepdims=True)
+        own = jnp.sum(jnp.where(expert_row == n[PEER_EXPERT + way], position, 0.0), axis=0, keepdims=True)
         picks.append((slot == own).astype(F32))
     picked = jnp.concatenate(picks, axis=0)
-    place_ref[...] = jnp.transpose(picked).astype(BF16)
+    place_ref[0] = jnp.transpose(picked).astype(BF16)
     picked = picked.astype(BF16)
     sent = dot_nn(picked, normed)
     sent_extra = contract_last(picked, extra)
@@ -289,15 +325,16 @@
         row_refs[way][:, width:] = sent_extra[at].astype(BF16)
 
 
-def expert_kernel(numbers, r0, r1, r2, r3, gate_ref, up_ref, hidden_ref, a_ref, b_ref, pooled_ref, info_ref, x_ref, weight_ref):
+def expert_kernel(n, r0, r1, r2, r3, gate_ref, up_ref, *refs):
+    pooled_ref, hidden_ref, a_ref, b_ref, info_ref, x_ref, weight_ref = refs[-7:]
     width = gate_ref.shape[0]
     experts = 16
 
     @pl.when(pl.program_id(0) == 0)
-    def _():
+    def start():
         x_ref[...] = jnp.concatenate([r[:, :width].astype(F32) for r in (r0, r1, r2, r3)], axis=0).astype(BF16)
         extra = jnp.concatenate([r[:, width:].astype(F32) for r in (r0, r1, r2, r3)], axis=0).astype(BF16)
-        own = numbers[0]
+        own = n[OWN_EXPERT]
 
         def mixer(source, goal):
             gates = (goal < experts) & ((source == goal) | (source == goal + experts))
@@ -308,7 +345,7 @@
 
         square = (ROW_EXTRA, ROW_EXTRA)
         info = dot_nn(extra, mixer(iota(square, 0), iota(square, 1)))
-        info_ref[...] = info
+        info_ref[0] = info
         turned = contract_last(mixer(iota(square, 1), iota(square, 0)), extra)
         sequence = turned[experts : experts + 1]
         weight = turned[experts + 1 : experts + 2] * turned[experts + 2 : experts + 3]
@@ -321,29 +358,29 @@
     sigmoid = 1.0 / (1.0 + jnp.exp(-pre_gate))
     silu = pre_gate * sigmoid
     hidden = (silu * pre_up).astype(BF16)
-    hidden_ref[...] = hidden
-    a_ref[...] = pre_up * sigmoid * (1.0 + pre_gate * (1.0 - sigmoid))
-    b_ref[...] = silu
+    hidden_ref[0] = hidden
+    a_ref[0] = pre_up * sigmoid * (1.0 + pre_gate * (1.0 - sigmoid))
+    b_ref[0] = silu
     pooled_ref[...] = fold(dot_nn(weight_ref[...], hidden))
 
 
-def embed_kernel(numbers, p0, p1, p2, p3, down_ref, t_ref, token_ref, o0, o1, o2, o3, part_ref):
+def embed_kernel(n, p0, p1, p2, p3, down_ref, t_ref, token_ref, _, o0, o1, o2, o3, part_ref):
     pooled = p0[...] + p1[...] + p2[...] + p3[...]
     part = fold(dot_nn(stacked_halves(pooled), down_ref[...]))
     sequences = part.shape[0]
     own = jnp.where(
-        iota((sequences, t_ref.shape[0]), 0).astype(F32) == token_ref[0:1, :], token_ref[1:2, :], 0.0
-    )
-    part_ref[...] = part + fold(dot_nn(stacked_halves(own), t_ref[...]))
+        iota((sequences, t_ref.shape[1]), 0).astype(F32) == token_ref[0:1, :], token_ref[1:2, :], 0.0
+    )
+    part_ref[...] = part + fold(dot_nn(stacked_halves(own), t_ref[0]))
     rows = o0.shape[0]
     for way, out in enumerate((o0, o1, o2, o3)):
-        out[...] = part_ref[pl.ds(pl.multiple_of(numbers[way] * rows, rows), rows), :]
-
-
-def contrast_kernel(numbers, q0, q1, q2, q3, down_ref, loss_ref, grad_ref, hidden_grad_ref, all_ref):
+        out[...] = part_ref[pl.ds(pl.multiple_of(n[PEER + way] * rows, rows), rows), :]
+
+
+def contrast_kernel(n, q0, q1, q2, q3, down_ref, _, loss_ref, grad_ref, hidden_grad_ref, all_ref):
     rows = q0.shape[0]
     for way, part in enumerate((q0, q1, q2, q3)):
-        all_ref[pl.ds(pl.multiple_of(numbers[way] * rows, rows), rows), :] = part[...]
+        all_ref[pl.ds(pl.multiple_of(n[PEER + way] * rows, rows), rows), :] = part[...]
     embedded = all_ref[...]
     count = embedded.shape[0]
     pairs = count // 2
@@ -379,11 +416,11 @@
     hidden_grad_ref[...] = fold(contract_last(stacked_halves(grad), down_ref[...]))
 
 
-def backward_kernel(capacity, numbers, a_ref, b_ref, hidden_ref, info_ref, dh_ref, gate_ref, up_ref, router_ref, o0, o1, o2, o3, dgate_ref, dup_ref, dlog_ref):
+def backward_kernel(capacity, n, a_ref, b_ref, hidden_ref, info_ref, dh_ref, gate_ref, up_ref, router_ref, _, o0, o1, o2, o3, dgate_ref, dup_ref, dlog_ref):
     experts = 16
 
     @pl.when(pl.program_id(0) == 0)
-    def _():
+    def start():
         info = info_ref[0]
         slots = info.shape[0]
         sequence = info[:, experts : experts + 1]
@@ -396,7 +433,7 @@
         moved = jnp.sum(dhidden * hidden_ref[0].astype(F32), axis=1, keepdims=True)
         lane = iota((slots, ROW_EXTRA), 1)
         gates = jnp.where(lane < experts, info, 0.0)
-        dlog_ref[...] = (moved * (jnp.where(lane == numbers[1], 1.0, 0.0) - gates)).astype(BF16)
+        dlog_ref[...] = (moved * (jnp.where(lane == n[OWN_EXPERT], 1.0, 0.0) - gates)).astype(BF16)
 
     total = (
         contract_last(dgate_ref[...], gate_ref[...])
@@ -407,13 +444,15 @@
         out[...] = total[way * capacity : (way + 1) * capacity].astype(BF16)
 
 
-def combine_kernel(numbers, place_ref, r0, r1, r2, r3, out_ref):
+def combine_kernel(n, place_ref, r0, r1, r2, r3, _, out_ref, narrow_ref):
     rows = jnp.concatenate([r[...].astype(F32) for r in (r0, r1, r2, r3)], axis=0).astype(BF16)
-    out_ref[...] = dot_nn(place_ref[0], rows)
-
-
-def finish_kernel(t_ref, gain_ref, grad_ref, token_ref, own_ref, r4, r5, r6, out_ref):
-    x = t_ref[...].astype(F32)
+    total = dot_nn(place_ref[0], rows)
+    out_ref[...] = total
+    narrow_ref[...] = total.astype(BF16)
+
+
+def finish_kernel(n, t_ref, gain_ref, grad_ref, token_ref, own_ref, r4, r5, r6, _, out_ref):
+    x = t_ref[0].astype(F32)
     scale = lax.rsqrt(jnp.mean(x * x, axis=1, keepdims=True) + EPSILON)
     sequences = grad_ref.shape[0]
     spread = jnp.where(
@@ -429,25 +468,55 @@
     out_ref[...] = out.astype(BF16)
 
 
-def whole_call(kernel, outs, *args, scratch=(), numbers=0, limit=40, flops=0):
-    spec = pl.BlockSpec(memory_space=pltpu.VMEM)
-    smem = pl.BlockSpec(memory_space=pltpu.SMEM)
-    moved = sum(a.size * a.dtype.itemsize for a in args)
-    return pl.pallas_call(
-        kernel,
-        out_shape=outs,
-        in_specs=[smem] * numbers + [spec] * (len(args) - numbers),
-        out_specs=jax.tree.map(lambda _: spec, outs),
-        scratch_shapes=scratch,
-        compiler_params=pltpu.CompilerParams(vmem_limit_bytes=limit * 2**20),
-        cost_estimate=pl.CostEstimate(flops=flops, bytes_accessed=moved, transcendentals=0),
-    )(*args)
+class Chain:
+    def __init__(self, numbers, first):
+        self.numbers = numbers
+        self.last = first
+
+    def __call__(self, kernel, ins, outs, *, steps=1, kept=(), scratch=(), flops=0):
+        args, in_specs = zip(*ins)
+        args, in_specs = list(args), list(in_specs)
+        shapes, out_specs = zip(*outs)
+        aliases = {}
+        for at, array in kept:
+            aliases[1 + len(args)] = at
+            args.append(array)
+            in_specs.append(pl.BlockSpec(memory_space=pl.ANY))
+        args.append(self.last)
+        in_specs.append(pl.BlockSpec(memory_space=pl.ANY))
+        result = pl.pallas_call(
+            kernel,
+            out_shape=list(shapes),
+            grid_spec=pltpu.PrefetchScalarGridSpec(
+                num_scalar_prefetch=1,
+                grid=(steps,),
+                in_specs=in_specs,
+                out_specs=list(out_specs),
+                scratch_shapes=scratch,
+            ),
+            input_output_aliases=aliases,
+            compiler_params=pltpu.CompilerParams(vmem_limit_bytes=VMEM_LIMIT),
+            cost_estimate=pl.CostEstimate(
+                flops=flops, bytes_accessed=sum(x.size * x.dtype.itemsize for x in args), transcendentals=0
+            ),
+        )(self.numbers, *args)
+        self.last = result[0]
+        return result
+
+
+def fixed(shape):
+    return pl.BlockSpec(shape, lambda j, n: (0,) * len(shape))
+
+
+def whole(array):
+    return array, fixed(array.shape)
 
 
 def fast_body(context, o_weight, resid, norm_gain, router, gate_weight, up_weight, down_weight, expert_ids, lengths):
     e = lax.axis_index("expert")
     z = lax.axis_index("tensor")
     rows, width = resid.shape
+    heads = context.shape[1]
     experts = router.shape[1]
     top = expert_ids.shape[1]
     seq_count = lengths.shape[1]
@@ -455,14 +524,20 @@
     hidden_width = gate_weight.shape[2]
     capacity = max(2, rows * top * 5 // (4 * experts))
     slots = 4 * capacity
-    is_leaf = (z == 0) | (z == 3)
+    leaf = (z == 0) | (z == 3)
     ways = e ^ jnp.arange(4, dtype=jnp.int32)
-    way_experts = ways * 4 + z
-    own_expert = (e * 4 + z).astype(jnp.int32)
+    numbers = jnp.concatenate(
+        [
+            jnp.stack([e * 4 + z, leaf.astype(jnp.int32), z]),
+            ways,
+            ways * 4 + z,
+            jnp.asarray(BLOCK_ORDER, jnp.int32)[z],
+        ]
+    ).astype(jnp.int32)
     gate_w, up_w, down_w = gate_weight[0], up_weight[0], down_weight[0]
     gain = norm_gain.reshape(1, width)
     router_turned = router.T
-    router_rows = jnp.zeros((ROW_EXTRA, width), BF16).at[:experts].set(router_turned)
+    router_rows = jnp.pad(router_turned, ((0, ROW_EXTRA - experts), (0, 0)))
 
     def along_z(value, pairs):
         return lax.ppermute(value, "tensor", pairs)
@@ -477,10 +552,6 @@
         (expert_ids[None, :, :] == jnp.arange(experts, dtype=jnp.int32)[:, None, None]).astype(F32), axis=2
     )
     mask_wide = jnp.concatenate([jnp.where(z == c, mask_own, 0.0) for c in range(4)], axis=1).astype(BF16)
-    mask_sum = mask_wide + along_z(mask_wide, LEAVES_IN)
-    mask_sum = mask_sum + along_z(mask_sum, INNER_SWAP)
-    mask_back = along_z(mask_sum, LEAVES_OUT)
-    mask_all = jnp.where(is_leaf, mask_back, mask_sum)
 
     seq_lengths = lengths[0]
     seq_ends = jnp.cumsum(seq_lengths)
@@ -498,179 +569,179 @@
         ],
         axis=0,
     )
-    token_own = lax.dynamic_slice_in_dim(token_info, z * rows, rows, 1)
-
-    totals, received, placed = [], [], []
-    for c in range(4):
-        part = jnp.dot(context[c * rows : (c + 1) * rows], o_weight, preferred_element_type=F32)
-        part = (part + jnp.where(z == c, resid.astype(F32), 0.0)).astype(BF16)
-        arrived = along_z(part, LEAVES_IN)
-        half = (part.astype(F32) + arrived.astype(F32)).astype(BF16)
-        other = along_z(half, INNER_SWAP)
-        total = (half.astype(F32) + other.astype(F32)).astype(BF16)
-        back = along_z(total, LEAVES_OUT)
-        total = jnp.where(is_leaf, back, total)
-        totals.append(total)
-        *sent, place = whole_call(
-            functools.partial(dispatch_kernel, capacity),
-            [jax.ShapeDtypeStruct((capacity, width + ROW_EXTRA), BF16)] * 4
-            + [jax.ShapeDtypeStruct((rows, slots), BF16)],
-            way_experts,
-            total,
-            gain,
-            router_turned,
-            mask_all[:, c * rows : (c + 1) * rows],
-            token_info[:, c * rows : (c + 1) * rows],
-            numbers=1,
+
+    chain = Chain(numbers, gain)
+    shape = jax.ShapeDtypeStruct
+    tile = 512
+    pieces = []
+    for c, cuts in enumerate(PIECES):
+        pieces += [(c, i * (rows // cuts), rows // cuts) for i in range(cuts)]
+    count = len(pieces)
+    parts, half, inner, back, from_leaf, from_inner = ([None] * count for _ in range(6))
+    received, pools, shared, kept_rows, kept_acts = [None] * 4, [None] * 4, {}, {}, {}
+
+    def first_hop(i):
+        c, offset, size = pieces[i]
+        tall = size + (experts if c == 0 else 0)
+        at = (c * rows + offset) // size
+        ins = [
+            (context, pl.BlockSpec((size, heads), lambda j, n: (at, 0))),
+            (o_weight, pl.BlockSpec((heads, tile), lambda j, n: (0, j))),
+            (resid, pl.BlockSpec((rows, tile), lambda j, n: (0, j))),
+        ]
+        if c == 0:
+            ins.append(whole(mask_wide))
+        (parts[i],) = chain(
+            functools.partial(project_kernel, c, offset),
+            ins,
+            [(shape((tall, width), BF16), pl.BlockSpec((tall, tile), lambda j, n: (0, j)))],
+            steps=width // tile,
+            flops=2 * size * heads * width,
+        )
+        from_leaf[i] = along_z(parts[i], LEAVES_IN)
+
+    def add(left, right):
+        like = shape(right.shape, BF16)
+        return chain(add_kernel, [whole(left), whole(right)], [(like, fixed(like.shape))], flops=left.size)[0]
+
+    def second_hop(i):
+        half[i] = add(parts[i], from_leaf[i])
+        from_inner[i] = along_z(half[i], INNER_SWAP)
+
+    def third_hop(i):
+        inner[i] = add(half[i], from_inner[i])
+        back[i] = along_z(inner[i], LEAVES_OUT)
+
+    def dispatch(c):
+        mine = [i for i in range(count) if pieces[i][0] == c]
+        ins = [whole(inner[i]) for i in mine] + [whole(back[i]) for i in mine]
+        ins += [
+            whole(gain),
+            whole(router_turned),
+            (token_info, pl.BlockSpec((8, rows), lambda j, n: (0, c))),
+        ]
+        if c > 0:
+            ins.append(whole(shared["mask"]))
+        sent_shape = (capacity, width + ROW_EXTRA)
+        outs = [(shape(sent_shape, BF16), fixed(sent_shape))] * 4
+        for size in ((rows, width), (rows, slots)):
+            outs.append((shape((4,) + size, BF16), pl.BlockSpec((1,) + size, lambda j, n: (c, 0, 0))))
+        if c == 0:
+            outs.append((shape((experts, 4 * rows), BF16), fixed((experts, 4 * rows))))
+        result = chain(
+            functools.partial(dispatch_kernel, capacity, c, len(mine)),
+            ins,
+            outs,
+            kept=sorted(kept_rows.items()),
             flops=2 * slots * rows * width,
         )
-        placed.append(place)
-        received.append([sent[0]] + [swap_e(sent[way], way) for way in (1, 2, 3)])
-
-    tile = 256
-    hiddens, a_parts, b_parts, pools, infos = [], [], [], [], []
-    for c in range(4):
-        whole = pl.BlockSpec((capacity, width + ROW_EXTRA), lambda j, n: (0, 0))
-        hid, a, b, pool, info = pl.pallas_call(
+        kept_rows.update({4: result[4], 5: result[5]})
+        if c == 0:
+            shared["mask"] = result[6]
+        received[c] = [result[0]] + [swap_e(result[way], way) for way in (1, 2, 3)]
+
+    def expert(c):
+        tile = 256
+        block = lambda size: pl.BlockSpec((1, slots, size), lambda j, n: (c, 0, j))
+        outs = [(shape((sequences, hidden_width), F32), pl.BlockSpec((sequences, tile), lambda j, n: (0, j)))]
+        outs += [(shape((4, slots, hidden_width), kind), block(tile)) for kind in (BF16, F32, F32)]
+        outs.append((shape((4, slots, ROW_EXTRA), F32), pl.BlockSpec((1, slots, ROW_EXTRA), lambda j, n: (c, 0, 0))))
+        weight_spec = pl.BlockSpec((width, tile), lambda j, n: (0, j))
+        result = chain(
             expert_kernel,
-            out_shape=[
-                jax.ShapeDtypeStruct((slots, hidden_width), BF16),
-                jax.ShapeDtypeStruct((slots, hidden_width), F32),
-                jax.ShapeDtypeStruct((slots, hidden_width), F32),
-                jax.ShapeDtypeStruct((sequences, hidden_width), F32),
-                jax.ShapeDtypeStruct((slots, ROW_EXTRA), F32),
-            ],
-            grid_spec=pltpu.PrefetchScalarGridSpec(
-                num_scalar_prefetch=1,
-                grid=(hidden_width // tile,),
-                in_specs=[whole] * 4 + [pl.BlockSpec((width, tile), lambda j, n: (0, j))] * 2,
-                out_specs=[
-                    pl.BlockSpec((slots, tile), lambda j, n: (0, j)),
-                    pl.BlockSpec((slots, tile), lambda j, n: (0, j)),
-                    pl.BlockSpec((slots, tile), lambda j, n: (0, j)),
-                    pl.BlockSpec((sequences, tile), lambda j, n: (0, j)),
-                    pl.BlockSpec((slots, ROW_EXTRA), lambda j, n: (0, 0)),
-                ],
-                scratch_shapes=[pltpu.VMEM((slots, width), BF16), pltpu.VMEM((2 * sequences, slots), BF16)],
-            ),
-            compiler_params=pltpu.CompilerParams(vmem_limit_bytes=40 * 2**20),
-            cost_estimate=pl.CostEstimate(
-                flops=4 * slots * width * hidden_width, bytes_accessed=4 * width * hidden_width, transcendentals=0
-            ),
-        )(own_expert.reshape(1), *received[c], gate_w, up_w)
-        hiddens.append(hid)
-        a_parts.append(a)
-        b_parts.append(b)
-        pools.append(pool)
-        infos.append(info)
-
-    total_own = lax.select_n(z, *totals)
-    seq_shape = jax.ShapeDtypeStruct((seq_count, width), F32)
-    quarters = whole_call(
+            [whole(r) for r in received[c]] + [(gate_w, weight_spec), (up_w, weight_spec)],
+            outs,
+            steps=hidden_width // tile,
+            kept=sorted(kept_acts.items()),
+            scratch=[pltpu.VMEM((slots, width), BF16), pltpu.VMEM((2 * sequences, slots), BF16)],
+            flops=4 * slots * width * hidden_width,
+        )
+        pools[c] = result[0]
+        kept_acts.update({i: result[i] for i in (1, 2, 3, 4)})
+
+    calls = {"p": first_hop, "s": second_hop, "t": third_hop, "d": dispatch, "x": expert}
+    for step in FORWARD_ORDER:
+        calls[step[0]](int(step[1:]))
+
+    total_all, place_all = kept_rows[4], kept_rows[5]
+    hidden_all, a_all, b_all, info_all = (kept_acts[i] for i in (1, 2, 3, 4))
+    own_rows = (total_all, pl.BlockSpec((1, rows, width), lambda j, n: (n[Z], 0, 0)))
+    own_tokens = (token_info, pl.BlockSpec((8, rows), lambda j, n: (0, n[Z])))
+    seq_shape = shape((seq_count, width), F32)
+    quarters = chain(
         embed_kernel,
-        [seq_shape] * 4,
-        ways,
-        *pools,
-        down_w,
-        total_own,
-        token_own,
+        [whole(pool) for pool in pools] + [whole(down_w), own_rows, own_tokens],
+        [(seq_shape, fixed(seq_shape.shape))] * 4,
         scratch=[pltpu.VMEM((sequences, width), F32)],
-        numbers=1,
         flops=4 * sequences * hidden_width * width,
     )
     mine = (quarters[0] + swap_e(quarters[1], 1)) + (swap_e(quarters[2], 2) + swap_e(quarters[3], 3))
     mine = (mine + swap_z(mine, 1)) + (swap_z(mine, 2) + swap_z(mine, 3))
-    pieces = [mine] + [swap_e(mine, way) for way in (1, 2, 3)]
-    loss, dembedded, hidden_grad = whole_call(
+    gathered = [mine] + [swap_e(mine, way) for way in (1, 2, 3)]
+    sizes = ((1, 128), (sequences, width), (sequences, hidden_width))
+    loss, dembedded, hidden_grad = chain(
         contrast_kernel,
-        [
-            jax.ShapeDtypeStruct((1, 128), F32),
-            jax.ShapeDtypeStruct((sequences, width), F32),
-            jax.ShapeDtypeStruct((sequences, hidden_width), F32),
-        ],
-        ways,
-        *pieces,
-        down_w,
+        [whole(piece) for piece in gathered] + [whole(down_w)],
+        [(shape(size, F32), fixed(size)) for size in sizes],
         scratch=[pltpu.VMEM((sequences, width), F32)],
-        numbers=1,
         flops=4 * sequences * hidden_width * width,
     )
-
-    hidden_all, a_all, b_all, info_all = (jnp.stack(part) for part in (hiddens, a_parts, b_parts, infos))
-    place_all = jnp.stack(placed)
-    order = jnp.asarray(BLOCK_ORDER, jnp.int32)[z]
-    tile = 512
-    sums = []
-    for j in range(4):
-        numbers = jnp.stack([order[j], own_expert])
-        block = lambda shape: pl.BlockSpec((1,) + shape, lambda i, n: (n[0], 0, 0))
-        out_spec = pl.BlockSpec((capacity, tile), lambda i, n: (0, i))
-        grads = pl.pallas_call(
+    returned, sums = [None] * 4, [None] * 4
+
+    def backward(k):
+        block = lambda size: pl.BlockSpec((1, slots, size), lambda j, n: (n[ORDER + k], 0, 0))
+        weight_spec = pl.BlockSpec((tile, hidden_width), lambda j, n: (j, 0))
+        grads = chain(
             functools.partial(backward_kernel, capacity),
-            out_shape=[jax.ShapeDtypeStruct((capacity, width), BF16)] * 4,
-            grid_spec=pltpu.PrefetchScalarGridSpec(
-                num_scalar_prefetch=1,
-                grid=(width // tile,),
-                in_specs=[
-                    block((slots, hidden_width)),
-                    block((slots, hidden_width)),
-                    block((slots, hidden_width)),
-                    block((slots, ROW_EXTRA)),
-                    pl.BlockSpec((sequences, hidden_width), lambda i, n: (0, 0)),
-                    pl.BlockSpec((tile, hidden_width), lambda i, n: (i, 0)),
-                    pl.BlockSpec((tile, hidden_width), lambda i, n: (i, 0)),
-                    pl.BlockSpec((ROW_EXTRA, tile), lambda i, n: (0, i)),
-                ],
-                out_specs=[out_spec] * 4,
-                scratch_shapes=[
-                    pltpu.VMEM((slots, hidden_width), BF16),
-                    pltpu.VMEM((slots, hidden_width), BF16),
-                    pltpu.VMEM((slots, ROW_EXTRA), BF16),
-                ],
-            ),
-            compiler_params=pltpu.CompilerParams(vmem_limit_bytes=40 * 2**20),
-            cost_estimate=pl.CostEstimate(
-                flops=4 * slots * width * hidden_width, bytes_accessed=4 * width * hidden_width, transcendentals=0
-            ),
-        )(numbers, a_all, b_all, hidden_all, info_all, hidden_grad, gate_w, up_w, router_rows)
-        back = [grads[0]] + [swap_e(grads[way], way) for way in (1, 2, 3)]
-        rows_spec = pl.BlockSpec((capacity, width), lambda i, n: (0, 0))
-        summed = pl.pallas_call(
+            [
+                (a_all, block(hidden_width)),
+                (b_all, block(hidden_width)),
+                (hidden_all, block(hidden_width)),
+                (info_all, block(ROW_EXTRA)),
+                whole(hidden_grad),
+                (gate_w, weight_spec),
+                (up_w, weight_spec),
+                (router_rows, pl.BlockSpec((ROW_EXTRA, tile), lambda j, n: (0, j))),
+            ],
+            [(shape((capacity, width), BF16), pl.BlockSpec((capacity, tile), lambda j, n: (0, j)))] * 4,
+            steps=width // tile,
+            scratch=[
+                pltpu.VMEM((slots, hidden_width), BF16),
+                pltpu.VMEM((slots, hidden_width), BF16),
+                pltpu.VMEM((slots, ROW_EXTRA), BF16),
+            ],
+            flops=4 * slots * width * hidden_width,
+        )
+        returned[k] = [grads[0]] + [swap_e(grads[way], way) for way in (1, 2, 3)]
+
+    def combine(k):
+        sums[k] = chain(
             combine_kernel,
-            out_shape=jax.ShapeDtypeStruct((rows, width), F32),
-            grid_spec=pltpu.PrefetchScalarGridSpec(
-                num_scalar_prefetch=1,
-                grid=(1,),
-                in_specs=[pl.BlockSpec((1, rows, slots), lambda i, n: (n[0], 0, 0))] + [rows_spec] * 4,
-                out_specs=pl.BlockSpec((rows, width), lambda i, n: (0, 0)),
-            ),
-            compiler_params=pltpu.CompilerParams(vmem_limit_bytes=40 * 2**20),
-            cost_estimate=pl.CostEstimate(
-                flops=2 * slots * rows * width, bytes_accessed=8 * rows * width, transcendentals=0
-            ),
-        )(numbers, place_all, *back)
-        sums.append(summed)
-
-    def narrow(value):
-        return value.astype(BF16)
-
-    got1 = along_z(narrow(sums[0]), LEAVES_IN)
-    got2 = along_z(narrow(sums[1]), LEAVES_IN)
-    got3 = along_z(narrow(sums[0] + got1.astype(F32)), INNER_SWAP)
-    got4 = along_z(narrow(sums[2]), LEAVES_IN)
-    got5 = along_z(narrow(sums[2] + got2.astype(F32)), INNER_SWAP)
-    got6 = along_z(narrow(sums[1] + got3.astype(F32)), LEAVES_OUT)
-    grad = whole_call(
+            [(place_all, pl.BlockSpec((1, rows, slots), lambda j, n: (n[ORDER + k], 0, 0)))]
+            + [whole(r) for r in returned[k]],
+            [(shape((rows, width), kind), fixed((rows, width))) for kind in (F32, BF16)],
+            flops=2 * slots * rows * width,
+        )
+
+    backward(0)
+    backward(1)
+    backward(2)
+    combine(0)
+    got1 = along_z(sums[0][1], LEAVES_IN)
+    backward(3)
+    combine(1)
+    got2 = along_z(sums[1][1], LEAVES_IN)
+    got3 = along_z(add(sums[0][0], got1), INNER_SWAP)
+    combine(2)
+    got4 = along_z(sums[2][1], LEAVES_IN)
+    combine(3)
+    got5 = along_z(add(sums[2][0], got2), INNER_SWAP)
+    got6 = along_z(add(sums[1][0], got3), LEAVES_OUT)
+    (grad,) = chain(
         finish_kernel,
-        jax.ShapeDtypeStruct((rows, width), BF16),
-        total_own,
-        gain,
-        dembedded,
-        token_own,
-        sums[3],
-        got4,
-        got5,
-        got6,
+        [own_rows, whole(gain), whole(dembedded), own_tokens]
+        + [whole(value) for value in (sums[3][0], got4, got5, got6)],
+        [(shape((rows, width), BF16), fixed((rows, width)))],
         flops=4 * rows * sequences * width,
     )
     return loss[0, :1], grad

time: 283 us -> 231 us (0.82)
  waiting for transfers between devices: 139 us -> 66.9 us
  Pallas kernels: 46 us -> 69.5 us
  starting transfers between devices: 64.2 us -> 82.2 us
  matrix products: 12.2 us -> 0 us
  other arithmetic: 11.4 us -> 1.19 us
    ppermute x21, waiting for transfers between devices: 94.2 us -> 37 us  [along_z(): return lax.ppermute(value, 'tensor', pairs)]
    pallas_call x19 -> x37, Pallas kernels: 46 us -> 69.5 us  [__call__(): pl.pallas_call(kernel, out_shape=list(shapes), grid_spec=pltpu.PrefetchSc...]
    ppermute x21, starting transfers between devices: 39.9 us -> 56.1 us  [along_z(): return lax.ppermute(value, 'tensor', pairs)]
    ppermute x30, waiting for transfers between devices: 40.1 us -> 25.2 us  [swap_e(): return lax.ppermute(value, 'expert', [(i, i ^ bits) for i in range(4)])]
    dot_general x4 -> x0, matrix products: 12.2 us -> none  [fast_body(): jnp.dot(context[c * rows:(c + 1) * rows], o_weight, preferred_element_typ...]
    convert_element_type x12 -> x0, other arithmetic: 4.62 us -> none  [the longest x4 3.63 us: fast_body(): half = (part.astype(F32) + arrived.astype(F32)).astype(BF16)]
    another operation x10 -> x2, other arithmetic: 3.51 us -> 0.19 us  [the longest x4 2.75 us: fast_body(): numbers = jnp.stack([order[j], own_expert])]
    select_n x2 -> x0, other arithmetic: 2.93 us -> none  [the longest x1 2.92 us: fast_body(): total_own = lax.select_n(z, *totals)]
  transfers between devices with their start and end apart: 54 -> 54, of which waited for: 23 -> 22; matrix products, arithmetic and copies ran while one was open for 7% -> 0% of each run, Pallas kernels for 11% -> 23%
where the time goes in v2:
time: 231 us; the launch traced here: 230 us
  starting transfers between devices  82.2 us (36%)
  Pallas kernels  69.5 us (30%)
  waiting for transfers between devices  66.9 us (29%)
  local copies, waits for them, and re-layouts  8.93 us (4%)
    pallas_call x37, Pallas kernels, __call__(): pl.pallas_call(kernel, out_shape=list(shapes), grid_spec=pltpu.PrefetchSc...  69.5 us
    ppermute x21, starting transfers between devices, along_z(): return lax.ppermute(value, 'tensor', pairs)  56.1 us
    ppermute x21, waiting for transfers between devices, along_z(): return lax.ppermute(value, 'tensor', pairs)  37 us
    ppermute x30, waiting for transfers between devices, swap_e(): return lax.ppermute(value, 'expert', [(i, i ^ bits) for i in range(4)])  25.2 us
    ppermute x30, starting transfers between devices, swap_e(): return lax.ppermute(value, 'expert', [(i, i ^ bits) for i in range(4)])  21.6 us
    unnamed x30, local copies, waits for them, and re-layouts  8.05 us
    ppermute x3, waiting for transfers between devices, swap_z(): return lax.ppermute(value, 'tensor', [(i, i ^ bits) for i in range(4)])  4.75 us
  transfers between devices with their start and end apart: 54, of which 22 were waited for; matrix products, arithmetic and copies ran while one was open for 0% of the time, Pallas kernels for 23%

profile of v2, /device:TPU:0, one launch (start us, length us, event | category | flops | bytes accessed | tf_op | source)
XLA Modules:
  0.0 230.2 jit_solution(12388774542779123705)
XLA Ops:
  7.3 2.3 shard_map.122.rest_0_.left_ref
  9.6 5.0 %collective-permute-start = (bf16[144,2048]{1,0:T(8,128)(2,1)S(1)}, bf16[144,2048]{1,0:T(8,128)(2,1)S(1)}, u32[]{:S(2)}, u32[]{:S(2)}) collective-permute-start(bf16[144,2048]{1,0:T(8,128)(2,1)S(1)} %shard_map.122.rest_0_.left_ref), channel_id=1, source_target_pairs={{0,1},{3,2},{4,5},{7,6},{8,9},{11,10},{12,13},{15,14},{16,17},{19,... | collective-permute-start | bytes 1769480 | tf_op jit(solution)/shard_map/ppermute | solution.py:543
  14.6 2.3 shard_map.123.rest_0_.left_ref
  18.2 2.3 shard_map.124._.left_ref
  20.5 7.8 %collective-permute-done.right_ref = bf16[144,2048]{1,0:T(8,128)(2,1)S(1)} collective-permute-done((bf16[144,2048]{1,0:T(8,128)(2,1)S(1)}, bf16[144,2048]{1,0:T(8,128)(2,1)S(1)}, u32[]{:S(2)}, u32[]{:S(2)}) %collective-permute-start) | collective-permute-done | bytes 589856 | tf_op jit(solution)/shard_map/ppermute | solution.py:543
  30.5 7.2 %collective-permute-start.5 = (bf16[128,2048]{1,0:T(8,128)(2,1)S(1)}, bf16[128,2048]{1,0:T(8,128)(2,1)}, u32[]{:S(2)}, u32[]{:S(2)}) collective-permute-start(bf16[128,2048]{1,0:T(8,128)(2,1)S(1)} %shard_map.124._.left_ref), channel_id=1, source_target_pairs={{0,1},{3,2},{4,5},{7,6},{8,9},{11,10},{12,13},{15,14},{16,17},{19,... | collective-permute-start | bytes 1572872 | tf_op jit(solution)/shard_map/ppermute | solution.py:543
  37.6 2.2 shard_map.126._.left_ref
  55.3 10.2 %collective-permute-start.11 = (bf16[64,2048]{1,0:T(8,128)(2,1)S(1)}, bf16[64,2048]{1,0:T(8,128)(2,1)S(1)}, u32[]{:S(2)}, u32[]{:S(2)}) collective-permute-start(bf16[64,2048]{1,0:T(8,128)(2,1)S(1)} %shard_map.126._.left_ref), channel_id=1, source_target_pairs={{0,1},{3,2},{4,5},{7,6},{8,9},{11,10},{12,13},{15,14},{16,17},{19,... | collective-permute-start | bytes 786440 | tf_op jit(solution)/shard_map/ppermute | solution.py:543
  69.4 4.4 %collective-permute-start.16 = (bf16[64,2048]{1,0:T(8,128)(2,1)S(1)}, bf16[64,2048]{1,0:T(8,128)(2,1)S(1)}, u32[]{:S(2)}, u32[]{:S(2)}) collective-permute-start(bf16[64,2048]{1,0:T(8,128)(2,1)S(1)} %shard_map.129._.left_ref), channel_id=1, source_target_pairs={{0,1},{3,2},{4,5},{7,6},{8,9},{11,10},{12,13},{15,14},{16,17},{19,... | collective-permute-start | bytes 786440 | tf_op jit(solution)/shard_map/ppermute | solution.py:543
  78.8 3.5 %shard_map.136 = (f32[32,768]{1,0:T(8,128)S(1)}, bf16[4,160,768]{2,1,0:T(8,128)(2,1)S(1)}, f32[4,160,768]{2,1,0:T(8,128)S(1)}, f32[4,160,768]{2,1,0:T(8,128)S(1)}, f32[4,160,128]{2,1,0:T(8,128)S(1)}) custom-call(s32[15]{0:T(128)S(1)} %concatenate.10.n, bf16[40,2176]{1,0:T(8,128)(2,1)S(1)} %get-tuple-element.77._.r0, ...), custom_call_target="tpu_custom_call" | custom-call | flops 1006632960 | bytes 7161856 | tf_op jit(solution)/shard_map/pallas_call | solution.py:487
  88.9 2.9 %collective-permute-done.15.refs_1_ = bf16[128,2048]{1,0:T(8,128)(2,1)S(1)} collective-permute-done((bf16[128,2048]{1,0:T(8,128)(2,1)S(1)}, bf16[128,2048]{1,0:T(8,128)(2,1)S(1)}, u32[]{:S(2)}, u32[]{:S(2)}) %collective-permute-start.15) | collective-permute-done | bytes 524320 | tf_op jit(solution)/shard_map/ppermute | solution.py:543
  96.6 3.5 %shard_map.141 = (f32[32,768]{1,0:T(8,128)S(1)}, bf16[4,160,768]{2,1,0:T(8,128)(2,1)S(1)}, f32[4,160,768]{2,1,0:T(8,128)S(1)}, f32[4,160,768]{2,1,0:T(8,128)S(1)}, f32[4,160,128]{2,1,0:T(8,128)S(1)}) custom-call(s32[15]{0:T(128)S(1)} %concatenate.10.n, ...), custom_call_target="tpu_custom_call", output_to_operand_aliasing={{1}: (7, {}), {2}: (8, {}), {3}: (9, {}), {4}: (10, {})} | custom-call | flops 1006632960 | bytes 12404736 | tf_op jit(solution)/shard_map/pallas_call | solution.py:487
  100.1 6.4 %collective-permute-done.22.refs_2_ = bf16[64,2048]{1,0:T(8,128)(2,1)S(1)} collective-permute-done((bf16[64,2048]{1,0:T(8,128)(2,1)S(1)}, bf16[64,2048]{1,0:T(8,128)(2,1)S(1)}, u32[]{:S(2)}, u32[]{:S(2)}) %collective-permute-start.22) | collective-permute-done | bytes 262176 | tf_op jit(solution)/shard_map/ppermute | solution.py:543
  106.5 4.9 %collective-permute-done.23.refs_3_ = bf16[64,2048]{1,0:T(8,128)(2,1)S(1)} collective-permute-done((bf16[64,2048]{1,0:T(8,128)(2,1)S(1)}, bf16[64,2048]{1,0:T(8,128)(2,1)S(1)}, u32[]{:S(2)}, u32[]{:S(2)}) %collective-permute-start.23) | collective-permute-done | bytes 262176 | tf_op jit(solution)/shard_map/ppermute | solution.py:543
  114.7 3.5 %shard_map.143 = (f32[32,768]{1,0:T(8,128)S(1)}, bf16[4,160,768]{2,1,0:T(8,128)(2,1)S(1)}, f32[4,160,768]{2,1,0:T(8,128)S(1)}, f32[4,160,768]{2,1,0:T(8,128)S(1)}, f32[4,160,128]{2,1,0:T(8,128)S(1)}) custom-call(s32[15]{0:T(128)S(1)} %concatenate.10.n, ...), custom_call_target="tpu_custom_call", output_to_operand_aliasing={{1}: (7, {}), {2}: (8, {}), {3}: (9, {}), {4}: (10, {})} | custom-call | flops 1006632960 | bytes 12404736 | tf_op jit(solution)/shard_map/pallas_call | solution.py:487
  120.1 2.8 %collective-permute-done.26.r3 = bf16[40,2176]{1,0:T(8,128)(2,1)S(1)} collective-permute-done((bf16[40,2176]{1,0:T(8,128)(2,1)S(1)}, bf16[40,2176]{1,0:T(8,128)(2,1)S(1)}, u32[]{:S(2)}, u32[]{:S(2)}) %collective-permute-start.26) | collective-permute-done | bytes 174112 | tf_op jit(solution)/shard_map/ppermute | solution.py:549
  123.0 3.5 %shard_map.144 = (f32[32,768]{1,0:T(8,128)S(1)}, bf16[4,160,768]{2,1,0:T(8,128)(2,1)S(1)}, f32[4,160,768]{2,1,0:T(8,128)S(1)}, f32[4,160,768]{2,1,0:T(8,128)S(1)}, f32[4,160,128]{2,1,0:T(8,128)S(1)}) custom-call(s32[15]{0:T(128)S(1)} %concatenate.10.n, ...), custom_call_target="tpu_custom_call", output_to_operand_aliasing={{1}: (7, {}), {2}: (8, {}), {3}: (9, {}), {4}: (10, {})} | custom-call | flops 1006632960 | bytes 12328960 | tf_op jit(solution)/shard_map/pallas_call | solution.py:487
  129.7 3.3 %collective-permute-done.28 = f32[8,2048]{1,0:T(8,128)S(1)} collective-permute-done((f32[8,2048]{1,0:T(8,128)S(1)}, f32[8,2048]{1,0:T(8,128)S(1)}, u32[]{:S(2)}, u32[]{:S(2)}) %collective-permute-start.28) | collective-permute-done | bytes 65568 | tf_op jit(solution)/shard_map/ppermute | solution.py:549
  133.2 3.0 %collective-permute-start.31 = (f32[8,2048]{1,0:T(8,128)S(1)}, f32[8,2048]{1,0:T(8,128)S(1)}, u32[]{:S(2)}, u32[]{:S(2)}) collective-permute-start(f32[8,2048]{1,0:T(8,128)S(1)} %add_add_fusion.1), channel_id=1, source_target_pairs={{0,2},{1,3},{2,0},{3,1},{4,6},{5,7},{6,4},{7,5},{8,10},{9,11},{10,... | collective-permute-start | bytes 196616 | tf_op jit(solution)/shard_map/ppermute | solution.py:546
  144.3 2.7 %collective-permute-done.34.q2 = f32[8,2048]{1,0:T(8,128)S(1)} collective-permute-done((f32[8,2048]{1,0:T(8,128)S(1)}, f32[8,2048]{1,0:T(8,128)S(1)}, u32[]{:S(2)}, u32[]{:S(2)}) %collective-permute-start.34) | collective-permute-done | bytes 65568 | tf_op jit(solution)/shard_map/ppermute | solution.py:549
  148.0 3.3 %shard_map.146 = (f32[1,128]{1,0:T(1,128)}, f32[32,2048]{1,0:T(8,128)S(1)}, f32[32,768]{1,0:T(8,128)S(1)}) custom-call(s32[15]{0:T(128)S(1)} %concatenate.10.n, f32[8,2048]{1,0:T(8,128)S(1)} %add_add_fusion.q0, f32[8,2048]{1,0:T(8,128)S(1)} %collective-permute-done.33.q1, f32[8,2048]{1,0:T(8,128)S(1)} %collective-permute-done.34.q2, ...), custom_call_target="tpu_custom_call" | custom-call | flops 201326592 | bytes 3473408 | tf_op jit(solution)/shard_map/pallas_call | solution.py:487
  152.0 4.1 %shard_map.147 = (bf16[40,2048]{1,0:T(8,128)(2,1)S(1)}, bf16[40,2048]{1,0:T(8,128)(2,1)S(1)}, bf16[40,2048]{1,0:T(8,128)(2,1)S(1)}, bf16[40,2048]{1,0:T(8,128)(2,1)S(1)}) custom-call(s32[15]{0:T(128)S(1)} %concatenate.10.n, f32[4,160,768]{2,1,0:T(8,128)S(1)} %get-tuple-element.124.a_ref, f32[4,160,768]{2,1,0:T(8,128)S(1)} %get-tuple-element.125.b_ref, ...), custom_call_target="tpu_custom_call" | custom-call | flops 1006632960 | bytes 12157440 | tf_op jit(solution)/shard_map/pallas_call | solution.py:487
  158.1 4.1 %shard_map.148 = (bf16[40,2048]{1,0:T(8,128)(2,1)S(1)}, bf16[40,2048]{1,0:T(8,128)(2,1)S(1)}, bf16[40,2048]{1,0:T(8,128)(2,1)S(1)}, bf16[40,2048]{1,0:T(8,128)(2,1)S(1)}) custom-call(s32[15]{0:T(128)S(1)} %concatenate.10.n, f32[4,160,768]{2,1,0:T(8,128)S(1)} %get-tuple-element.124.a_ref, f32[4,160,768]{2,1,0:T(8,128)S(1)} %get-tuple-element.125.b_ref, ...), custom_call_target="tpu_custom_call" | custom-call | flops 1006632960 | bytes 12320768 | tf_op jit(solution)/shard_map/pallas_call | solution.py:487
  162.2 4.1 %shard_map.149 = (bf16[40,2048]{1,0:T(8,128)(2,1)S(1)}, bf16[40,2048]{1,0:T(8,128)(2,1)S(1)}, bf16[40,2048]{1,0:T(8,128)(2,1)S(1)}, bf16[40,2048]{1,0:T(8,128)(2,1)S(1)}) custom-call(s32[15]{0:T(128)S(1)} %concatenate.10.n, f32[4,160,768]{2,1,0:T(8,128)S(1)} %get-tuple-element.124.a_ref, f32[4,160,768]{2,1,0:T(8,128)S(1)} %get-tuple-element.125.b_ref, ...), custom_call_target="tpu_custom_call" | custom-call | flops 1006632960 | bytes 12320768 | tf_op jit(solution)/shard_map/pallas_call | solution.py:487
  167.1 3.0 %collective-permute-start.45 = (bf16[128,2048]{1,0:T(8,128)(2,1)S(1)}, bf16[128,2048]{1,0:T(8,128)(2,1)S(1)}, u32[]{:S(2)}, u32[]{:S(2)}) collective-permute-start(bf16[128,2048]{1,0:T(8,128)(2,1)S(1)} %get-tuple-element.143), channel_id=1, source_target_pairs={{0,1},{3,2},{4,5},{7,6},{8,9},{11,10},{12,13},{15,14},{16,17},{19,... | collective-permute-start | bytes 1572872 | tf_op jit(solution)/shard_map/ppermute | solution.py:543
  172.0 4.1 %shard_map.151 = (bf16[40,2048]{1,0:T(8,128)(2,1)S(1)}, bf16[40,2048]{1,0:T(8,128)(2,1)S(1)}, bf16[40,2048]{1,0:T(8,128)(2,1)S(1)}, bf16[40,2048]{1,0:T(8,128)(2,1)S(1)}) custom-call(s32[15]{0:T(128)S(1)} %concatenate.10.n, f32[4,160,768]{2,1,0:T(8,128)S(1)} %get-tuple-element.124.a_ref, f32[4,160,768]{2,1,0:T(8,128)S(1)} %get-tuple-element.125.b_ref, ...), custom_call_target="tpu_custom_call" | custom-call | flops 1006632960 | bytes 13205504 | tf_op jit(solution)/shard_map/pallas_call | solution.py:487
  177.4 2.2 collective-permute-done.48.r3
  185.9 4.9 %collective-permute-done.43.r2 = bf16[40,2048]{1,0:T(8,128)(2,1)S(1)} collective-permute-done((bf16[40,2048]{1,0:T(8,128)(2,1)S(1)}, bf16[40,2048]{1,0:T(8,128)(2,1)S(1)}, u32[]{:S(2)}, u32[]{:S(2)}) %collective-permute-start.43) | collective-permute-done | bytes 163872 | tf_op jit(solution)/shard_map/ppermute | solution.py:549
  202.6 9.2 %collective-permute-start.49 = (bf16[128,2048]{1,0:T(8,128)(2,1)S(1)}, bf16[128,2048]{1,0:T(8,128)(2,1)S(1)}, u32[]{:S(2)}, u32[]{:S(2)}) collective-permute-start(bf16[128,2048]{1,0:T(8,128)(2,1)S(1)} %get-tuple-element.150), channel_id=1, source_target_pairs={{0,1},{3,2},{4,5},{7,6},{8,9},{11,10},{12,13},{15,14},{16,17},{19,... | collective-permute-start | bytes 1572872 | tf_op jit(solution)/shard_map/ppermute | solution.py:543
  213.7 9.4 %collective-permute-done.49.r4 = bf16[128,2048]{1,0:T(8,128)(2,1)S(1)} collective-permute-done((bf16[128,2048]{1,0:T(8,128)(2,1)S(1)}, bf16[128,2048]{1,0:T(8,128)(2,1)S(1)}, u32[]{:S(2)}, u32[]{:S(2)}) %collective-permute-start.49) | collective-permute-done | bytes 524320 | tf_op jit(solution)/shard_map/ppermute | solution.py:543
  223.2 4.8 %collective-permute-done.53.r6 = bf16[128,2048]{1,0:T(8,128)(2,1)S(1)} collective-permute-done((bf16[128,2048]{1,0:T(8,128)(2,1)S(1)}, bf16[128,2048]{1,0:T(8,128)(2,1)S(1)}, u32[]{:S(2)}, u32[]{:S(2)}) %collective-permute-start.53) | collective-permute-done | bytes 524320 | tf_op jit(solution)/shard_map/ppermute | solution.py:543
  227.9 2.2 shard_map.158
  (160 shorter events, 89.9 us)
Async XLA Ops:
  9.6 18.7 %collective-permute-start = (bf16[144,2048]{1,0:T(8,128)(2,1)S(1)}, bf16[144,2048]{1,0:T(8,128)(2,1)S(1)}, u32[]{:S(2)}, u32[]{:S(2)}) collective-permute-start(bf16[144,2048]{1,0:T(8,128)(2,1)S(1)} %shard_map.122.rest_0_.left_ref), channel_id=1, source_target_pairs={{0,1},{3,2},{4,5},{7,6},{8,9},{11,10},{12,13},{15,14},{16,17},{19,... | collective-permute-start | bytes 1769480 | tf_op jit(solution)/shard_map/ppermute | solution.py:543
  16.8 23.0 %collective-permute-start.2 = (bf16[128,2048]{1,0:T(8,128)(2,1)S(1)}, bf16[128,2048]{1,0:T(8,128)(2,1)S(1)}, u32[]{:S(2)}, u32[]{:S(2)}) collective-permute-start(bf16[128,2048]{1,0:T(8,128)(2,1)S(1)} %shard_map.123.rest_0_.left_ref), channel_id=1, source_target_pairs={{0,1},{3,2},{4,5},{7,6},{8,9},{11,10},{12,13},{15,14},{16,17},{19,... | collective-permute-start | bytes 1572872 | tf_op jit(solution)/shard_map/ppermute | solution.py:543
  28.9 13.4 %collective-permute-start.1 = (bf16[144,2048]{1,0:T(8,128)(2,1)S(1)}, bf16[144,2048]{1,0:T(8,128)(2,1)}, u32[]{:S(2)}, u32[]{:S(2)}) collective-permute-start(bf16[144,2048]{1,0:T(8,128)(2,1)S(1)} %shard_map.125.rest_0_.left_ref), channel_id=1, source_target_pairs={{1,2},{2,1},{5,6},{6,5},{9,10},{10,9},{13,14},{14,13},{17,18},{18,... | collective-permute-start | bytes 1769480 | tf_op jit(solution)/shard_map/ppermute | solution.py:543
  30.5 19.4 %collective-permute-start.5 = (bf16[128,2048]{1,0:T(8,128)(2,1)S(1)}, bf16[128,2048]{1,0:T(8,128)(2,1)}, u32[]{:S(2)}, u32[]{:S(2)}) collective-permute-start(bf16[128,2048]{1,0:T(8,128)(2,1)S(1)} %shard_map.124._.left_ref), channel_id=1, source_target_pairs={{0,1},{3,2},{4,5},{7,6},{8,9},{11,10},{12,13},{15,14},{16,17},{19,... | collective-permute-start | bytes 1572872 | tf_op jit(solution)/shard_map/ppermute | solution.py:543
  40.5 11.7 %collective-permute-start.4 = (bf16[128,2048]{1,0:T(8,128)(2,1)S(1)}, bf16[128,2048]{1,0:T(8,128)(2,1)}, u32[]{:S(2)}, u32[]{:S(2)}) collective-permute-start(bf16[128,2048]{1,0:T(8,128)(2,1)S(1)} %shard_map.127._.left_ref), channel_id=1, source_target_pairs={{1,2},{2,1},{5,6},{6,5},{9,10},{10,9},{13,14},{14,13},{17,18},{18,... | collective-permute-start | bytes 1572872 | tf_op jit(solution)/shard_map/ppermute | solution.py:543
  44.0 21.6 %collective-permute-start.3 = (bf16[144,2048]{1,0:T(8,128)(2,1)S(1)}, bf16[144,2048]{1,0:T(8,128)(2,1)S(1)}, u32[]{:S(2)}, u32[]{:S(2)}) collective-permute-start(bf16[144,2048]{1,0:T(8,128)(2,1)S(1)} %shard_map.128.rest_0_.refs_0_), channel_id=1, source_target_pairs={{1,0},{2,3},{5,4},{6,7},{9,8},{10,11},{13,12},{14,15},{17,16},{18,... | collective-permute-start | bytes 1769480 | tf_op jit(solution)/shard_map/ppermute | solution.py:543
  51.5 17.9 %collective-permute-start.10 = (bf16[128,2048]{1,0:T(8,128)(2,1)S(1)}, bf16[128,2048]{1,0:T(8,128)(2,1)S(1)}, u32[]{:S(2)}, u32[]{:S(2)}) collective-permute-start(bf16[128,2048]{1,0:T(8,128)(2,1)S(1)} %shard_map.130._.left_ref), channel_id=1, source_target_pairs={{1,2},{2,1},{5,6},{6,5},{9,10},{10,9},{13,14},{14,13},{17,18},{18,... | collective-permute-start | bytes 1572872 | tf_op jit(solution)/shard_map/ppermute | solution.py:543
  53.9 21.1 %collective-permute-start.9 = (bf16[128,2048]{1,0:T(8,128)(2,1)S(1)}, bf16[128,2048]{1,0:T(8,128)(2,1)S(1)}, u32[]{:S(2)}, u32[]{:S(2)}) collective-permute-start(bf16[128,2048]{1,0:T(8,128)(2,1)S(1)} %shard_map.131.refs_5_.refs_0_), channel_id=1, source_target_pairs={{1,0},{2,3},{5,4},{6,7},{9,8},{10,11},{13,12},{14,15},{17,16},{18,... | collective-permute-start | bytes 1572872 | tf_op jit(solution)/shard_map/ppermute | solution.py:543
  55.3 14.0 %collective-permute-start.11 = (bf16[64,2048]{1,0:T(8,128)(2,1)S(1)}, bf16[64,2048]{1,0:T(8,128)(2,1)S(1)}, u32[]{:S(2)}, u32[]{:S(2)}) collective-permute-start(bf16[64,2048]{1,0:T(8,128)(2,1)S(1)} %shard_map.126._.left_ref), channel_id=1, source_target_pairs={{0,1},{3,2},{4,5},{7,6},{8,9},{11,10},{12,13},{15,14},{16,17},{19,... | collective-permute-start | bytes 786440 | tf_op jit(solution)/shard_map/ppermute | solution.py:543
  67.1 11.0 %collective-permute-start.6 = (bf16[40,2176]{1,0:T(8,128)(2,1)S(1)}, bf16[40,2176]{1,0:T(8,128)(2,1)S(1)}, u32[]{:S(2)}, u32[]{:S(2)}) collective-permute-start(bf16[40,2176]{1,0:T(8,128)(2,1)S(1)} %get-tuple-element.78), channel_id=1, source_target_pairs={{0,4},{4,0},{8,12},{12,8},{1,5},{5,1},{9,13},{13,9},{2,6},{6,2},{1... | collective-permute-start | bytes 522248 | tf_op jit(solution)/shard_map/ppermute | solution.py:549
  67.1 11.6 %collective-permute-start.7 = (bf16[40,2176]{1,0:T(8,128)(2,1)S(1)}, bf16[40,2176]{1,0:T(8,128)(2,1)S(1)}, u32[]{:S(2)}, u32[]{:S(2)}) collective-permute-start(bf16[40,2176]{1,0:T(8,128)(2,1)S(1)} %get-tuple-element.79), channel_id=1, source_target_pairs={{0,8},{4,12},{8,0},{12,4},{1,9},{5,13},{9,1},{13,5},{2,10},{6,14},... | collective-permute-start | bytes 522248 | tf_op jit(solution)/shard_map/ppermute | solution.py:549
  69.4 9.4 %collective-permute-start.8 = (bf16[40,2176]{1,0:T(8,128)(2,1)S(1)}, bf16[40,2176]{1,0:T(8,128)(2,1)S(1)}, u32[]{:S(2)}, u32[]{:S(2)}) collective-permute-start(bf16[40,2176]{1,0:T(8,128)(2,1)S(1)} %get-tuple-element.80), channel_id=1, source_target_pairs={{0,12},{4,8},{8,4},{12,0},{1,13},{5,9},{9,5},{13,1},{2,14},{6,10},... | collective-permute-start | bytes 522248 | tf_op jit(solution)/shard_map/ppermute | solution.py:549
  69.4 12.9 %collective-permute-start.16 = (bf16[64,2048]{1,0:T(8,128)(2,1)S(1)}, bf16[64,2048]{1,0:T(8,128)(2,1)S(1)}, u32[]{:S(2)}, u32[]{:S(2)}) collective-permute-start(bf16[64,2048]{1,0:T(8,128)(2,1)S(1)} %shard_map.129._.left_ref), channel_id=1, source_target_pairs={{0,1},{3,2},{4,5},{7,6},{8,9},{11,10},{12,13},{15,14},{16,17},{19,... | collective-permute-start | bytes 786440 | tf_op jit(solution)/shard_map/ppermute | solution.py:543
  75.1 16.7 %collective-permute-start.15 = (bf16[128,2048]{1,0:T(8,128)(2,1)S(1)}, bf16[128,2048]{1,0:T(8,128)(2,1)S(1)}, u32[]{:S(2)}, u32[]{:S(2)}) collective-permute-start(bf16[128,2048]{1,0:T(8,128)(2,1)S(1)} %shard_map.134.refs_8_.refs_0_), channel_id=1, source_target_pairs={{1,0},{2,3},{5,4},{6,7},{9,8},{10,11},{13,12},{14,15},{17,16},{18,... | collective-permute-start | bytes 1572872 | tf_op jit(solution)/shard_map/ppermute | solution.py:543
  83.6 11.0 %collective-permute-start.12 = (bf16[40,2176]{1,0:T(8,128)(2,1)S(1)}, bf16[40,2176]{1,0:T(8,128)(2,1)S(1)}, u32[]{:S(2)}, u32[]{:S(2)}) collective-permute-start(bf16[40,2176]{1,0:T(8,128)(2,1)S(1)} %get-tuple-element.86), channel_id=1, source_target_pairs={{0,4},{4,0},{8,12},{12,8},{1,5},{5,1},{9,13},{13,9},{2,6},{6,2},{1... | collective-permute-start | bytes 522248 | tf_op jit(solution)/shard_map/ppermute | solution.py:549
  85.0 10.1 %collective-permute-start.13 = (bf16[40,2176]{1,0:T(8,128)(2,1)S(1)}, bf16[40,2176]{1,0:T(8,128)(2,1)S(1)}, u32[]{:S(2)}, u32[]{:S(2)}) collective-permute-start(bf16[40,2176]{1,0:T(8,128)(2,1)S(1)} %get-tuple-element.87), channel_id=1, source_target_pairs={{0,8},{4,12},{8,0},{12,4},{1,9},{5,13},{9,1},{13,5},{2,10},{6,14},... | collective-permute-start | bytes 522248 | tf_op jit(solution)/shard_map/ppermute | solution.py:549
  85.5 10.4 %collective-permute-start.14 = (bf16[40,2176]{1,0:T(8,128)(2,1)S(1)}, bf16[40,2176]{1,0:T(8,128)(2,1)S(1)}, u32[]{:S(2)}, u32[]{:S(2)}) collective-permute-start(bf16[40,2176]{1,0:T(8,128)(2,1)S(1)} %get-tuple-element.88), channel_id=1, source_target_pairs={{0,12},{4,8},{8,4},{12,0},{1,13},{5,9},{9,5},{13,1},{2,14},{6,10},... | collective-permute-start | bytes 522248 | tf_op jit(solution)/shard_map/ppermute | solution.py:549
  87.0 19.5 %collective-permute-start.22 = (bf16[64,2048]{1,0:T(8,128)(2,1)S(1)}, bf16[64,2048]{1,0:T(8,128)(2,1)S(1)}, u32[]{:S(2)}, u32[]{:S(2)}) collective-permute-start(bf16[64,2048]{1,0:T(8,128)(2,1)S(1)} %shard_map.138._.refs_0_), channel_id=1, source_target_pairs={{1,0},{2,3},{5,4},{6,7},{9,8},{10,11},{13,12},{14,15},{17,16},{18,... | collective-permute-start | bytes 786440 | tf_op jit(solution)/shard_map/ppermute | solution.py:543
  91.8 19.6 %collective-permute-start.23 = (bf16[64,2048]{1,0:T(8,128)(2,1)S(1)}, bf16[64,2048]{1,0:T(8,128)(2,1)S(1)}, u32[]{:S(2)}, u32[]{:S(2)}) collective-permute-start(bf16[64,2048]{1,0:T(8,128)(2,1)S(1)} %shard_map.139.refs_8_.refs_1_), channel_id=1, source_target_pairs={{1,0},{2,3},{5,4},{6,7},{9,8},{10,11},{13,12},{14,15},{17,16},{18,... | collective-permute-start | bytes 786440 | tf_op jit(solution)/shard_map/ppermute | solution.py:543
  94.6 18.3 %collective-permute-start.19 = (bf16[40,2176]{1,0:T(8,128)(2,1)S(1)}, bf16[40,2176]{1,0:T(8,128)(2,1)S(1)}, u32[]{:S(2)}, u32[]{:S(2)}) collective-permute-start(bf16[40,2176]{1,0:T(8,128)(2,1)S(1)} %get-tuple-element.97), channel_id=1, source_target_pairs={{0,4},{4,0},{8,12},{12,8},{1,5},{5,1},{9,13},{13,9},{2,6},{6,2},{1... | collective-permute-start | bytes 522248 | tf_op jit(solution)/shard_map/ppermute | solution.py:549
  95.1 19.6 %collective-permute-start.20 = (bf16[40,2176]{1,0:T(8,128)(2,1)S(1)}, bf16[40,2176]{1,0:T(8,128)(2,1)S(1)}, u32[]{:S(2)}, u32[]{:S(2)}) collective-permute-start(bf16[40,2176]{1,0:T(8,128)(2,1)S(1)} %get-tuple-element.98), channel_id=1, source_target_pairs={{0,8},{4,12},{8,0},{12,4},{1,9},{5,13},{9,1},{13,5},{2,10},{6,14},... | collective-permute-start | bytes 522248 | tf_op jit(solution)/shard_map/ppermute | solution.py:549
  95.9 18.8 %collective-permute-start.21 = (bf16[40,2176]{1,0:T(8,128)(2,1)S(1)}, bf16[40,2176]{1,0:T(8,128)(2,1)S(1)}, u32[]{:S(2)}, u32[]{:S(2)}) collective-permute-start(bf16[40,2176]{1,0:T(8,128)(2,1)S(1)} %get-tuple-element.99), channel_id=1, source_target_pairs={{0,12},{4,8},{8,4},{12,0},{1,13},{5,9},{9,5},{13,1},{2,14},{6,10},... | collective-permute-start | bytes 522248 | tf_op jit(solution)/shard_map/ppermute | solution.py:549
  112.9 10.0 %collective-permute-start.26 = (bf16[40,2176]{1,0:T(8,128)(2,1)S(1)}, bf16[40,2176]{1,0:T(8,128)(2,1)S(1)}, u32[]{:S(2)}, u32[]{:S(2)}) collective-permute-start(bf16[40,2176]{1,0:T(8,128)(2,1)S(1)} %get-tuple-element.110), channel_id=1, source_target_pairs={{0,12},{4,8},{8,4},{12,0},{1,13},{5,9},{9,5},{13,1},{2,14},{6,10},... | collective-permute-start | bytes 522248 | tf_op jit(solution)/shard_map/ppermute | solution.py:549
  156.1 10.1 %collective-permute-start.36 = (bf16[40,2048]{1,0:T(8,128)(2,1)S(1)}, bf16[40,2048]{1,0:T(8,128)(2,1)S(1)}, u32[]{:S(2)}, u32[]{:S(2)}) collective-permute-start(bf16[40,2048]{1,0:T(8,128)(2,1)S(1)} %get-tuple-element.130), channel_id=1, source_target_pairs={{0,4},{4,0},{8,12},{12,8},{1,5},{5,1},{9,13},{13,9},{2,6},{6,2},{1... | collective-permute-start | bytes 491528 | tf_op jit(solution)/shard_map/ppermute | solution.py:549
  156.3 10.0 %collective-permute-start.37 = (bf16[40,2048]{1,0:T(8,128)(2,1)S(1)}, bf16[40,2048]{1,0:T(8,128)(2,1)S(1)}, u32[]{:S(2)}, u32[]{:S(2)}) collective-permute-start(bf16[40,2048]{1,0:T(8,128)(2,1)S(1)} %get-tuple-element.131), channel_id=1, source_target_pairs={{0,8},{4,12},{8,0},{12,4},{1,9},{5,13},{9,1},{13,5},{2,10},{6,14},... | collective-permute-start | bytes 491528 | tf_op jit(solution)/shard_map/ppermute | solution.py:549
  167.1 14.8 %collective-permute-start.45 = (bf16[128,2048]{1,0:T(8,128)(2,1)S(1)}, bf16[128,2048]{1,0:T(8,128)(2,1)S(1)}, u32[]{:S(2)}, u32[]{:S(2)}) collective-permute-start(bf16[128,2048]{1,0:T(8,128)(2,1)S(1)} %get-tuple-element.143), channel_id=1, source_target_pairs={{0,1},{3,2},{4,5},{7,6},{8,9},{11,10},{12,13},{15,14},{16,17},{19,... | collective-permute-start | bytes 1572872 | tf_op jit(solution)/shard_map/ppermute | solution.py:543
  180.5 20.8 %collective-permute-start.50 = (bf16[128,2048]{1,0:T(8,128)(2,1)S(1)}, bf16[128,2048]{1,0:T(8,128)(2,1)S(1)}, u32[]{:S(2)}, u32[]{:S(2)}) collective-permute-start(bf16[128,2048]{1,0:T(8,128)(2,1)S(1)} %get-tuple-element.151), channel_id=1, source_target_pairs={{0,1},{3,2},{4,5},{7,6},{8,9},{11,10},{12,13},{15,14},{16,17},{19,... | collective-permute-start | bytes 1572872 | tf_op jit(solution)/shard_map/ppermute | solution.py:543
  182.5 29.2 %collective-permute-start.52 = (bf16[128,2048]{1,0:T(8,128)(2,1)S(1)}, bf16[128,2048]{1,0:T(8,128)(2,1)S(1)}, u32[]{:S(2)}, u32[]{:S(2)}) collective-permute-start(bf16[128,2048]{1,0:T(8,128)(2,1)S(1)} %shard_map.153._), channel_id=1, source_target_pairs={{1,2},{2,1},{5,6},{6,5},{9,10},{10,9},{13,14},{14,13},{17,18},{18,... | collective-permute-start | bytes 1572872 | tf_op jit(solution)/shard_map/ppermute | solution.py:543
  185.2 10.4 %collective-permute-start.39 = (bf16[40,2048]{1,0:T(8,128)(2,1)S(1)}, bf16[40,2048]{1,0:T(8,128)(2,1)S(1)}, u32[]{:S(2)}, u32[]{:S(2)}) collective-permute-start(bf16[40,2048]{1,0:T(8,128)(2,1)S(1)} %get-tuple-element.137), channel_id=1, source_target_pairs={{0,4},{4,0},{8,12},{12,8},{1,5},{5,1},{9,13},{13,9},{2,6},{6,2},{1... | collective-permute-start | bytes 491528 | tf_op jit(solution)/shard_map/ppermute | solution.py:549
  201.9 11.8 %collective-permute-start.51 = (bf16[128,2048]{1,0:T(8,128)(2,1)S(1)}, bf16[128,2048]{1,0:T(8,128)(2,1)S(1)}, u32[]{:S(2)}, u32[]{:S(2)}) collective-permute-start(bf16[128,2048]{1,0:T(8,128)(2,1)S(1)} %shard_map.156._), channel_id=1, source_target_pairs={{1,2},{2,1},{5,6},{6,5},{9,10},{10,9},{13,14},{14,13},{17,18},{18,... | collective-permute-start | bytes 1572872 | tf_op jit(solution)/shard_map/ppermute | solution.py:543
  202.6 20.6 %collective-permute-start.49 = (bf16[128,2048]{1,0:T(8,128)(2,1)S(1)}, bf16[128,2048]{1,0:T(8,128)(2,1)S(1)}, u32[]{:S(2)}, u32[]{:S(2)}) collective-permute-start(bf16[128,2048]{1,0:T(8,128)(2,1)S(1)} %get-tuple-element.150), channel_id=1, source_target_pairs={{0,1},{3,2},{4,5},{7,6},{8,9},{11,10},{12,13},{15,14},{16,17},{19,... | collective-permute-start | bytes 1572872 | tf_op jit(solution)/shard_map/ppermute | solution.py:543
  212.4 15.5 %collective-permute-start.53 = (bf16[128,2048]{1,0:T(8,128)(2,1)S(1)}, bf16[128,2048]{1,0:T(8,128)(2,1)S(1)}, u32[]{:S(2)}, u32[]{:S(2)}) collective-permute-start(bf16[128,2048]{1,0:T(8,128)(2,1)S(1)} %shard_map.157._), channel_id=1, source_target_pairs={{1,0},{2,3},{5,4},{6,7},{9,8},{10,11},{13,12},{14,15},{17,16},{18,... | collective-permute-start | bytes 1572872 | tf_op jit(solution)/shard_map/ppermute | solution.py:543
  (37 other events, 233.6 us)

commit v3 on v2

--- a/solution.py
+++ b/solution.py
@@ -209,9 +209,12 @@
 LEAVES_IN = ((0, 1), (3, 2))
 INNER_SWAP = ((1, 2), (2, 1))
 LEAVES_OUT = ((1, 0), (2, 3))
-PIECES = (1, 1, 1, 2)
+PIECES = (1, 1, 1, 1)
 FORWARD_ORDER = (
-    "p0", "p1", "p2", "s0", "p3", "s1", "t0", "p4", "s2", "t1", "d0", "s3", "t2", "d1", "x0", "s4", "t3", "t4", "d2", "x1", "d3", "x2", "x3",
+    "p0", "p1", "p2", "s0", "p3", "s1", "t0", "s2", "t1", "s3", "d0", "t2", "d1", "t3", "x0", "d2", "x1", "d3", "x2", "x3",
+)
+BACKWARD_ORDER = (
+    "b0", "b1", "c0", "b2", "c1", "b3", "c2", "i0", "c3", "i1", "l0",
 )
 VMEM_LIMIT = 24 * 2**20
 BLOCK_ORDER = ((3, 2, 1, 0), (3, 0, 2, 1), (0, 3, 1, 2), (0, 1, 2, 3))
@@ -251,7 +254,8 @@
     out_ref[:rows, :] = (part + share).astype(BF16)
     if block == 0:
         mask = rest[0][...]
-        out_ref[rows:, :] = jnp.where(pl.program_id(0) == 0, mask.astype(F32), 0.0).astype(BF16)
+        out_ref[rows:, :] = jnp.zeros((mask.shape[0], out_ref.shape[1]), BF16)
+        out_ref[rows:, : mask.shape[1]] = mask
 
 
 def add_kernel(n, left_ref, right_ref, _, out_ref):
@@ -364,6 +368,11 @@
     pooled_ref[...] = fold(dot_nn(weight_ref[...], hidden))
 
 
+def sum_kernel(n, p0, p1, p2, p3, _, out_ref):
+    near = p0[...].astype(F32) + p1[...].astype(F32)
+    out_ref[...] = (near + (p2[...].astype(F32) + p3[...].astype(F32))).astype(BF16)
+
+
 def embed_kernel(n, p0, p1, p2, p3, down_ref, t_ref, token_ref, _, o0, o1, o2, o3, part_ref):
     pooled = p0[...] + p1[...] + p2[...] + p3[...]
     part = fold(dot_nn(stacked_halves(pooled), down_ref[...]))
@@ -374,13 +383,13 @@
     part_ref[...] = part + fold(dot_nn(stacked_halves(own), t_ref[0]))
     rows = o0.shape[0]
     for way, out in enumerate((o0, o1, o2, o3)):
-        out[...] = part_ref[pl.ds(pl.multiple_of(n[PEER + way] * rows, rows), rows), :]
+        out[...] = part_ref[pl.ds(pl.multiple_of(n[PEER + way] * rows, rows), rows), :].astype(out.dtype)
 
 
 def contrast_kernel(n, q0, q1, q2, q3, down_ref, _, loss_ref, grad_ref, hidden_grad_ref, all_ref):
     rows = q0.shape[0]
     for way, part in enumerate((q0, q1, q2, q3)):
-        all_ref[pl.ds(pl.multiple_of(n[PEER + way] * rows, rows), rows), :] = part[...]
+        all_ref[pl.ds(pl.multiple_of(n[PEER + way] * rows, rows), rows), :] = part[...].astype(F32)
     embedded = all_ref[...]
     count = embedded.shape[0]
     pairs = count // 2
@@ -496,9 +505,7 @@
             ),
             input_output_aliases=aliases,
             compiler_params=pltpu.CompilerParams(vmem_limit_bytes=VMEM_LIMIT),
-            cost_estimate=pl.CostEstimate(
-                flops=flops, bytes_accessed=sum(x.size * x.dtype.itemsize for x in args), transcendentals=0
-            ),
+            cost_estimate=pl.CostEstimate(flops=1, bytes_accessed=1, transcendentals=0),
         )(self.numbers, *args)
         self.last = result[0]
         return result
@@ -509,7 +516,7 @@
 
 
 def whole(array):
-    return array, fixed(array.shape)
+    return array, pl.BlockSpec(memory_space=pltpu.VMEM)
 
 
 def fast_body(context, o_weight, resid, norm_gain, router, gate_weight, up_weight, down_weight, expert_ids, lengths):
@@ -586,16 +593,15 @@
         at = (c * rows + offset) // size
         ins = [
             (context, pl.BlockSpec((size, heads), lambda j, n: (at, 0))),
-            (o_weight, pl.BlockSpec((heads, tile), lambda j, n: (0, j))),
-            (resid, pl.BlockSpec((rows, tile), lambda j, n: (0, j))),
+            whole(o_weight),
+            whole(resid),
         ]
         if c == 0:
             ins.append(whole(mask_wide))
         (parts[i],) = chain(
             functools.partial(project_kernel, c, offset),
             ins,
-            [(shape((tall, width), BF16), pl.BlockSpec((tall, tile), lambda j, n: (0, j)))],
-            steps=width // tile,
+            [(shape((tall, width), BF16), fixed((tall, width)))],
             flops=2 * size * heads * width,
         )
         from_leaf[i] = along_z(parts[i], LEAVES_IN)
@@ -641,12 +647,12 @@
         received[c] = [result[0]] + [swap_e(result[way], way) for way in (1, 2, 3)]
 
     def expert(c):
-        tile = 256
+        tile = hidden_width
         block = lambda size: pl.BlockSpec((1, slots, size), lambda j, n: (c, 0, j))
         outs = [(shape((sequences, hidden_width), F32), pl.BlockSpec((sequences, tile), lambda j, n: (0, j)))]
         outs += [(shape((4, slots, hidden_width), kind), block(tile)) for kind in (BF16, F32, F32)]
         outs.append((shape((4, slots, ROW_EXTRA), F32), pl.BlockSpec((1, slots, ROW_EXTRA), lambda j, n: (c, 0, 0))))
-        weight_spec = pl.BlockSpec((width, tile), lambda j, n: (0, j))
+        weight_spec = pl.BlockSpec(memory_space=pltpu.VMEM)
         result = chain(
             expert_kernel,
             [whole(r) for r in received[c]] + [(gate_w, weight_spec), (up_w, weight_spec)],
@@ -667,16 +673,20 @@
     hidden_all, a_all, b_all, info_all = (kept_acts[i] for i in (1, 2, 3, 4))
     own_rows = (total_all, pl.BlockSpec((1, rows, width), lambda j, n: (n[Z], 0, 0)))
     own_tokens = (token_info, pl.BlockSpec((8, rows), lambda j, n: (0, n[Z])))
-    seq_shape = shape((seq_count, width), F32)
+    seq_size = (seq_count, width)
     quarters = chain(
         embed_kernel,
         [whole(pool) for pool in pools] + [whole(down_w), own_rows, own_tokens],
-        [(seq_shape, fixed(seq_shape.shape))] * 4,
+        [(shape(seq_size, kind), fixed(seq_size)) for kind in (F32, BF16, BF16, BF16)],
         scratch=[pltpu.VMEM((sequences, width), F32)],
         flops=4 * sequences * hidden_width * width,
     )
-    mine = (quarters[0] + swap_e(quarters[1], 1)) + (swap_e(quarters[2], 2) + swap_e(quarters[3], 3))
-    mine = (mine + swap_z(mine, 1)) + (swap_z(mine, 2) + swap_z(mine, 3))
+
+    def add_four(values):
+        return chain(sum_kernel, [whole(v) for v in values], [(shape(seq_size, BF16), fixed(seq_size))])[0]
+
+    mine = add_four([quarters[0]] + [swap_e(quarters[way], way) for way in (1, 2, 3)])
+    mine = add_four([mine] + [swap_z(mine, way) for way in (1, 2, 3)])
     gathered = [mine] + [swap_e(mine, way) for way in (1, 2, 3)]
     sizes = ((1, 128), (sequences, width), (sequences, hidden_width))
     loss, dembedded, hidden_grad = chain(
@@ -689,8 +699,9 @@
     returned, sums = [None] * 4, [None] * 4
 
     def backward(k):
+        tile = width
         block = lambda size: pl.BlockSpec((1, slots, size), lambda j, n: (n[ORDER + k], 0, 0))
-        weight_spec = pl.BlockSpec((tile, hidden_width), lambda j, n: (j, 0))
+        weight_spec = pl.BlockSpec(memory_space=pltpu.VMEM)
         grads = chain(
             functools.partial(backward_kernel, capacity),
             [
@@ -723,24 +734,27 @@
             flops=2 * slots * rows * width,
         )
 
-    backward(0)
-    backward(1)
-    backward(2)
-    combine(0)
-    got1 = along_z(sums[0][1], LEAVES_IN)
-    backward(3)
-    combine(1)
-    got2 = along_z(sums[1][1], LEAVES_IN)
-    got3 = along_z(add(sums[0][0], got1), INNER_SWAP)
-    combine(2)
-    got4 = along_z(sums[2][1], LEAVES_IN)
-    combine(3)
-    got5 = along_z(add(sums[2][0], got2), INNER_SWAP)
-    got6 = along_z(add(sums[1][0], got3), LEAVES_OUT)
+    hops = {}
+
+    def combined(k):
+        combine(k)
+        if k < 3:
+            hops[k] = along_z(sums[k][1], LEAVES_IN)
+
+    def inner_hop(k):
+        total = add(sums[(0, 2)[k]][0], hops[(0, 1)[k]])
+        hops[3 + k] = along_z(total, INNER_SWAP)
+
+    def last_hop(_):
+        hops[5] = along_z(add(sums[1][0], hops[3]), LEAVES_OUT)
+
+    calls = {"b": backward, "c": combined, "i": inner_hop, "l": last_hop}
+    for step in BACKWARD_ORDER:
+        calls[step[0]](int(step[1:]))
     (grad,) = chain(
         finish_kernel,
         [own_rows, whole(gain), whole(dembedded), own_tokens]
-        + [whole(value) for value in (sums[3][0], got4, got5, got6)],
+        + [whole(value) for value in (sums[3][0], hops[2], hops[4], hops[5])],
         [(shape((rows, width), BF16), fixed((rows, width)))],
         flops=4 * rows * sequences * width,
     )

time: 231 us -> 209 us (0.905)
  Pallas kernels: 69.5 us -> 52.7 us
  starting transfers between devices: 82.2 us -> 65.4 us
  waiting for transfers between devices: 66.9 us -> 80.6 us
    pallas_call x37 -> x36, Pallas kernels: 69.5 us -> 52.7 us  [__call__(): pl.pallas_call(kernel, out_shape=list(shapes), grid_spec=pltpu.PrefetchSc...]
    ppermute x21 -> x18, starting transfers between devices: 56.1 us -> 39.5 us  [along_z(): return lax.ppermute(value, 'tensor', pairs)]
    ppermute x30, waiting for transfers between devices: 25.2 us -> 33.5 us  [swap_e(): return lax.ppermute(value, 'expert', [(i, i ^ bits) for i in range(4)])]
    ppermute x21 -> x18, waiting for transfers between devices: 37 us -> 43.7 us  [along_z(): return lax.ppermute(value, 'tensor', pairs)]
    unnamed x30 -> x26, local copies, waits for them, and re-layouts: 8.05 us -> 5.86 us
  transfers between devices with their start and end apart: 54 -> 51, of which waited for: 22 -> 27; matrix products, arithmetic and copies ran while one was open for 0% -> 0% of each run, Pallas kernels for 23% -> 18%
where the time goes in v3:
time: 209 us; the launch traced here: 208 us
  waiting for transfers between devices  80.6 us (39%)
  starting transfers between devices  65.4 us (31%)
  Pallas kernels  52.7 us (25%)
  local copies, waits for them, and re-layouts  6.74 us (3%)
    pallas_call x36, Pallas kernels, __call__(): pl.pallas_call(kernel, out_shape=list(shapes), grid_spec=pltpu.PrefetchSc...  52.7 us
    ppermute x18, waiting for transfers between devices, along_z(): return lax.ppermute(value, 'tensor', pairs)  43.7 us
    ppermute x18, starting transfers between devices, along_z(): return lax.ppermute(value, 'tensor', pairs)  39.5 us
    ppermute x30, waiting for transfers between devices, swap_e(): return lax.ppermute(value, 'expert', [(i, i ^ bits) for i in range(4)])  33.5 us
    ppermute x30, starting transfers between devices, swap_e(): return lax.ppermute(value, 'expert', [(i, i ^ bits) for i in range(4)])  20.9 us
    unnamed x26, local copies, waits for them, and re-layouts  5.86 us
    ppermute x3, starting transfers between devices, swap_z(): return lax.ppermute(value, 'tensor', [(i, i ^ bits) for i in range(4)])  5.01 us
  transfers between devices with their start and end apart: 51, of which 27 were waited for; matrix products, arithmetic and copies ran while one was open for 0% of the time, Pallas kernels for 18%

profile of v3, /device:TPU:0, one launch (start us, length us, event | category | flops | bytes accessed | tf_op | source)
XLA Modules:
  0.0 207.9 jit_solution(14672863119143977320)
XLA Ops:
  2.1 2.2 %copy-done.2 = bf16[1024,2048]{1,0:T(8,128)(2,1)S(1)} copy-done((bf16[1024,2048]{1,0:T(8,128)(2,1)S(1)}, bf16[1024,2048]{1,0:T(8,128)(2,1)}, u32[]{:S(2)}) %copy-start.2) | copy-done | bytes 4194328
  8.6 5.0 %collective-permute-start = (bf16[144,2048]{1,0:T(8,128)(2,1)S(1)}, bf16[144,2048]{1,0:T(8,128)(2,1)S(1)}, u32[]{:S(2)}, u32[]{:S(2)}) collective-permute-start(bf16[144,2048]{1,0:T(8,128)(2,1)S(1)} %shard_map.122.rest_0_.left_ref), channel_id=1, source_target_pairs={{0,1},{3,2},{4,5},{7,6},{8,9},{11,10},{12,13},{15,14},{16,17},{19,... | collective-permute-start | bytes 1769480 | tf_op jit(solution)/shard_map/ppermute | solution.py:550
  17.5 9.7 %collective-permute-done.right_ref = bf16[144,2048]{1,0:T(8,128)(2,1)S(1)} collective-permute-done((bf16[144,2048]{1,0:T(8,128)(2,1)S(1)}, bf16[144,2048]{1,0:T(8,128)(2,1)S(1)}, u32[]{:S(2)}, u32[]{:S(2)}) %collective-permute-start) | collective-permute-done | bytes 589856 | tf_op jit(solution)/shard_map/ppermute | solution.py:550
  28.6 8.0 %collective-permute-start.6 = (bf16[128,2048]{1,0:T(8,128)(2,1)S(1)}, bf16[128,2048]{1,0:T(8,128)(2,1)}, u32[]{:S(2)}, u32[]{:S(2)}) collective-permute-start(bf16[128,2048]{1,0:T(8,128)(2,1)S(1)} %shard_map.124._.left_ref), channel_id=1, source_target_pairs={{0,1},{3,2},{4,5},{7,6},{8,9},{11,10},{12,13},{15,14},{16,17},{19,... | collective-permute-start | bytes 1572872 | tf_op jit(solution)/shard_map/ppermute | solution.py:550
  40.6 6.4 %collective-permute-start.4 = (bf16[128,2048]{1,0:T(8,128)(2,1)S(1)}, bf16[128,2048]{1,0:T(8,128)(2,1)S(1)}, u32[]{:S(2)}, u32[]{:S(2)}) collective-permute-start(bf16[128,2048]{1,0:T(8,128)(2,1)S(1)} %shard_map.126._.left_ref), channel_id=1, source_target_pairs={{0,1},{3,2},{4,5},{7,6},{8,9},{11,10},{12,13},{15,14},{16,17},{19,... | collective-permute-start | bytes 1572872 | tf_op jit(solution)/shard_map/ppermute | solution.py:550
  55.2 4.6 %collective-permute-done.4.right_ref = bf16[128,2048]{1,0:T(8,128)(2,1)S(1)} collective-permute-done((bf16[128,2048]{1,0:T(8,128)(2,1)S(1)}, bf16[128,2048]{1,0:T(8,128)(2,1)S(1)}, u32[]{:S(2)}, u32[]{:S(2)}) %collective-permute-start.4) | collective-permute-done | bytes 524320 | tf_op jit(solution)/shard_map/ppermute | solution.py:550
  61.3 4.6 %collective-permute-done.3.refs_1_ = bf16[144,2048]{1,0:T(8,128)(2,1)S(1)} collective-permute-done((bf16[144,2048]{1,0:T(8,128)(2,1)S(1)}, bf16[144,2048]{1,0:T(8,128)(2,1)S(1)}, u32[]{:S(2)}, u32[]{:S(2)}) %collective-permute-start.3) | collective-permute-done | bytes 589856 | tf_op jit(solution)/shard_map/ppermute | solution.py:550
  69.3 7.7 %collective-permute-done.11.refs_1_ = bf16[128,2048]{1,0:T(8,128)(2,1)S(1)} collective-permute-done((bf16[128,2048]{1,0:T(8,128)(2,1)S(1)}, bf16[128,2048]{1,0:T(8,128)(2,1)S(1)}, u32[]{:S(2)}, u32[]{:S(2)}) %collective-permute-start.11) | collective-permute-done | bytes 524320 | tf_op jit(solution)/shard_map/ppermute | solution.py:550
  82.9 5.1 %collective-permute-done.8.r2 = bf16[40,2176]{1,0:T(8,128)(2,1)S(1)} collective-permute-done((bf16[40,2176]{1,0:T(8,128)(2,1)S(1)}, bf16[40,2176]{1,0:T(8,128)(2,1)S(1)}, u32[]{:S(2)}, u32[]{:S(2)}) %collective-permute-start.8) | collective-permute-done | bytes 174112 | tf_op jit(solution)/shard_map/ppermute | solution.py:556
  90.8 2.1 %collective-permute-start.15 = (bf16[40,2176]{1,0:T(8,128)(2,1)S(1)}, bf16[40,2176]{1,0:T(8,128)(2,1)S(1)}, u32[]{:S(2)}, u32[]{:S(2)}) collective-permute-start(bf16[40,2176]{1,0:T(8,128)(2,1)S(1)} %get-tuple-element.88), channel_id=1, source_target_pairs={{0,12},{4,8},{8,4},{12,0},{1,13},{5,9},{9,5},{13,1},{2,14},{6,10},... | collective-permute-start | bytes 522248 | tf_op jit(solution)/shard_map/ppermute | solution.py:556
  103.7 2.8 %collective-permute-done.19.r3 = bf16[40,2176]{1,0:T(8,128)(2,1)S(1)} collective-permute-done((bf16[40,2176]{1,0:T(8,128)(2,1)S(1)}, bf16[40,2176]{1,0:T(8,128)(2,1)S(1)}, u32[]{:S(2)}, u32[]{:S(2)}) %collective-permute-start.19) | collective-permute-done | bytes 174112 | tf_op jit(solution)/shard_map/ppermute | solution.py:556
  106.5 2.0 shard_map.140
  108.5 2.7 %collective-permute-done.22.r2 = bf16[40,2176]{1,0:T(8,128)(2,1)S(1)} collective-permute-done((bf16[40,2176]{1,0:T(8,128)(2,1)S(1)}, bf16[40,2176]{1,0:T(8,128)(2,1)S(1)}, u32[]{:S(2)}, u32[]{:S(2)}) %collective-permute-start.22) | collective-permute-done | bytes 174112 | tf_op jit(solution)/shard_map/ppermute | solution.py:556
  111.1 2.8 %collective-permute-done.23.r3 = bf16[40,2176]{1,0:T(8,128)(2,1)S(1)} collective-permute-done((bf16[40,2176]{1,0:T(8,128)(2,1)S(1)}, bf16[40,2176]{1,0:T(8,128)(2,1)S(1)}, u32[]{:S(2)}, u32[]{:S(2)}) %collective-permute-start.23) | collective-permute-done | bytes 174112 | tf_op jit(solution)/shard_map/ppermute | solution.py:556
  119.2 2.5 %collective-permute-done.25.p2 = bf16[8,2048]{1,0:T(8,128)(2,1)S(1)} collective-permute-done((bf16[8,2048]{1,0:T(8,128)(2,1)S(1)}, bf16[8,2048]{1,0:T(8,128)(2,1)S(1)}, u32[]{:S(2)}, u32[]{:S(2)}) %collective-permute-start.25) | collective-permute-done | bytes 32800 | tf_op jit(solution)/shard_map/ppermute | solution.py:556
  122.6 2.6 %collective-permute-start.27 = (bf16[8,2048]{1,0:T(8,128)(2,1)S(1)}, bf16[8,2048]{1,0:T(8,128)(2,1)S(1)}, u32[]{:S(2)}, u32[]{:S(2)}) collective-permute-start(bf16[8,2048]{1,0:T(8,128)(2,1)S(1)} %shard_map.143.p0._), channel_id=1, source_target_pairs={{0,1},{1,0},{2,3},{3,2},{4,5},{5,4},{6,7},{7,6},{8,9},{9,8},{10,11... | collective-permute-start | bytes 98312 | tf_op jit(solution)/shard_map/ppermute | solution.py:553
  125.2 2.4 %collective-permute-start.29 = (bf16[8,2048]{1,0:T(8,128)(2,1)S(1)}, bf16[8,2048]{1,0:T(8,128)(2,1)S(1)}, u32[]{:S(2)}, u32[]{:S(2)}) collective-permute-start(bf16[8,2048]{1,0:T(8,128)(2,1)S(1)} %shard_map.143.p0._), channel_id=1, source_target_pairs={{0,3},{1,2},{2,1},{3,0},{4,7},{5,6},{6,5},{7,4},{8,11},{9,10},{10,... | collective-permute-start | bytes 98312 | tf_op jit(solution)/shard_map/ppermute | solution.py:553
  127.6 2.8 %collective-permute-done.28.p2 = bf16[8,2048]{1,0:T(8,128)(2,1)S(1)} collective-permute-done((bf16[8,2048]{1,0:T(8,128)(2,1)S(1)}, bf16[8,2048]{1,0:T(8,128)(2,1)S(1)}, u32[]{:S(2)}, u32[]{:S(2)}) %collective-permute-start.28) | collective-permute-done | bytes 32800 | tf_op jit(solution)/shard_map/ppermute | solution.py:553
  133.6 2.1 collective-permute-done.31.q2
  136.1 3.3 %shard_map.145 = (f32[1,128]{1,0:T(1,128)}, f32[32,2048]{1,0:T(8,128)S(1)}, f32[32,768]{1,0:T(8,128)S(1)}) custom-call(s32[15]{0:T(128)S(1)} %concatenate.10.n, bf16[8,2048]{1,0:T(8,128)(2,1)S(1)} %shard_map.144.q0._, bf16[8,2048]{1,0:T(8,128)(2,1)S(1)} %collective-permute-done.30.q1, bf16[8,2048]{1,0:T(8,128)(2,1)S(1)} %collective-permute-done.31.q2, ...), custom_call_target="tpu_custom_call" | custom-call | flops 1 | bytes 1 | tf_op jit(solution)/shard_map/pallas_call | solution.py:496
  140.0 3.1 %shard_map.146 = (bf16[40,2048]{1,0:T(8,128)(2,1)S(1)}, bf16[40,2048]{1,0:T(8,128)(2,1)S(1)}, bf16[40,2048]{1,0:T(8,128)(2,1)S(1)}, bf16[40,2048]{1,0:T(8,128)(2,1)S(1)}) custom-call(s32[15]{0:T(128)S(1)} %concatenate.10.n, f32[4,160,768]{2,1,0:T(8,128)S(1)} %get-tuple-element.124.a_ref, f32[4,160,768]{2,1,0:T(8,128)S(1)} %get-tuple-element.125.b_ref, ...), custom_call_target="tpu_custom_call" | custom-call | flops 1 | bytes 1 | tf_op jit(solution)/shard_map/pallas_call | solution.py:496
  145.1 3.3 %shard_map.147 = (bf16[40,2048]{1,0:T(8,128)(2,1)S(1)}, bf16[40,2048]{1,0:T(8,128)(2,1)S(1)}, bf16[40,2048]{1,0:T(8,128)(2,1)S(1)}, bf16[40,2048]{1,0:T(8,128)(2,1)S(1)}) custom-call(s32[15]{0:T(128)S(1)} %concatenate.10.n, f32[4,160,768]{2,1,0:T(8,128)S(1)} %get-tuple-element.124.a_ref, f32[4,160,768]{2,1,0:T(8,128)S(1)} %get-tuple-element.125.b_ref, ...), custom_call_target="tpu_custom_call" | custom-call | flops 1 | bytes 1 | tf_op jit(solution)/shard_map/pallas_call | solution.py:496
  150.4 2.4 %collective-permute-done.38.r3 = bf16[40,2048]{1,0:T(8,128)(2,1)S(1)} collective-permute-done((bf16[40,2048]{1,0:T(8,128)(2,1)S(1)}, bf16[40,2048]{1,0:T(8,128)(2,1)S(1)}, u32[]{:S(2)}, u32[]{:S(2)}) %collective-permute-start.38) | collective-permute-done | bytes 163872 | tf_op jit(solution)/shard_map/ppermute | solution.py:556
  153.6 2.6 %collective-permute-start.42 = (bf16[128,2048]{1,0:T(8,128)(2,1)S(1)}, bf16[128,2048]{1,0:T(8,128)(2,1)S(1)}, u32[]{:S(2)}, u32[]{:S(2)}) collective-permute-start(bf16[128,2048]{1,0:T(8,128)(2,1)S(1)} %get-tuple-element.144), channel_id=1, source_target_pairs={{0,1},{3,2},{4,5},{7,6},{8,9},{11,10},{12,13},{15,14},{16,17},{19,... | collective-permute-start | bytes 1572872 | tf_op jit(solution)/shard_map/ppermute | solution.py:550
  158.2 3.1 %shard_map.149 = (bf16[40,2048]{1,0:T(8,128)(2,1)S(1)}, bf16[40,2048]{1,0:T(8,128)(2,1)S(1)}, bf16[40,2048]{1,0:T(8,128)(2,1)S(1)}, bf16[40,2048]{1,0:T(8,128)(2,1)S(1)}) custom-call(s32[15]{0:T(128)S(1)} %concatenate.10.n, f32[4,160,768]{2,1,0:T(8,128)S(1)} %get-tuple-element.124.a_ref, f32[4,160,768]{2,1,0:T(8,128)S(1)} %get-tuple-element.125.b_ref, ...), custom_call_target="tpu_custom_call" | custom-call | flops 1 | bytes 1 | tf_op jit(solution)/shard_map/pallas_call | solution.py:496
  163.5 2.4 %collective-permute-done.35.r3 = bf16[40,2048]{1,0:T(8,128)(2,1)S(1)} collective-permute-done((bf16[40,2048]{1,0:T(8,128)(2,1)S(1)}, bf16[40,2048]{1,0:T(8,128)(2,1)S(1)}, u32[]{:S(2)}, u32[]{:S(2)}) %collective-permute-start.35) | collective-permute-done | bytes 163872 | tf_op jit(solution)/shard_map/ppermute | solution.py:556
  166.7 3.1 %shard_map.151 = (bf16[40,2048]{1,0:T(8,128)(2,1)S(1)}, bf16[40,2048]{1,0:T(8,128)(2,1)S(1)}, bf16[40,2048]{1,0:T(8,128)(2,1)S(1)}, bf16[40,2048]{1,0:T(8,128)(2,1)S(1)}) custom-call(s32[15]{0:T(128)S(1)} %concatenate.10.n, f32[4,160,768]{2,1,0:T(8,128)S(1)} %get-tuple-element.124.a_ref, f32[4,160,768]{2,1,0:T(8,128)S(1)} %get-tuple-element.125.b_ref, ...), custom_call_target="tpu_custom_call" | custom-call | flops 1 | bytes 1 | tf_op jit(solution)/shard_map/pallas_call | solution.py:496
  177.0 3.2 %collective-permute-start.46 = (bf16[128,2048]{1,0:T(8,128)(2,1)S(1)}, bf16[128,2048]{1,0:T(8,128)(2,1)S(1)}, u32[]{:S(2)}, u32[]{:S(2)}) collective-permute-start(bf16[128,2048]{1,0:T(8,128)(2,1)S(1)} %get-tuple-element.150), channel_id=1, source_target_pairs={{0,1},{3,2},{4,5},{7,6},{8,9},{11,10},{12,13},{15,14},{16,17},{19,... | collective-permute-start | bytes 1572872 | tf_op jit(solution)/shard_map/ppermute | solution.py:550
  180.2 2.4 %collective-permute-done.40.r2 = bf16[40,2048]{1,0:T(8,128)(2,1)S(1)} collective-permute-done((bf16[40,2048]{1,0:T(8,128)(2,1)S(1)}, bf16[40,2048]{1,0:T(8,128)(2,1)S(1)}, u32[]{:S(2)}, u32[]{:S(2)}) %collective-permute-start.40) | collective-permute-done | bytes 163872 | tf_op jit(solution)/shard_map/ppermute | solution.py:556
  189.4 4.9 %collective-permute-done.46.r4 = bf16[128,2048]{1,0:T(8,128)(2,1)S(1)} collective-permute-done((bf16[128,2048]{1,0:T(8,128)(2,1)S(1)}, bf16[128,2048]{1,0:T(8,128)(2,1)S(1)}, u32[]{:S(2)}, u32[]{:S(2)}) %collective-permute-start.46) | collective-permute-done | bytes 524320 | tf_op jit(solution)/shard_map/ppermute | solution.py:550
  194.2 11.4 %collective-permute-done.50.r6 = bf16[128,2048]{1,0:T(8,128)(2,1)S(1)} collective-permute-done((bf16[128,2048]{1,0:T(8,128)(2,1)S(1)}, bf16[128,2048]{1,0:T(8,128)(2,1)S(1)}, u32[]{:S(2)}, u32[]{:S(2)}) %collective-permute-start.50) | collective-permute-done | bytes 524320 | tf_op jit(solution)/shard_map/ppermute | solution.py:550
  205.6 2.2 %shard_map.157 = bf16[128,2048]{1,0:T(8,128)(2,1)} custom-call(s32[15]{0:T(128)S(1)} %concatenate.10.n, bf16[4,128,2048]{2,1,0:T(8,128)(2,1)S(1)} %get-tuple-element.116.t_ref, f32[1,2048]{1,0:T(1,128)S(1)} %bitcast.45, f32[32,2048]{1,0:T(8,128)S(1)} %get-tuple-element.122.grad_ref, f32[8,512]{1,0:T(8,128)S(1)} %maximum_maximum_fusion.refs_4_.token_ref, ...), custom_call_target="tpu_custom_call" | custom-call | flops 1 | bytes 1 | tf_op jit(solution)/shard_map/pallas_call | solution.py:496
  (147 shorter events, 81.2 us)
Async XLA Ops:
  8.6 18.6 %collective-permute-start = (bf16[144,2048]{1,0:T(8,128)(2,1)S(1)}, bf16[144,2048]{1,0:T(8,128)(2,1)S(1)}, u32[]{:S(2)}, u32[]{:S(2)}) collective-permute-start(bf16[144,2048]{1,0:T(8,128)(2,1)S(1)} %shard_map.122.rest_0_.left_ref), channel_id=1, source_target_pairs={{0,1},{3,2},{4,5},{7,6},{8,9},{11,10},{12,13},{15,14},{16,17},{19,... | collective-permute-start | bytes 1769480 | tf_op jit(solution)/shard_map/ppermute | solution.py:550
  14.9 23.6 %collective-permute-start.2 = (bf16[128,2048]{1,0:T(8,128)(2,1)S(1)}, bf16[128,2048]{1,0:T(8,128)(2,1)S(1)}, u32[]{:S(2)}, u32[]{:S(2)}) collective-permute-start(bf16[128,2048]{1,0:T(8,128)(2,1)S(1)} %shard_map.123.rest_0_.left_ref), channel_id=1, source_target_pairs={{0,1},{3,2},{4,5},{7,6},{8,9},{11,10},{12,13},{15,14},{16,17},{19,... | collective-permute-start | bytes 1572872 | tf_op jit(solution)/shard_map/ppermute | solution.py:550
  27.9 19.4 %collective-permute-start.1 = (bf16[144,2048]{1,0:T(8,128)(2,1)S(1)}, bf16[144,2048]{1,0:T(8,128)(2,1)S(1)}, u32[]{:S(2)}, u32[]{:S(2)}) collective-permute-start(bf16[144,2048]{1,0:T(8,128)(2,1)S(1)} %shard_map.125.rest_0_.left_ref), channel_id=1, source_target_pairs={{1,2},{2,1},{5,6},{6,5},{9,10},{10,9},{13,14},{14,13},{17,18},{18,... | collective-permute-start | bytes 1769480 | tf_op jit(solution)/shard_map/ppermute | solution.py:550
  28.6 21.1 %collective-permute-start.6 = (bf16[128,2048]{1,0:T(8,128)(2,1)S(1)}, bf16[128,2048]{1,0:T(8,128)(2,1)}, u32[]{:S(2)}, u32[]{:S(2)}) collective-permute-start(bf16[128,2048]{1,0:T(8,128)(2,1)S(1)} %shard_map.124._.left_ref), channel_id=1, source_target_pairs={{0,1},{3,2},{4,5},{7,6},{8,9},{11,10},{12,13},{15,14},{16,17},{19,... | collective-permute-start | bytes 1572872 | tf_op jit(solution)/shard_map/ppermute | solution.py:550
  39.1 13.1 %collective-permute-start.5 = (bf16[128,2048]{1,0:T(8,128)(2,1)S(1)}, bf16[128,2048]{1,0:T(8,128)(2,1)}, u32[]{:S(2)}, u32[]{:S(2)}) collective-permute-start(bf16[128,2048]{1,0:T(8,128)(2,1)S(1)} %shard_map.127._.left_ref), channel_id=1, source_target_pairs={{1,2},{2,1},{5,6},{6,5},{9,10},{10,9},{13,14},{14,13},{17,18},{18,... | collective-permute-start | bytes 1572872 | tf_op jit(solution)/shard_map/ppermute | solution.py:550
  40.6 19.2 %collective-permute-start.4 = (bf16[128,2048]{1,0:T(8,128)(2,1)S(1)}, bf16[128,2048]{1,0:T(8,128)(2,1)S(1)}, u32[]{:S(2)}, u32[]{:S(2)}) collective-permute-start(bf16[128,2048]{1,0:T(8,128)(2,1)S(1)} %shard_map.126._.left_ref), channel_id=1, source_target_pairs={{0,1},{3,2},{4,5},{7,6},{8,9},{11,10},{12,13},{15,14},{16,17},{19,... | collective-permute-start | bytes 1572872 | tf_op jit(solution)/shard_map/ppermute | solution.py:550
  48.0 17.8 %collective-permute-start.3 = (bf16[144,2048]{1,0:T(8,128)(2,1)S(1)}, bf16[144,2048]{1,0:T(8,128)(2,1)S(1)}, u32[]{:S(2)}, u32[]{:S(2)}) collective-permute-start(bf16[144,2048]{1,0:T(8,128)(2,1)S(1)} %shard_map.128._.refs_0_), channel_id=1, source_target_pairs={{1,0},{2,3},{5,4},{6,7},{9,8},{10,11},{13,12},{14,15},{17,16},{18,... | collective-permute-start | bytes 1769480 | tf_op jit(solution)/shard_map/ppermute | solution.py:550
  51.4 15.8 %collective-permute-start.12 = (bf16[128,2048]{1,0:T(8,128)(2,1)S(1)}, bf16[128,2048]{1,0:T(8,128)(2,1)S(1)}, u32[]{:S(2)}, u32[]{:S(2)}) collective-permute-start(bf16[128,2048]{1,0:T(8,128)(2,1)S(1)} %shard_map.129._.left_ref), channel_id=1, source_target_pairs={{1,2},{2,1},{5,6},{6,5},{9,10},{10,9},{13,14},{14,13},{17,18},{18,... | collective-permute-start | bytes 1572872 | tf_op jit(solution)/shard_map/ppermute | solution.py:550
  53.9 23.1 %collective-permute-start.11 = (bf16[128,2048]{1,0:T(8,128)(2,1)S(1)}, bf16[128,2048]{1,0:T(8,128)(2,1)S(1)}, u32[]{:S(2)}, u32[]{:S(2)}) collective-permute-start(bf16[128,2048]{1,0:T(8,128)(2,1)S(1)} %shard_map.130._.refs_0_), channel_id=1, source_target_pairs={{1,0},{2,3},{5,4},{6,7},{9,8},{10,11},{13,12},{14,15},{17,16},{18,... | collective-permute-start | bytes 1572872 | tf_op jit(solution)/shard_map/ppermute | solution.py:550
  60.5 18.0 %collective-permute-start.10 = (bf16[128,2048]{1,0:T(8,128)(2,1)S(1)}, bf16[128,2048]{1,0:T(8,128)(2,1)S(1)}, u32[]{:S(2)}, u32[]{:S(2)}) collective-permute-start(bf16[128,2048]{1,0:T(8,128)(2,1)S(1)} %shard_map.131.refs_5_.left_ref), channel_id=1, source_target_pairs={{1,2},{2,1},{5,6},{6,5},{9,10},{10,9},{13,14},{14,13},{17,18},{18,... | collective-permute-start | bytes 1572872 | tf_op jit(solution)/shard_map/ppermute | solution.py:550
  67.9 27.0 %collective-permute-start.16 = (bf16[128,2048]{1,0:T(8,128)(2,1)S(1)}, bf16[128,2048]{1,0:T(8,128)(2,1)S(1)}, u32[]{:S(2)}, u32[]{:S(2)}) collective-permute-start(bf16[128,2048]{1,0:T(8,128)(2,1)S(1)} %shard_map.133.refs_8_.refs_0_), channel_id=1, source_target_pairs={{1,0},{2,3},{5,4},{6,7},{9,8},{10,11},{13,12},{14,15},{17,16},{18,... | collective-permute-start | bytes 1572872 | tf_op jit(solution)/shard_map/ppermute | solution.py:550
  79.1 21.1 %collective-permute-start.20 = (bf16[128,2048]{1,0:T(8,128)(2,1)S(1)}, bf16[128,2048]{1,0:T(8,128)(2,1)S(1)}, u32[]{:S(2)}, u32[]{:S(2)}) collective-permute-start(bf16[128,2048]{1,0:T(8,128)(2,1)S(1)} %shard_map.135.refs_0_), channel_id=1, source_target_pairs={{1,0},{2,3},{5,4},{6,7},{9,8},{10,11},{13,12},{14,15},{17,16},{18,... | collective-permute-start | bytes 1572872 | tf_op jit(solution)/shard_map/ppermute | solution.py:550
  82.2 8.6 %collective-permute-start.9 = (bf16[40,2176]{1,0:T(8,128)(2,1)S(1)}, bf16[40,2176]{1,0:T(8,128)(2,1)S(1)}, u32[]{:S(2)}, u32[]{:S(2)}) collective-permute-start(bf16[40,2176]{1,0:T(8,128)(2,1)S(1)} %get-tuple-element.80), channel_id=1, source_target_pairs={{0,12},{4,8},{8,4},{12,0},{1,13},{5,9},{9,5},{13,1},{2,14},{6,10},... | collective-permute-start | bytes 522248 | tf_op jit(solution)/shard_map/ppermute | solution.py:556
  82.5 13.8 %collective-permute-start.13 = (bf16[40,2176]{1,0:T(8,128)(2,1)S(1)}, bf16[40,2176]{1,0:T(8,128)(2,1)S(1)}, u32[]{:S(2)}, u32[]{:S(2)}) collective-permute-start(bf16[40,2176]{1,0:T(8,128)(2,1)S(1)} %get-tuple-element.86), channel_id=1, source_target_pairs={{0,4},{4,0},{8,12},{12,8},{1,5},{5,1},{9,13},{13,9},{2,6},{6,2},{1... | collective-permute-start | bytes 522248 | tf_op jit(solution)/shard_map/ppermute | solution.py:556
  88.0 9.0 %collective-permute-start.14 = (bf16[40,2176]{1,0:T(8,128)(2,1)S(1)}, bf16[40,2176]{1,0:T(8,128)(2,1)S(1)}, u32[]{:S(2)}, u32[]{:S(2)}) collective-permute-start(bf16[40,2176]{1,0:T(8,128)(2,1)S(1)} %get-tuple-element.87), channel_id=1, source_target_pairs={{0,8},{4,12},{8,0},{12,4},{1,9},{5,13},{9,1},{13,5},{2,10},{6,14},... | collective-permute-start | bytes 522248 | tf_op jit(solution)/shard_map/ppermute | solution.py:556
  90.8 7.5 %collective-permute-start.15 = (bf16[40,2176]{1,0:T(8,128)(2,1)S(1)}, bf16[40,2176]{1,0:T(8,128)(2,1)S(1)}, u32[]{:S(2)}, u32[]{:S(2)}) collective-permute-start(bf16[40,2176]{1,0:T(8,128)(2,1)S(1)} %get-tuple-element.88), channel_id=1, source_target_pairs={{0,12},{4,8},{8,4},{12,0},{1,13},{5,9},{9,5},{13,1},{2,14},{6,10},... | collective-permute-start | bytes 522248 | tf_op jit(solution)/shard_map/ppermute | solution.py:556
  96.4 7.3 %collective-permute-start.18 = (bf16[40,2176]{1,0:T(8,128)(2,1)S(1)}, bf16[40,2176]{1,0:T(8,128)(2,1)S(1)}, u32[]{:S(2)}, u32[]{:S(2)}) collective-permute-start(bf16[40,2176]{1,0:T(8,128)(2,1)S(1)} %get-tuple-element.98), channel_id=1, source_target_pairs={{0,8},{4,12},{8,0},{12,4},{1,9},{5,13},{9,1},{13,5},{2,10},{6,14},... | collective-permute-start | bytes 522248 | tf_op jit(solution)/shard_map/ppermute | solution.py:556
  97.0 9.5 %collective-permute-start.19 = (bf16[40,2176]{1,0:T(8,128)(2,1)S(1)}, bf16[40,2176]{1,0:T(8,128)(2,1)S(1)}, u32[]{:S(2)}, u32[]{:S(2)}) collective-permute-start(bf16[40,2176]{1,0:T(8,128)(2,1)S(1)} %get-tuple-element.99), channel_id=1, source_target_pairs={{0,12},{4,8},{8,4},{12,0},{1,13},{5,9},{9,5},{13,1},{2,14},{6,10},... | collective-permute-start | bytes 522248 | tf_op jit(solution)/shard_map/ppermute | solution.py:556
  102.0 9.1 %collective-permute-start.22 = (bf16[40,2176]{1,0:T(8,128)(2,1)S(1)}, bf16[40,2176]{1,0:T(8,128)(2,1)S(1)}, u32[]{:S(2)}, u32[]{:S(2)}) collective-permute-start(bf16[40,2176]{1,0:T(8,128)(2,1)S(1)} %get-tuple-element.109), channel_id=1, source_target_pairs={{0,8},{4,12},{8,0},{12,4},{1,9},{5,13},{9,1},{13,5},{2,10},{6,14},... | collective-permute-start | bytes 522248 | tf_op jit(solution)/shard_map/ppermute | solution.py:556
  103.6 10.4 %collective-permute-start.23 = (bf16[40,2176]{1,0:T(8,128)(2,1)S(1)}, bf16[40,2176]{1,0:T(8,128)(2,1)S(1)}, u32[]{:S(2)}, u32[]{:S(2)}) collective-permute-start(bf16[40,2176]{1,0:T(8,128)(2,1)S(1)} %get-tuple-element.110), channel_id=1, source_target_pairs={{0,12},{4,8},{8,4},{12,0},{1,13},{5,9},{9,5},{13,1},{2,14},{6,10},... | collective-permute-start | bytes 522248 | tf_op jit(solution)/shard_map/ppermute | solution.py:556
  144.4 8.4 %collective-permute-start.38 = (bf16[40,2048]{1,0:T(8,128)(2,1)S(1)}, bf16[40,2048]{1,0:T(8,128)(2,1)S(1)}, u32[]{:S(2)}, u32[]{:S(2)}) collective-permute-start(bf16[40,2048]{1,0:T(8,128)(2,1)S(1)} %get-tuple-element.136), channel_id=1, source_target_pairs={{0,12},{4,8},{8,4},{12,0},{1,13},{5,9},{9,5},{13,1},{2,14},{6,10},... | collective-permute-start | bytes 491528 | tf_op jit(solution)/shard_map/ppermute | solution.py:556
  153.6 20.1 %collective-permute-start.42 = (bf16[128,2048]{1,0:T(8,128)(2,1)S(1)}, bf16[128,2048]{1,0:T(8,128)(2,1)S(1)}, u32[]{:S(2)}, u32[]{:S(2)}) collective-permute-start(bf16[128,2048]{1,0:T(8,128)(2,1)S(1)} %get-tuple-element.144), channel_id=1, source_target_pairs={{0,1},{3,2},{4,5},{7,6},{8,9},{11,10},{12,13},{15,14},{16,17},{19,... | collective-permute-start | bytes 1572872 | tf_op jit(solution)/shard_map/ppermute | solution.py:550
  157.4 8.4 %collective-permute-start.35 = (bf16[40,2048]{1,0:T(8,128)(2,1)S(1)}, bf16[40,2048]{1,0:T(8,128)(2,1)S(1)}, u32[]{:S(2)}, u32[]{:S(2)}) collective-permute-start(bf16[40,2048]{1,0:T(8,128)(2,1)S(1)} %get-tuple-element.133), channel_id=1, source_target_pairs={{0,12},{4,8},{8,4},{12,0},{1,13},{5,9},{9,5},{13,1},{2,14},{6,10},... | collective-permute-start | bytes 491528 | tf_op jit(solution)/shard_map/ppermute | solution.py:556
  161.3 9.9 %collective-permute-start.43 = (bf16[40,2048]{1,0:T(8,128)(2,1)S(1)}, bf16[40,2048]{1,0:T(8,128)(2,1)S(1)}, u32[]{:S(2)}, u32[]{:S(2)}) collective-permute-start(bf16[40,2048]{1,0:T(8,128)(2,1)S(1)} %get-tuple-element.145), channel_id=1, source_target_pairs={{0,4},{4,0},{8,12},{12,8},{1,5},{5,1},{9,13},{13,9},{2,6},{6,2},{1... | collective-permute-start | bytes 491528 | tf_op jit(solution)/shard_map/ppermute | solution.py:556
  161.8 9.4 %collective-permute-start.44 = (bf16[40,2048]{1,0:T(8,128)(2,1)S(1)}, bf16[40,2048]{1,0:T(8,128)(2,1)S(1)}, u32[]{:S(2)}, u32[]{:S(2)}) collective-permute-start(bf16[40,2048]{1,0:T(8,128)(2,1)S(1)} %get-tuple-element.146), channel_id=1, source_target_pairs={{0,8},{4,12},{8,0},{12,4},{1,9},{5,13},{9,1},{13,5},{2,10},{6,14},... | collective-permute-start | bytes 491528 | tf_op jit(solution)/shard_map/ppermute | solution.py:556
  163.5 9.4 %collective-permute-start.45 = (bf16[40,2048]{1,0:T(8,128)(2,1)S(1)}, bf16[40,2048]{1,0:T(8,128)(2,1)S(1)}, u32[]{:S(2)}, u32[]{:S(2)}) collective-permute-start(bf16[40,2048]{1,0:T(8,128)(2,1)S(1)} %get-tuple-element.147), channel_id=1, source_target_pairs={{0,12},{4,8},{8,4},{12,0},{1,13},{5,9},{9,5},{13,1},{2,14},{6,10},... | collective-permute-start | bytes 491528 | tf_op jit(solution)/shard_map/ppermute | solution.py:556
  169.9 16.2 %collective-permute-start.47 = (bf16[128,2048]{1,0:T(8,128)(2,1)S(1)}, bf16[128,2048]{1,0:T(8,128)(2,1)S(1)}, u32[]{:S(2)}, u32[]{:S(2)}) collective-permute-start(bf16[128,2048]{1,0:T(8,128)(2,1)S(1)} %get-tuple-element.151), channel_id=1, source_target_pairs={{0,1},{3,2},{4,5},{7,6},{8,9},{11,10},{12,13},{15,14},{16,17},{19,... | collective-permute-start | bytes 1572872 | tf_op jit(solution)/shard_map/ppermute | solution.py:550
  174.4 13.0 %collective-permute-start.49 = (bf16[128,2048]{1,0:T(8,128)(2,1)S(1)}, bf16[128,2048]{1,0:T(8,128)(2,1)S(1)}, u32[]{:S(2)}, u32[]{:S(2)}) collective-permute-start(bf16[128,2048]{1,0:T(8,128)(2,1)S(1)} %shard_map.153._), channel_id=1, source_target_pairs={{1,2},{2,1},{5,6},{6,5},{9,10},{10,9},{13,14},{14,13},{17,18},{18,... | collective-permute-start | bytes 1572872 | tf_op jit(solution)/shard_map/ppermute | solution.py:550
  176.6 7.9 %collective-permute-start.41 = (bf16[40,2048]{1,0:T(8,128)(2,1)S(1)}, bf16[40,2048]{1,0:T(8,128)(2,1)S(1)}, u32[]{:S(2)}, u32[]{:S(2)}) collective-permute-start(bf16[40,2048]{1,0:T(8,128)(2,1)S(1)} %get-tuple-element.143), channel_id=1, source_target_pairs={{0,12},{4,8},{8,4},{12,0},{1,13},{5,9},{9,5},{13,1},{2,14},{6,10},... | collective-permute-start | bytes 491528 | tf_op jit(solution)/shard_map/ppermute | solution.py:556
  177.0 17.2 %collective-permute-start.46 = (bf16[128,2048]{1,0:T(8,128)(2,1)S(1)}, bf16[128,2048]{1,0:T(8,128)(2,1)S(1)}, u32[]{:S(2)}, u32[]{:S(2)}) collective-permute-start(bf16[128,2048]{1,0:T(8,128)(2,1)S(1)} %get-tuple-element.150), channel_id=1, source_target_pairs={{0,1},{3,2},{4,5},{7,6},{8,9},{11,10},{12,13},{15,14},{16,17},{19,... | collective-permute-start | bytes 1572872 | tf_op jit(solution)/shard_map/ppermute | solution.py:550
  186.7 7.5 %collective-permute-start.48 = (bf16[128,2048]{1,0:T(8,128)(2,1)S(1)}, bf16[128,2048]{1,0:T(8,128)(2,1)S(1)}, u32[]{:S(2)}, u32[]{:S(2)}) collective-permute-start(bf16[128,2048]{1,0:T(8,128)(2,1)S(1)} %shard_map.155._), channel_id=1, source_target_pairs={{1,2},{2,1},{5,6},{6,5},{9,10},{10,9},{13,14},{14,13},{17,18},{18,... | collective-permute-start | bytes 1572872 | tf_op jit(solution)/shard_map/ppermute | solution.py:550
  188.1 17.6 %collective-permute-start.50 = (bf16[128,2048]{1,0:T(8,128)(2,1)S(1)}, bf16[128,2048]{1,0:T(8,128)(2,1)S(1)}, u32[]{:S(2)}, u32[]{:S(2)}) collective-permute-start(bf16[128,2048]{1,0:T(8,128)(2,1)S(1)} %shard_map.156._), channel_id=1, source_target_pairs={{1,0},{2,3},{5,4},{6,7},{9,8},{10,11},{13,12},{14,15},{17,16},{18,... | collective-permute-start | bytes 1572872 | tf_op jit(solution)/shard_map/ppermute | solution.py:550
  (32 other events, 217.6 us)

commit v4 on v3

--- a/solution.py
+++ b/solution.py
@@ -211,12 +211,14 @@
 LEAVES_OUT = ((1, 0), (2, 3))
 PIECES = (1, 1, 1, 1)
 FORWARD_ORDER = (
-    "p0", "p1", "p2", "s0", "p3", "s1", "t0", "s2", "t1", "s3", "d0", "t2", "d1", "t3", "x0", "d2", "x1", "d3", "x2", "x3",
+    "p0", "p1", "p2", "p3", "s0", "s1", "t0", "s2", "t1", "s3", "d0", "t2", "d1", "x0", "t3", "d2", "x1", "d3", "x2", "x3",
 )
 BACKWARD_ORDER = (
     "b0", "b1", "c0", "b2", "c1", "b3", "c2", "i0", "c3", "i1", "l0",
 )
 VMEM_LIMIT = 24 * 2**20
+FIRST_LIMIT = 54 * 2**20
+FIRST_CUTS = 8
 BLOCK_ORDER = ((3, 2, 1, 0), (3, 0, 2, 1), (0, 3, 1, 2), (0, 1, 2, 3))
 OWN_EXPERT, LEAF, Z, PEER, PEER_EXPERT, ORDER = 0, 1, 2, 3, 7, 11
 BF16 = jnp.bfloat16
@@ -252,10 +254,39 @@
     part = dot_nn(context_ref[...], weight_ref[...])
     share = jnp.where(n[Z] == block, resid_ref[offset : offset + rows, :].astype(F32), 0.0)
     out_ref[:rows, :] = (part + share).astype(BF16)
-    if block == 0:
-        mask = rest[0][...]
-        out_ref[rows:, :] = jnp.zeros((mask.shape[0], out_ref.shape[1]), BF16)
-        out_ref[rows:, : mask.shape[1]] = mask
+
+
+def first_kernel(experts, ids_ref, context_hbm, weight_hbm, resid_hbm, out_ref, context_ref, weight_ref, resid_ref, sems):
+    rows, heads = context_ref.shape
+    cuts = sems.shape[0] - 2
+    step = heads // cuts
+    copies = []
+    for i in range(cuts):
+        at = pl.ds(i * step, step)
+        copies.append(pltpu.make_async_copy(weight_hbm.at[at], weight_ref.at[at], sems.at[i]))
+    context_copy = pltpu.make_async_copy(context_hbm.at[pl.ds(0, rows)], context_ref, sems.at[cuts])
+    resid_copy = pltpu.make_async_copy(resid_hbm.at[pl.ds(0, rows)], resid_ref, sems.at[cuts + 1])
+    context_copy.start()
+    for copy in copies:
+        copy.start()
+    resid_copy.start()
+    z = lax.axis_index("tensor")
+    mask = jnp.zeros((experts, rows), F32)
+    for k in range(ids_ref.shape[0]):
+        mask += (ids_ref[k : k + 1, :] == iota((experts, rows), 0)).astype(F32)
+    out_ref[rows:, :] = jnp.zeros((experts, out_ref.shape[1]), BF16)
+    for block in range(4):
+        out_ref[rows:, block * rows : (block + 1) * rows] = jnp.where(z == block, mask, 0.0).astype(BF16)
+    context_copy.wait()
+    part = None
+    for i, copy in enumerate(copies):
+        copy.wait()
+        at = slice(i * step, (i + 1) * step)
+        term = dot_nn(context_ref[:, at], weight_ref[at, :])
+        part = term if part is None else part + term
+    resid_copy.wait()
+    share = jnp.where(z == 0, resid_ref[...].astype(F32), 0.0)
+    out_ref[:rows, :] = (part + share).astype(BF16)
 
 
 def add_kernel(n, left_ref, right_ref, _, out_ref):
@@ -386,7 +417,7 @@
         out[...] = part_ref[pl.ds(pl.multiple_of(n[PEER + way] * rows, rows), rows), :].astype(out.dtype)
 
 
-def contrast_kernel(n, q0, q1, q2, q3, down_ref, _, loss_ref, grad_ref, hidden_grad_ref, all_ref):
+def contrast_kernel(n, q0, q1, q2, q3, down_ref, _, grad_ref, hidden_grad_ref, loss_ref, all_ref):
     rows = q0.shape[0]
     for way, part in enumerate((q0, q1, q2, q3)):
         all_ref[pl.ds(pl.multiple_of(n[PEER + way] * rows, rows), rows), :] = part[...].astype(F32)
@@ -410,7 +441,7 @@
     row_total = jnp.where(is_query, row_total, 1.0)
     own_score = jnp.sum(jnp.where(matched, scores, 0.0), axis=1, keepdims=True)
     terms = jnp.where(is_query, jnp.log(row_total) - own_score, 0.0)
-    loss_ref[...] = jnp.broadcast_to(jnp.sum(terms, axis=0, keepdims=True) / pairs, loss_ref.shape)
+    loss_ref[0] = jnp.sum(terms) / pairs
     dscore = (exp_scores / row_total - jnp.where(matched, 1.0, 0.0)) * (LOSS_SCALE / pairs)
     both = dscore + jnp.transpose(dscore)
     dunit = (
@@ -460,21 +491,24 @@
     narrow_ref[...] = total.astype(BF16)
 
 
-def finish_kernel(n, t_ref, gain_ref, grad_ref, token_ref, own_ref, r4, r5, r6, _, out_ref):
+def spread_kernel(n, t_ref, grad_ref, token_ref, _, out_ref, scale_ref):
     x = t_ref[0].astype(F32)
     scale = lax.rsqrt(jnp.mean(x * x, axis=1, keepdims=True) + EPSILON)
-    sequences = grad_ref.shape[0]
-    spread = jnp.where(
-        iota((sequences, x.shape[0]), 0).astype(F32) == token_ref[0:1, :], 1.0, 0.0
-    )
+    spread = jnp.where(iota((grad_ref.shape[0], x.shape[0]), 0).astype(F32) == token_ref[0:1, :], 1.0, 0.0)
     spread = jnp.transpose(spread).astype(BF16)
     inverse = jnp.transpose(token_ref[...])[:, 1:2]
     high, low = halves(grad_ref[...])
-    dresid = inverse * (dot_nn(spread, high) + dot_nn(spread, low))
+    out_ref[...] = inverse * (dot_nn(spread, high) + dot_nn(spread, low))
+    scale_ref[...] = jnp.broadcast_to(scale, scale_ref.shape)
+
+
+def finish_kernel(n, t_ref, gain_ref, dresid_ref, scale_ref, own_ref, r4, r5, r6, _, out_ref):
+    x = t_ref[0].astype(F32)
+    scale = scale_ref[:, :1]
     dnormed = own_ref[...] + r4[...].astype(F32) + r5[...].astype(F32) + r6[...].astype(F32)
     gained = dnormed * gain_ref[...]
-    out = dresid + scale * gained - x * (scale * scale * scale) * jnp.mean(gained * x, axis=1, keepdims=True)
-    out_ref[...] = out.astype(BF16)
+    pull = (scale * scale * scale) * jnp.mean(gained * x, axis=1, keepdims=True)
+    out_ref[...] = (dresid_ref[...] + scale * gained - x * pull).astype(BF16)
 
 
 class Chain:
@@ -555,11 +589,6 @@
     def swap_e(value, bits):
         return lax.ppermute(value, "expert", [(i, i ^ bits) for i in range(4)])
 
-    mask_own = jnp.sum(
-        (expert_ids[None, :, :] == jnp.arange(experts, dtype=jnp.int32)[:, None, None]).astype(F32), axis=2
-    )
-    mask_wide = jnp.concatenate([jnp.where(z == c, mask_own, 0.0) for c in range(4)], axis=1).astype(BF16)
-
     seq_lengths = lengths[0]
     seq_ends = jnp.cumsum(seq_lengths)
     places = jnp.arange(4 * rows, dtype=jnp.int32)
@@ -589,19 +618,34 @@
 
     def first_hop(i):
         c, offset, size = pieces[i]
-        tall = size + (experts if c == 0 else 0)
+        if i == 0:
+            away = pl.BlockSpec(memory_space=pl.ANY)
+            near = pl.BlockSpec(memory_space=pltpu.VMEM)
+            chain.last = parts[0] = pl.pallas_call(
+                functools.partial(first_kernel, experts),
+                out_shape=shape((size + experts, width), BF16),
+                in_specs=[near, away, away, away],
+                out_specs=near,
+                scratch_shapes=[
+                    pltpu.VMEM((size, heads), BF16),
+                    pltpu.VMEM((heads, width), BF16),
+                    pltpu.VMEM((size, width), BF16),
+                    pltpu.SemaphoreType.DMA((FIRST_CUTS + 2,)),
+                ],
+                compiler_params=pltpu.CompilerParams(vmem_limit_bytes=FIRST_LIMIT),
+            )(expert_ids.T, context, o_weight, resid)
+            from_leaf[0] = along_z(parts[0], LEAVES_IN)
+            return
         at = (c * rows + offset) // size
         ins = [
             (context, pl.BlockSpec((size, heads), lambda j, n: (at, 0))),
             whole(o_weight),
             whole(resid),
         ]
-        if c == 0:
-            ins.append(whole(mask_wide))
         (parts[i],) = chain(
             functools.partial(project_kernel, c, offset),
             ins,
-            [(shape((tall, width), BF16), fixed((tall, width)))],
+            [(shape((size, width), BF16), fixed((size, width)))],
             flops=2 * size * heads * width,
         )
         from_leaf[i] = along_z(parts[i], LEAVES_IN)
@@ -688,11 +732,12 @@
     mine = add_four([quarters[0]] + [swap_e(quarters[way], way) for way in (1, 2, 3)])
     mine = add_four([mine] + [swap_z(mine, way) for way in (1, 2, 3)])
     gathered = [mine] + [swap_e(mine, way) for way in (1, 2, 3)]
-    sizes = ((1, 128), (sequences, width), (sequences, hidden_width))
-    loss, dembedded, hidden_grad = chain(
+    sizes = ((sequences, width), (sequences, hidden_width))
+    dembedded, hidden_grad, loss = chain(
         contrast_kernel,
         [whole(piece) for piece in gathered] + [whole(down_w)],
-        [(shape(size, F32), fixed(size)) for size in sizes],
+        [(shape(size, F32), fixed(size)) for size in sizes]
+        + [(shape((1,), F32), pl.BlockSpec(memory_space=pltpu.SMEM))],
         scratch=[pltpu.VMEM((sequences, width), F32)],
         flops=4 * sequences * hidden_width * width,
     )
@@ -751,14 +796,19 @@
     calls = {"b": backward, "c": combined, "i": inner_hop, "l": last_hop}
     for step in BACKWARD_ORDER:
         calls[step[0]](int(step[1:]))
+    dresid, scales = chain(
+        spread_kernel,
+        [own_rows, whole(dembedded), own_tokens],
+        [(shape((rows, width), F32), fixed((rows, width))), (shape((rows, 128), F32), fixed((rows, 128)))],
+    )
     (grad,) = chain(
         finish_kernel,
-        [own_rows, whole(gain), whole(dembedded), own_tokens]
+        [own_rows, whole(gain), whole(dresid), whole(scales)]
         + [whole(value) for value in (sums[3][0], hops[2], hops[4], hops[5])],
         [(shape((rows, width), BF16), fixed((rows, width)))],
         flops=4 * rows * sequences * width,
     )
-    return loss[0, :1], grad
+    return loss, grad
 
 
 def solution(mesh):

time: 209 us -> 200 us (0.957)
  waiting for transfers between devices: 80.6 us -> 73.2 us
  Pallas kernels: 52.7 us -> 57.5 us
  starting transfers between devices: 65.4 us -> 62.5 us
  local copies, waits for them, and re-layouts: 6.74 us -> 4.19 us
    ppermute x30, waiting for transfers between devices: 33.5 us -> 28.1 us  [swap_e(): return lax.ppermute(value, 'expert', [(i, i ^ bits) for i in range(4)])]
    pallas_call x0 -> x1, Pallas kernels: none -> 4.6 us  [first_hop(): pl.pallas_call(functools.partial(first_kernel, experts), out_shape=shape(...]
    unnamed x26 -> x22, local copies, waits for them, and re-layouts: 5.86 us -> 3.3 us
  transfers between devices with their start and end apart: 51 -> 51, of which waited for: 27 -> 26; matrix products, arithmetic and copies ran while one was open for 0% -> 1% of each run, Pallas kernels for 18% -> 20%
where the time goes in v4:
time: 200 us; the launch traced here: 199 us
  waiting for transfers between devices  73.2 us (37%)
  starting transfers between devices  62.5 us (31%)
  Pallas kernels  57.5 us (29%)
  local copies, waits for them, and re-layouts  4.19 us (2%)
    pallas_call x36, Pallas kernels, __call__(): pl.pallas_call(kernel, out_shape=list(shapes), grid_spec=pltpu.PrefetchSc...  52.9 us
    ppermute x18, waiting for transfers between devices, along_z(): return lax.ppermute(value, 'tensor', pairs)  42 us
    ppermute x18, starting transfers between devices, along_z(): return lax.ppermute(value, 'tensor', pairs)  39.2 us
    ppermute x30, waiting for transfers between devices, swap_e(): return lax.ppermute(value, 'expert', [(i, i ^ bits) for i in range(4)])  28.1 us
    ppermute x30, starting transfers between devices, swap_e(): return lax.ppermute(value, 'expert', [(i, i ^ bits) for i in range(4)])  18.9 us
    pallas_call x1, Pallas kernels, first_hop(): pl.pallas_call(functools.partial(first_kernel, experts), out_shape=shape(...  4.6 us
    ppermute x3, starting transfers between devices, swap_z(): return lax.ppermute(value, 'tensor', [(i, i ^ bits) for i in range(4)])  4.45 us
  transfers between devices with their start and end apart: 51, of which 26 were waited for; matrix products, arithmetic and copies ran while one was open for 1% of the time, Pallas kernels for 20%

profile of v4, /device:TPU:0, one launch (start us, length us, event | category | flops | bytes accessed | tf_op | source)
XLA Modules:
  0.0 199.0 jit_solution(15339880503097252099)
XLA Ops:
  0.6 4.6 %shard_map.122.rest_0_.left_ref = bf16[144,2048]{1,0:T(8,128)(2,1)} custom-call(s32[4,128]{1,0:T(4,128)} %bitcast.46, bf16[512,1024]{1,0:T(8,128)(2,1)} %context_ref.5, bf16[1024,2048]{1,0:T(8,128)(2,1)} %weight_ref.5, bf16[128,2048]{1,0:T(8,128)(2,1)} %resid_ref.5), custom_call_target="tpu_custom_call" | custom-call | tf_op jit(solution)/shard_map/pallas_call | solution.py:624
  5.3 5.0 %collective-permute-start = (bf16[144,2048]{1,0:T(8,128)(2,1)}, bf16[144,2048]{1,0:T(8,128)(2,1)S(1)}, u32[]{:S(2)}, u32[]{:S(2)}) collective-permute-start(bf16[144,2048]{1,0:T(8,128)(2,1)} %shard_map.122.rest_0_.left_ref), channel_id=1, source_target_pairs={{0,1},{3,2},{4,5},{7,6},{8,9},{11,10},{12,13},{15,14},{16,17},{19,... | collective-permute-start | bytes 1769480 | tf_op jit(solution)/shard_map/ppermute | solution.py:584
  11.0 2.2 %copy-done.2 = bf16[1024,2048]{1,0:T(8,128)(2,1)S(1)} copy-done((bf16[1024,2048]{1,0:T(8,128)(2,1)S(1)}, bf16[1024,2048]{1,0:T(8,128)(2,1)}, u32[]{:S(2)}) %copy-start.2) | copy-done | bytes 4194328
  19.5 4.7 %collective-permute-done.right_ref = bf16[144,2048]{1,0:T(8,128)(2,1)S(1)} collective-permute-done((bf16[144,2048]{1,0:T(8,128)(2,1)}, bf16[144,2048]{1,0:T(8,128)(2,1)S(1)}, u32[]{:S(2)}, u32[]{:S(2)}) %collective-permute-start) | collective-permute-done | bytes 589856 | tf_op jit(solution)/shard_map/ppermute | solution.py:584
  25.6 7.9 %collective-permute-start.6 = (bf16[128,2048]{1,0:T(8,128)(2,1)S(1)}, bf16[128,2048]{1,0:T(8,128)(2,1)}, u32[]{:S(2)}, u32[]{:S(2)}) collective-permute-start(bf16[128,2048]{1,0:T(8,128)(2,1)S(1)} %shard_map.124.rest_0_.left_ref), channel_id=1, source_target_pairs={{0,1},{3,2},{4,5},{7,6},{8,9},{11,10},{12,13},{15,14},{16,17},{19,... | collective-permute-start | bytes 1572872 | tf_op jit(solution)/shard_map/ppermute | solution.py:584
  37.5 7.3 %collective-permute-start.4 = (bf16[128,2048]{1,0:T(8,128)(2,1)S(1)}, bf16[128,2048]{1,0:T(8,128)(2,1)}, u32[]{:S(2)}, u32[]{:S(2)}) collective-permute-start(bf16[128,2048]{1,0:T(8,128)(2,1)S(1)} %shard_map.125._.left_ref), channel_id=1, source_target_pairs={{0,1},{3,2},{4,5},{7,6},{8,9},{11,10},{12,13},{15,14},{16,17},{19,... | collective-permute-start | bytes 1572872 | tf_op jit(solution)/shard_map/ppermute | solution.py:584
  52.8 3.9 %collective-permute-done.4.right_ref = bf16[128,2048]{1,0:T(8,128)(2,1)} collective-permute-done((bf16[128,2048]{1,0:T(8,128)(2,1)S(1)}, bf16[128,2048]{1,0:T(8,128)(2,1)}, u32[]{:S(2)}, u32[]{:S(2)}) %collective-permute-start.4) | collective-permute-done | bytes 524320 | tf_op jit(solution)/shard_map/ppermute | solution.py:584
  59.2 4.7 %collective-permute-done.3.refs_1_ = bf16[144,2048]{1,0:T(8,128)(2,1)S(1)} collective-permute-done((bf16[144,2048]{1,0:T(8,128)(2,1)S(1)}, bf16[144,2048]{1,0:T(8,128)(2,1)S(1)}, u32[]{:S(2)}, u32[]{:S(2)}) %collective-permute-start.3) | collective-permute-done | bytes 589856 | tf_op jit(solution)/shard_map/ppermute | solution.py:584
  67.9 3.5 %collective-permute-done.10.refs_1_ = bf16[128,2048]{1,0:T(8,128)(2,1)S(1)} collective-permute-done((bf16[128,2048]{1,0:T(8,128)(2,1)S(1)}, bf16[128,2048]{1,0:T(8,128)(2,1)S(1)}, u32[]{:S(2)}, u32[]{:S(2)}) %collective-permute-start.10) | collective-permute-done | bytes 524320 | tf_op jit(solution)/shard_map/ppermute | solution.py:584
  81.5 4.0 %collective-permute-done.15.refs_1_ = bf16[128,2048]{1,0:T(8,128)(2,1)S(1)} collective-permute-done((bf16[128,2048]{1,0:T(8,128)(2,1)S(1)}, bf16[128,2048]{1,0:T(8,128)(2,1)S(1)}, u32[]{:S(2)}, u32[]{:S(2)}) %collective-permute-start.15) | collective-permute-done | bytes 524320 | tf_op jit(solution)/shard_map/ppermute | solution.py:584
  89.5 2.0 shard_map.138
  91.5 4.0 %collective-permute-done.20.refs_1_ = bf16[128,2048]{1,0:T(8,128)(2,1)S(1)} collective-permute-done((bf16[128,2048]{1,0:T(8,128)(2,1)S(1)}, bf16[128,2048]{1,0:T(8,128)(2,1)S(1)}, u32[]{:S(2)}, u32[]{:S(2)}) %collective-permute-start.20) | collective-permute-done | bytes 524320 | tf_op jit(solution)/shard_map/ppermute | solution.py:584
  100.7 3.5 %collective-permute-done.22.r2 = bf16[40,2176]{1,0:T(8,128)(2,1)S(1)} collective-permute-done((bf16[40,2176]{1,0:T(8,128)(2,1)S(1)}, bf16[40,2176]{1,0:T(8,128)(2,1)S(1)}, u32[]{:S(2)}, u32[]{:S(2)}) %collective-permute-start.22) | collective-permute-done | bytes 174112 | tf_op jit(solution)/shard_map/ppermute | solution.py:590
  104.2 2.8 %collective-permute-done.23.r3 = bf16[40,2176]{1,0:T(8,128)(2,1)S(1)} collective-permute-done((bf16[40,2176]{1,0:T(8,128)(2,1)S(1)}, bf16[40,2176]{1,0:T(8,128)(2,1)S(1)}, u32[]{:S(2)}, u32[]{:S(2)}) %collective-permute-start.23) | collective-permute-done | bytes 174112 | tf_op jit(solution)/shard_map/ppermute | solution.py:590
  107.0 2.0 shard_map.141
  112.2 2.3 %collective-permute-done.25.p2 = bf16[8,2048]{1,0:T(8,128)(2,1)S(1)} collective-permute-done((bf16[8,2048]{1,0:T(8,128)(2,1)S(1)}, bf16[8,2048]{1,0:T(8,128)(2,1)S(1)}, u32[]{:S(2)}, u32[]{:S(2)}) %collective-permute-start.25) | collective-permute-done | bytes 32800 | tf_op jit(solution)/shard_map/ppermute | solution.py:590
  118.1 2.6 %collective-permute-start.29 = (bf16[8,2048]{1,0:T(8,128)(2,1)S(1)}, bf16[8,2048]{1,0:T(8,128)(2,1)S(1)}, u32[]{:S(2)}, u32[]{:S(2)}) collective-permute-start(bf16[8,2048]{1,0:T(8,128)(2,1)S(1)} %shard_map.143.p0._), channel_id=1, source_target_pairs={{0,3},{1,2},{2,1},{3,0},{4,7},{5,6},{6,5},{7,4},{8,11},{9,10},{10,... | collective-permute-start | bytes 98312 | tf_op jit(solution)/shard_map/ppermute | solution.py:587
  121.8 2.0 %collective-permute-done.29.p3 = bf16[8,2048]{1,0:T(8,128)(2,1)S(1)} collective-permute-done((bf16[8,2048]{1,0:T(8,128)(2,1)S(1)}, bf16[8,2048]{1,0:T(8,128)(2,1)S(1)}, u32[]{:S(2)}, u32[]{:S(2)}) %collective-permute-start.29) | collective-permute-done | bytes 32800 | tf_op jit(solution)/shard_map/ppermute | solution.py:587
  126.4 2.3 %collective-permute-done.31.q2 = bf16[8,2048]{1,0:T(8,128)(2,1)S(1)} collective-permute-done((bf16[8,2048]{1,0:T(8,128)(2,1)S(1)}, bf16[8,2048]{1,0:T(8,128)(2,1)S(1)}, u32[]{:S(2)}, u32[]{:S(2)}) %collective-permute-start.31) | collective-permute-done | bytes 32800 | tf_op jit(solution)/shard_map/ppermute | solution.py:590
  128.9 3.3 %shard_map.145 = (f32[32,2048]{1,0:T(8,128)S(1)}, f32[32,768]{1,0:T(8,128)S(1)}, f32[1]{0:T(128)}) custom-call(s32[15]{0:T(128)S(1)} %concatenate.6.n, bf16[8,2048]{1,0:T(8,128)(2,1)S(1)} %shard_map.144.q0._, bf16[8,2048]{1,0:T(8,128)(2,1)S(1)} %collective-permute-done.30.q1, bf16[8,2048]{1,0:T(8,128)(2,1)S(1)} %collective-permute-done.31.q2, ...), custom_call_target="tpu_custom_call" | custom-call | flops 1 | bytes 1 | tf_op jit(solution)/shard_map/pallas_call | solution.py:530
  132.3 3.1 %shard_map.146 = (bf16[40,2048]{1,0:T(8,128)(2,1)S(1)}, bf16[40,2048]{1,0:T(8,128)(2,1)S(1)}, bf16[40,2048]{1,0:T(8,128)(2,1)S(1)}, bf16[40,2048]{1,0:T(8,128)(2,1)S(1)}) custom-call(s32[15]{0:T(128)S(1)} %concatenate.6.n, f32[4,160,768]{2,1,0:T(8,128)S(1)} %get-tuple-element.126.a_ref, f32[4,160,768]{2,1,0:T(8,128)S(1)} %get-tuple-element.127.b_ref, ...), custom_call_target="tpu_custom_call" | custom-call | flops 1 | bytes 1 | tf_op jit(solution)/shard_map/pallas_call | solution.py:530
  137.4 3.1 %shard_map.147 = (bf16[40,2048]{1,0:T(8,128)(2,1)S(1)}, bf16[40,2048]{1,0:T(8,128)(2,1)S(1)}, bf16[40,2048]{1,0:T(8,128)(2,1)S(1)}, bf16[40,2048]{1,0:T(8,128)(2,1)S(1)}) custom-call(s32[15]{0:T(128)S(1)} %concatenate.6.n, f32[4,160,768]{2,1,0:T(8,128)S(1)} %get-tuple-element.126.a_ref, f32[4,160,768]{2,1,0:T(8,128)S(1)} %get-tuple-element.127.b_ref, ...), custom_call_target="tpu_custom_call" | custom-call | flops 1 | bytes 1 | tf_op jit(solution)/shard_map/pallas_call | solution.py:530
  140.5 2.1 %collective-permute-done.37.r2 = bf16[40,2048]{1,0:T(8,128)(2,1)S(1)} collective-permute-done((bf16[40,2048]{1,0:T(8,128)(2,1)S(1)}, bf16[40,2048]{1,0:T(8,128)(2,1)S(1)}, u32[]{:S(2)}, u32[]{:S(2)}) %collective-permute-start.37) | collective-permute-done | bytes 163872 | tf_op jit(solution)/shard_map/ppermute | solution.py:590
  142.6 2.6 %collective-permute-done.38.r3 = bf16[40,2048]{1,0:T(8,128)(2,1)S(1)} collective-permute-done((bf16[40,2048]{1,0:T(8,128)(2,1)S(1)}, bf16[40,2048]{1,0:T(8,128)(2,1)S(1)}, u32[]{:S(2)}, u32[]{:S(2)}) %collective-permute-start.38) | collective-permute-done | bytes 163872 | tf_op jit(solution)/shard_map/ppermute | solution.py:590
  149.6 3.1 %shard_map.149 = (bf16[40,2048]{1,0:T(8,128)(2,1)S(1)}, bf16[40,2048]{1,0:T(8,128)(2,1)S(1)}, bf16[40,2048]{1,0:T(8,128)(2,1)S(1)}, bf16[40,2048]{1,0:T(8,128)(2,1)S(1)}) custom-call(s32[15]{0:T(128)S(1)} %concatenate.6.n, f32[4,160,768]{2,1,0:T(8,128)S(1)} %get-tuple-element.126.a_ref, f32[4,160,768]{2,1,0:T(8,128)S(1)} %get-tuple-element.127.b_ref, ...), custom_call_target="tpu_custom_call" | custom-call | flops 1 | bytes 1 | tf_op jit(solution)/shard_map/pallas_call | solution.py:530
  154.9 2.3 %collective-permute-done.35.r3 = bf16[40,2048]{1,0:T(8,128)(2,1)S(1)} collective-permute-done((bf16[40,2048]{1,0:T(8,128)(2,1)S(1)}, bf16[40,2048]{1,0:T(8,128)(2,1)S(1)}, u32[]{:S(2)}, u32[]{:S(2)}) %collective-permute-start.35) | collective-permute-done | bytes 163872 | tf_op jit(solution)/shard_map/ppermute | solution.py:590
  158.0 3.1 %shard_map.151 = (bf16[40,2048]{1,0:T(8,128)(2,1)S(1)}, bf16[40,2048]{1,0:T(8,128)(2,1)S(1)}, bf16[40,2048]{1,0:T(8,128)(2,1)S(1)}, bf16[40,2048]{1,0:T(8,128)(2,1)S(1)}) custom-call(s32[15]{0:T(128)S(1)} %concatenate.6.n, f32[4,160,768]{2,1,0:T(8,128)S(1)} %get-tuple-element.126.a_ref, f32[4,160,768]{2,1,0:T(8,128)S(1)} %get-tuple-element.127.b_ref, ...), custom_call_target="tpu_custom_call" | custom-call | flops 1 | bytes 1 | tf_op jit(solution)/shard_map/pallas_call | solution.py:530
  168.3 3.1 %collective-permute-start.48 = (bf16[128,2048]{1,0:T(8,128)(2,1)S(1)}, bf16[128,2048]{1,0:T(8,128)(2,1)S(1)}, u32[]{:S(2)}, u32[]{:S(2)}) collective-permute-start(bf16[128,2048]{1,0:T(8,128)(2,1)S(1)} %get-tuple-element.155), channel_id=1, source_target_pairs={{0,1},{3,2},{4,5},{7,6},{8,9},{11,10},{12,13},{15,14},{16,17},{19,... | collective-permute-start | bytes 1572872 | tf_op jit(solution)/shard_map/ppermute | solution.py:584
  171.4 2.5 %collective-permute-done.46.r2 = bf16[40,2048]{1,0:T(8,128)(2,1)S(1)} collective-permute-done((bf16[40,2048]{1,0:T(8,128)(2,1)S(1)}, bf16[40,2048]{1,0:T(8,128)(2,1)S(1)}, u32[]{:S(2)}, u32[]{:S(2)}) %collective-permute-start.46) | collective-permute-done | bytes 163872 | tf_op jit(solution)/shard_map/ppermute | solution.py:590
  181.7 3.8 %collective-permute-done.48.r4 = bf16[128,2048]{1,0:T(8,128)(2,1)S(1)} collective-permute-done((bf16[128,2048]{1,0:T(8,128)(2,1)S(1)}, bf16[128,2048]{1,0:T(8,128)(2,1)S(1)}, u32[]{:S(2)}, u32[]{:S(2)}) %collective-permute-start.48) | collective-permute-done | bytes 524320 | tf_op jit(solution)/shard_map/ppermute | solution.py:584
  185.5 11.5 %collective-permute-done.50.r6 = bf16[128,2048]{1,0:T(8,128)(2,1)S(1)} collective-permute-done((bf16[128,2048]{1,0:T(8,128)(2,1)S(1)}, bf16[128,2048]{1,0:T(8,128)(2,1)S(1)}, u32[]{:S(2)}, u32[]{:S(2)}) %collective-permute-start.50) | collective-permute-done | bytes 524320 | tf_op jit(solution)/shard_map/ppermute | solution.py:584
  197.0 2.0 shard_map.158
  (141 shorter events, 81.1 us)
Async XLA Ops:
  5.3 19.0 %collective-permute-start = (bf16[144,2048]{1,0:T(8,128)(2,1)}, bf16[144,2048]{1,0:T(8,128)(2,1)S(1)}, u32[]{:S(2)}, u32[]{:S(2)}) collective-permute-start(bf16[144,2048]{1,0:T(8,128)(2,1)} %shard_map.122.rest_0_.left_ref), channel_id=1, source_target_pairs={{0,1},{3,2},{4,5},{7,6},{8,9},{11,10},{12,13},{15,14},{16,17},{19,... | collective-permute-start | bytes 1769480 | tf_op jit(solution)/shard_map/ppermute | solution.py:584
  15.6 19.8 %collective-permute-start.2 = (bf16[128,2048]{1,0:T(8,128)(2,1)S(1)}, bf16[128,2048]{1,0:T(8,128)(2,1)S(1)}, u32[]{:S(2)}, u32[]{:S(2)}) collective-permute-start(bf16[128,2048]{1,0:T(8,128)(2,1)S(1)} %shard_map.123.rest_0_.left_ref), channel_id=1, source_target_pairs={{0,1},{3,2},{4,5},{7,6},{8,9},{11,10},{12,13},{15,14},{16,17},{19,... | collective-permute-start | bytes 1572872 | tf_op jit(solution)/shard_map/ppermute | solution.py:584
  24.9 20.1 %collective-permute-start.1 = (bf16[144,2048]{1,0:T(8,128)(2,1)S(1)}, bf16[144,2048]{1,0:T(8,128)(2,1)S(1)}, u32[]{:S(2)}, u32[]{:S(2)}) collective-permute-start(bf16[144,2048]{1,0:T(8,128)(2,1)S(1)} %shard_map.126._.left_ref), channel_id=1, source_target_pairs={{1,2},{2,1},{5,6},{6,5},{9,10},{10,9},{13,14},{14,13},{17,18},{18,... | collective-permute-start | bytes 1769480 | tf_op jit(solution)/shard_map/ppermute | solution.py:584
  25.6 21.5 %collective-permute-start.6 = (bf16[128,2048]{1,0:T(8,128)(2,1)S(1)}, bf16[128,2048]{1,0:T(8,128)(2,1)}, u32[]{:S(2)}, u32[]{:S(2)}) collective-permute-start(bf16[128,2048]{1,0:T(8,128)(2,1)S(1)} %shard_map.124.rest_0_.left_ref), channel_id=1, source_target_pairs={{0,1},{3,2},{4,5},{7,6},{8,9},{11,10},{12,13},{15,14},{16,17},{19,... | collective-permute-start | bytes 1572872 | tf_op jit(solution)/shard_map/ppermute | solution.py:584
  36.0 13.7 %collective-permute-start.5 = (bf16[128,2048]{1,0:T(8,128)(2,1)S(1)}, bf16[128,2048]{1,0:T(8,128)(2,1)}, u32[]{:S(2)}, u32[]{:S(2)}) collective-permute-start(bf16[128,2048]{1,0:T(8,128)(2,1)S(1)} %shard_map.127._.left_ref), channel_id=1, source_target_pairs={{1,2},{2,1},{5,6},{6,5},{9,10},{10,9},{13,14},{14,13},{17,18},{18,... | collective-permute-start | bytes 1572872 | tf_op jit(solution)/shard_map/ppermute | solution.py:584
  37.5 19.2 %collective-permute-start.4 = (bf16[128,2048]{1,0:T(8,128)(2,1)S(1)}, bf16[128,2048]{1,0:T(8,128)(2,1)}, u32[]{:S(2)}, u32[]{:S(2)}) collective-permute-start(bf16[128,2048]{1,0:T(8,128)(2,1)S(1)} %shard_map.125._.left_ref), channel_id=1, source_target_pairs={{0,1},{3,2},{4,5},{7,6},{8,9},{11,10},{12,13},{15,14},{16,17},{19,... | collective-permute-start | bytes 1572872 | tf_op jit(solution)/shard_map/ppermute | solution.py:584
  45.7 18.2 %collective-permute-start.3 = (bf16[144,2048]{1,0:T(8,128)(2,1)S(1)}, bf16[144,2048]{1,0:T(8,128)(2,1)S(1)}, u32[]{:S(2)}, u32[]{:S(2)}) collective-permute-start(bf16[144,2048]{1,0:T(8,128)(2,1)S(1)} %shard_map.128._.refs_0_), channel_id=1, source_target_pairs={{1,0},{2,3},{5,4},{6,7},{9,8},{10,11},{13,12},{14,15},{17,16},{18,... | collective-permute-start | bytes 1769480 | tf_op jit(solution)/shard_map/ppermute | solution.py:584
  48.8 18.0 %collective-permute-start.11 = (bf16[128,2048]{1,0:T(8,128)(2,1)S(1)}, bf16[128,2048]{1,0:T(8,128)(2,1)S(1)}, u32[]{:S(2)}, u32[]{:S(2)}) collective-permute-start(bf16[128,2048]{1,0:T(8,128)(2,1)S(1)} %shard_map.129._.left_ref), channel_id=1, source_target_pairs={{1,2},{2,1},{5,6},{6,5},{9,10},{10,9},{13,14},{14,13},{17,18},{18,... | collective-permute-start | bytes 1572872 | tf_op jit(solution)/shard_map/ppermute | solution.py:584
  51.4 20.0 %collective-permute-start.10 = (bf16[128,2048]{1,0:T(8,128)(2,1)S(1)}, bf16[128,2048]{1,0:T(8,128)(2,1)S(1)}, u32[]{:S(2)}, u32[]{:S(2)}) collective-permute-start(bf16[128,2048]{1,0:T(8,128)(2,1)S(1)} %shard_map.130._.refs_0_), channel_id=1, source_target_pairs={{1,0},{2,3},{5,4},{6,7},{9,8},{10,11},{13,12},{14,15},{17,16},{18,... | collective-permute-start | bytes 1572872 | tf_op jit(solution)/shard_map/ppermute | solution.py:584
  58.4 19.0 %collective-permute-start.16 = (bf16[128,2048]{1,0:T(8,128)(2,1)S(1)}, bf16[128,2048]{1,0:T(8,128)(2,1)S(1)}, u32[]{:S(2)}, u32[]{:S(2)}) collective-permute-start(bf16[128,2048]{1,0:T(8,128)(2,1)S(1)} %shard_map.131.refs_5_.left_ref), channel_id=1, source_target_pairs={{1,2},{2,1},{5,6},{6,5},{9,10},{10,9},{13,14},{14,13},{17,18},{18,... | collective-permute-start | bytes 1572872 | tf_op jit(solution)/shard_map/ppermute | solution.py:584
  65.2 8.8 %collective-permute-start.7 = (bf16[40,2176]{1,0:T(8,128)(2,1)S(1)}, bf16[40,2176]{1,0:T(8,128)(2,1)S(1)}, u32[]{:S(2)}, u32[]{:S(2)}) collective-permute-start(bf16[40,2176]{1,0:T(8,128)(2,1)S(1)} %get-tuple-element.80), channel_id=1, source_target_pairs={{0,4},{4,0},{8,12},{12,8},{1,5},{5,1},{9,13},{13,9},{2,6},{6,2},{1... | collective-permute-start | bytes 522248 | tf_op jit(solution)/shard_map/ppermute | solution.py:590
  65.3 8.7 %collective-permute-start.8 = (bf16[40,2176]{1,0:T(8,128)(2,1)S(1)}, bf16[40,2176]{1,0:T(8,128)(2,1)S(1)}, u32[]{:S(2)}, u32[]{:S(2)}) collective-permute-start(bf16[40,2176]{1,0:T(8,128)(2,1)S(1)} %get-tuple-element.81), channel_id=1, source_target_pairs={{0,8},{4,12},{8,0},{12,4},{1,9},{5,13},{9,1},{13,5},{2,10},{6,14},... | collective-permute-start | bytes 522248 | tf_op jit(solution)/shard_map/ppermute | solution.py:590
  66.9 8.6 %collective-permute-start.9 = (bf16[40,2176]{1,0:T(8,128)(2,1)S(1)}, bf16[40,2176]{1,0:T(8,128)(2,1)S(1)}, u32[]{:S(2)}, u32[]{:S(2)}) collective-permute-start(bf16[40,2176]{1,0:T(8,128)(2,1)S(1)} %get-tuple-element.82), channel_id=1, source_target_pairs={{0,12},{4,8},{8,4},{12,0},{1,13},{5,9},{9,5},{13,1},{2,14},{6,10},... | collective-permute-start | bytes 522248 | tf_op jit(solution)/shard_map/ppermute | solution.py:590
  71.3 14.2 %collective-permute-start.15 = (bf16[128,2048]{1,0:T(8,128)(2,1)S(1)}, bf16[128,2048]{1,0:T(8,128)(2,1)S(1)}, u32[]{:S(2)}, u32[]{:S(2)}) collective-permute-start(bf16[128,2048]{1,0:T(8,128)(2,1)S(1)} %shard_map.133.refs_8_.refs_0_), channel_id=1, source_target_pairs={{1,0},{2,3},{5,4},{6,7},{9,8},{10,11},{13,12},{14,15},{17,16},{18,... | collective-permute-start | bytes 1572872 | tf_op jit(solution)/shard_map/ppermute | solution.py:584
  78.1 17.4 %collective-permute-start.20 = (bf16[128,2048]{1,0:T(8,128)(2,1)S(1)}, bf16[128,2048]{1,0:T(8,128)(2,1)S(1)}, u32[]{:S(2)}, u32[]{:S(2)}) collective-permute-start(bf16[128,2048]{1,0:T(8,128)(2,1)S(1)} %shard_map.136.refs_8_.refs_0_), channel_id=1, source_target_pairs={{1,0},{2,3},{5,4},{6,7},{9,8},{10,11},{13,12},{14,15},{17,16},{18,... | collective-permute-start | bytes 1572872 | tf_op jit(solution)/shard_map/ppermute | solution.py:584
  79.9 8.6 %collective-permute-start.13 = (bf16[40,2176]{1,0:T(8,128)(2,1)S(1)}, bf16[40,2176]{1,0:T(8,128)(2,1)S(1)}, u32[]{:S(2)}, u32[]{:S(2)}) collective-permute-start(bf16[40,2176]{1,0:T(8,128)(2,1)S(1)} %get-tuple-element.89), channel_id=1, source_target_pairs={{0,8},{4,12},{8,0},{12,4},{1,9},{5,13},{9,1},{13,5},{2,10},{6,14},... | collective-permute-start | bytes 522248 | tf_op jit(solution)/shard_map/ppermute | solution.py:590
  81.4 8.1 %collective-permute-start.14 = (bf16[40,2176]{1,0:T(8,128)(2,1)S(1)}, bf16[40,2176]{1,0:T(8,128)(2,1)S(1)}, u32[]{:S(2)}, u32[]{:S(2)}) collective-permute-start(bf16[40,2176]{1,0:T(8,128)(2,1)S(1)} %get-tuple-element.90), channel_id=1, source_target_pairs={{0,12},{4,8},{8,4},{12,0},{1,13},{5,9},{9,5},{13,1},{2,14},{6,10},... | collective-permute-start | bytes 522248 | tf_op jit(solution)/shard_map/ppermute | solution.py:590
  86.9 11.6 %collective-permute-start.17 = (bf16[40,2176]{1,0:T(8,128)(2,1)S(1)}, bf16[40,2176]{1,0:T(8,128)(2,1)S(1)}, u32[]{:S(2)}, u32[]{:S(2)}) collective-permute-start(bf16[40,2176]{1,0:T(8,128)(2,1)S(1)} %get-tuple-element.99), channel_id=1, source_target_pairs={{0,4},{4,0},{8,12},{12,8},{1,5},{5,1},{9,13},{13,9},{2,6},{6,2},{1... | collective-permute-start | bytes 522248 | tf_op jit(solution)/shard_map/ppermute | solution.py:590
  87.0 11.8 %collective-permute-start.18 = (bf16[40,2176]{1,0:T(8,128)(2,1)S(1)}, bf16[40,2176]{1,0:T(8,128)(2,1)S(1)}, u32[]{:S(2)}, u32[]{:S(2)}) collective-permute-start(bf16[40,2176]{1,0:T(8,128)(2,1)S(1)} %get-tuple-element.100), channel_id=1, source_target_pairs={{0,8},{4,12},{8,0},{12,4},{1,9},{5,13},{9,1},{13,5},{2,10},{6,14},... | collective-permute-start | bytes 522248 | tf_op jit(solution)/shard_map/ppermute | solution.py:590
  88.5 10.2 %collective-permute-start.19 = (bf16[40,2176]{1,0:T(8,128)(2,1)S(1)}, bf16[40,2176]{1,0:T(8,128)(2,1)S(1)}, u32[]{:S(2)}, u32[]{:S(2)}) collective-permute-start(bf16[40,2176]{1,0:T(8,128)(2,1)S(1)} %get-tuple-element.101), channel_id=1, source_target_pairs={{0,12},{4,8},{8,4},{12,0},{1,13},{5,9},{9,5},{13,1},{2,14},{6,10},... | collective-permute-start | bytes 522248 | tf_op jit(solution)/shard_map/ppermute | solution.py:590
  98.5 8.6 %collective-permute-start.23 = (bf16[40,2176]{1,0:T(8,128)(2,1)S(1)}, bf16[40,2176]{1,0:T(8,128)(2,1)S(1)}, u32[]{:S(2)}, u32[]{:S(2)}) collective-permute-start(bf16[40,2176]{1,0:T(8,128)(2,1)S(1)} %get-tuple-element.112), channel_id=1, source_target_pairs={{0,12},{4,8},{8,4},{12,0},{1,13},{5,9},{9,5},{13,1},{2,14},{6,10},... | collective-permute-start | bytes 522248 | tf_op jit(solution)/shard_map/ppermute | solution.py:590
  136.6 8.5 %collective-permute-start.38 = (bf16[40,2048]{1,0:T(8,128)(2,1)S(1)}, bf16[40,2048]{1,0:T(8,128)(2,1)S(1)}, u32[]{:S(2)}, u32[]{:S(2)}) collective-permute-start(bf16[40,2048]{1,0:T(8,128)(2,1)S(1)} %get-tuple-element.138), channel_id=1, source_target_pairs={{0,12},{4,8},{8,4},{12,0},{1,13},{5,9},{9,5},{13,1},{2,14},{6,10},... | collective-permute-start | bytes 491528 | tf_op jit(solution)/shard_map/ppermute | solution.py:590
  146.0 19.1 %collective-permute-start.39 = (bf16[128,2048]{1,0:T(8,128)(2,1)S(1)}, bf16[128,2048]{1,0:T(8,128)(2,1)S(1)}, u32[]{:S(2)}, u32[]{:S(2)}) collective-permute-start(bf16[128,2048]{1,0:T(8,128)(2,1)S(1)} %get-tuple-element.142), channel_id=1, source_target_pairs={{0,1},{3,2},{4,5},{7,6},{8,9},{11,10},{12,13},{15,14},{16,17},{19,... | collective-permute-start | bytes 1572872 | tf_op jit(solution)/shard_map/ppermute | solution.py:584
  148.8 8.4 %collective-permute-start.35 = (bf16[40,2048]{1,0:T(8,128)(2,1)S(1)}, bf16[40,2048]{1,0:T(8,128)(2,1)S(1)}, u32[]{:S(2)}, u32[]{:S(2)}) collective-permute-start(bf16[40,2048]{1,0:T(8,128)(2,1)S(1)} %get-tuple-element.135), channel_id=1, source_target_pairs={{0,12},{4,8},{8,4},{12,0},{1,13},{5,9},{9,5},{13,1},{2,14},{6,10},... | collective-permute-start | bytes 491528 | tf_op jit(solution)/shard_map/ppermute | solution.py:590
  152.7 9.8 %collective-permute-start.40 = (bf16[40,2048]{1,0:T(8,128)(2,1)S(1)}, bf16[40,2048]{1,0:T(8,128)(2,1)S(1)}, u32[]{:S(2)}, u32[]{:S(2)}) collective-permute-start(bf16[40,2048]{1,0:T(8,128)(2,1)S(1)} %get-tuple-element.143), channel_id=1, source_target_pairs={{0,4},{4,0},{8,12},{12,8},{1,5},{5,1},{9,13},{13,9},{2,6},{6,2},{1... | collective-permute-start | bytes 491528 | tf_op jit(solution)/shard_map/ppermute | solution.py:590
  153.2 9.3 %collective-permute-start.41 = (bf16[40,2048]{1,0:T(8,128)(2,1)S(1)}, bf16[40,2048]{1,0:T(8,128)(2,1)S(1)}, u32[]{:S(2)}, u32[]{:S(2)}) collective-permute-start(bf16[40,2048]{1,0:T(8,128)(2,1)S(1)} %get-tuple-element.144), channel_id=1, source_target_pairs={{0,8},{4,12},{8,0},{12,4},{1,9},{5,13},{9,1},{13,5},{2,10},{6,14},... | collective-permute-start | bytes 491528 | tf_op jit(solution)/shard_map/ppermute | solution.py:590
  154.9 9.3 %collective-permute-start.42 = (bf16[40,2048]{1,0:T(8,128)(2,1)S(1)}, bf16[40,2048]{1,0:T(8,128)(2,1)S(1)}, u32[]{:S(2)}, u32[]{:S(2)}) collective-permute-start(bf16[40,2048]{1,0:T(8,128)(2,1)S(1)} %get-tuple-element.145), channel_id=1, source_target_pairs={{0,12},{4,8},{8,4},{12,0},{1,13},{5,9},{9,5},{13,1},{2,14},{6,10},... | collective-permute-start | bytes 491528 | tf_op jit(solution)/shard_map/ppermute | solution.py:590
  161.2 16.2 %collective-permute-start.44 = (bf16[128,2048]{1,0:T(8,128)(2,1)S(1)}, bf16[128,2048]{1,0:T(8,128)(2,1)S(1)}, u32[]{:S(2)}, u32[]{:S(2)}) collective-permute-start(bf16[128,2048]{1,0:T(8,128)(2,1)S(1)} %get-tuple-element.148), channel_id=1, source_target_pairs={{0,1},{3,2},{4,5},{7,6},{8,9},{11,10},{12,13},{15,14},{16,17},{19,... | collective-permute-start | bytes 1572872 | tf_op jit(solution)/shard_map/ppermute | solution.py:584
  165.7 13.0 %collective-permute-start.43 = (bf16[128,2048]{1,0:T(8,128)(2,1)S(1)}, bf16[128,2048]{1,0:T(8,128)(2,1)S(1)}, u32[]{:S(2)}, u32[]{:S(2)}) collective-permute-start(bf16[128,2048]{1,0:T(8,128)(2,1)S(1)} %shard_map.153._), channel_id=1, source_target_pairs={{1,2},{2,1},{5,6},{6,5},{9,10},{10,9},{13,14},{14,13},{17,18},{18,... | collective-permute-start | bytes 1572872 | tf_op jit(solution)/shard_map/ppermute | solution.py:584
  167.9 7.9 %collective-permute-start.47 = (bf16[40,2048]{1,0:T(8,128)(2,1)S(1)}, bf16[40,2048]{1,0:T(8,128)(2,1)S(1)}, u32[]{:S(2)}, u32[]{:S(2)}) collective-permute-start(bf16[40,2048]{1,0:T(8,128)(2,1)S(1)} %get-tuple-element.151), channel_id=1, source_target_pairs={{0,12},{4,8},{8,4},{12,0},{1,13},{5,9},{9,5},{13,1},{2,14},{6,10},... | collective-permute-start | bytes 491528 | tf_op jit(solution)/shard_map/ppermute | solution.py:590
  168.3 17.2 %collective-permute-start.48 = (bf16[128,2048]{1,0:T(8,128)(2,1)S(1)}, bf16[128,2048]{1,0:T(8,128)(2,1)S(1)}, u32[]{:S(2)}, u32[]{:S(2)}) collective-permute-start(bf16[128,2048]{1,0:T(8,128)(2,1)S(1)} %get-tuple-element.155), channel_id=1, source_target_pairs={{0,1},{3,2},{4,5},{7,6},{8,9},{11,10},{12,13},{15,14},{16,17},{19,... | collective-permute-start | bytes 1572872 | tf_op jit(solution)/shard_map/ppermute | solution.py:584
  179.4 17.7 %collective-permute-start.50 = (bf16[128,2048]{1,0:T(8,128)(2,1)S(1)}, bf16[128,2048]{1,0:T(8,128)(2,1)S(1)}, u32[]{:S(2)}, u32[]{:S(2)}) collective-permute-start(bf16[128,2048]{1,0:T(8,128)(2,1)S(1)} %shard_map.156._), channel_id=1, source_target_pairs={{1,0},{2,3},{5,4},{6,7},{9,8},{10,11},{13,12},{14,15},{17,16},{18,... | collective-permute-start | bytes 1572872 | tf_op jit(solution)/shard_map/ppermute | solution.py:584
  (30 other events, 200.9 us)

commit v5 on v4

--- a/solution.py
+++ b/solution.py
@@ -421,18 +421,16 @@
     rows = q0.shape[0]
     for way, part in enumerate((q0, q1, q2, q3)):
         all_ref[pl.ds(pl.multiple_of(n[PEER + way] * rows, rows), rows), :] = part[...].astype(F32)
-    embedded = all_ref[...]
+    embedded = all_ref[...].astype(BF16)
     count = embedded.shape[0]
     pairs = count // 2
-    norms = jnp.sqrt(jnp.sum(embedded * embedded, axis=1, keepdims=True) + EPSILON)
-    unit = embedded / norms
-    scores = (
-        lax.dot_general(
-            unit, unit, (((1,), (1,)), ((), ())), precision=EXACT_PRECISION, preferred_element_type=F32
-        )
-        / SOFTMAX_WARMTH
-    )
+    products = contract_last(embedded, embedded)
     row, column = iota((count, count), 0), iota((count, count), 1)
+    squares = jnp.where(row == column, products, 0.0)
+    inverse = 1.0 / jnp.sqrt(jnp.sum(squares, axis=1, keepdims=True) + EPSILON)
+    inverse_row = 1.0 / jnp.sqrt(jnp.sum(squares, axis=0, keepdims=True) + EPSILON)
+    cosines = products * inverse * inverse_row
+    scores = cosines / SOFTMAX_WARMTH
     is_pair = (row % 2 == 0) & (column % 2 == 1)
     matched = is_pair & (column == row + 1)
     exp_scores = jnp.where(is_pair, jnp.exp(jnp.where(is_pair, scores, 0.0)), 0.0)
@@ -444,14 +442,10 @@
     loss_ref[0] = jnp.sum(terms) / pairs
     dscore = (exp_scores / row_total - jnp.where(matched, 1.0, 0.0)) * (LOSS_SCALE / pairs)
     both = dscore + jnp.transpose(dscore)
-    dunit = (
-        lax.dot_general(
-            both, unit, (((1,), (0,)), ((), ())), precision=EXACT_PRECISION, preferred_element_type=F32
-        )
-        / SOFTMAX_WARMTH
-    )
-    radial = jnp.sum(unit * dunit, axis=1, keepdims=True)
-    grad = (dunit - unit * radial) / norms
+    both = both / SOFTMAX_WARMTH
+    radial = jnp.sum(both * cosines, axis=1, keepdims=True)
+    mixer = (both - jnp.where(row == column, radial, 0.0)) * inverse * inverse_row
+    grad = fold(dot_nn(stacked_halves(mixer), embedded))
     grad_ref[...] = grad
     hidden_grad_ref[...] = fold(contract_last(stacked_halves(grad), down_ref[...]))
 

time: 200 us -> 199 us (level)
  no operation moved by 1% of the time
where the time goes in v5:
time: 199 us; the launch traced here: 198 us
  waiting for transfers between devices  73.6 us (37%)
  starting transfers between devices  62.3 us (31%)
  Pallas kernels  56.5 us (28%)
  local copies, waits for them, and re-layouts  4.19 us (2%)
    pallas_call x36, Pallas kernels, __call__(): pl.pallas_call(kernel, out_shape=list(shapes), grid_spec=pltpu.PrefetchSc...  51.9 us
    ppermute x18, waiting for transfers between devices, along_z(): return lax.ppermute(value, 'tensor', pairs)  41.8 us
    ppermute x18, starting transfers between devices, along_z(): return lax.ppermute(value, 'tensor', pairs)  39 us
    ppermute x30, waiting for transfers between devices, swap_e(): return lax.ppermute(value, 'expert', [(i, i ^ bits) for i in range(4)])  28.7 us
    ppermute x30, starting transfers between devices, swap_e(): return lax.ppermute(value, 'expert', [(i, i ^ bits) for i in range(4)])  18.8 us
    pallas_call x1, Pallas kernels, first_hop(): pl.pallas_call(functools.partial(first_kernel, experts), out_shape=shape(...  4.6 us
    ppermute x3, starting transfers between devices, swap_z(): return lax.ppermute(value, 'tensor', [(i, i ^ bits) for i in range(4)])  4.45 us
  transfers between devices with their start and end apart: 51, of which 26 were waited for; matrix products, arithmetic and copies ran while one was open for 1% of the time, Pallas kernels for 20%

profile of v5, /device:TPU:0, one launch (start us, length us, event | category | flops | bytes accessed | tf_op | source)
XLA Modules:
  0.0 198.2 jit_solution(11096694196712790331)
XLA Ops:
  0.6 4.6 %shard_map.122.rest_0_.left_ref = bf16[144,2048]{1,0:T(8,128)(2,1)} custom-call(s32[4,128]{1,0:T(4,128)} %bitcast.46, bf16[512,1024]{1,0:T(8,128)(2,1)} %context_ref.5, bf16[1024,2048]{1,0:T(8,128)(2,1)} %weight_ref.5, bf16[128,2048]{1,0:T(8,128)(2,1)} %resid_ref.5), custom_call_target="tpu_custom_call" | custom-call | tf_op jit(solution)/shard_map/pallas_call | solution.py:618
  5.3 5.0 %collective-permute-start = (bf16[144,2048]{1,0:T(8,128)(2,1)}, bf16[144,2048]{1,0:T(8,128)(2,1)S(1)}, u32[]{:S(2)}, u32[]{:S(2)}) collective-permute-start(bf16[144,2048]{1,0:T(8,128)(2,1)} %shard_map.122.rest_0_.left_ref), channel_id=1, source_target_pairs={{0,1},{3,2},{4,5},{7,6},{8,9},{11,10},{12,13},{15,14},{16,17},{19,... | collective-permute-start | bytes 1769480 | tf_op jit(solution)/shard_map/ppermute | solution.py:578
  11.0 2.2 %copy-done.2 = bf16[1024,2048]{1,0:T(8,128)(2,1)S(1)} copy-done((bf16[1024,2048]{1,0:T(8,128)(2,1)S(1)}, bf16[1024,2048]{1,0:T(8,128)(2,1)}, u32[]{:S(2)}) %copy-start.2) | copy-done | bytes 4194328
  19.5 4.7 %collective-permute-done.right_ref = bf16[144,2048]{1,0:T(8,128)(2,1)S(1)} collective-permute-done((bf16[144,2048]{1,0:T(8,128)(2,1)}, bf16[144,2048]{1,0:T(8,128)(2,1)S(1)}, u32[]{:S(2)}, u32[]{:S(2)}) %collective-permute-start) | collective-permute-done | bytes 589856 | tf_op jit(solution)/shard_map/ppermute | solution.py:578
  25.6 7.9 %collective-permute-start.6 = (bf16[128,2048]{1,0:T(8,128)(2,1)S(1)}, bf16[128,2048]{1,0:T(8,128)(2,1)}, u32[]{:S(2)}, u32[]{:S(2)}) collective-permute-start(bf16[128,2048]{1,0:T(8,128)(2,1)S(1)} %shard_map.124.rest_0_.left_ref), channel_id=1, source_target_pairs={{0,1},{3,2},{4,5},{7,6},{8,9},{11,10},{12,13},{15,14},{16,17},{19,... | collective-permute-start | bytes 1572872 | tf_op jit(solution)/shard_map/ppermute | solution.py:578
  37.5 7.3 %collective-permute-start.4 = (bf16[128,2048]{1,0:T(8,128)(2,1)S(1)}, bf16[128,2048]{1,0:T(8,128)(2,1)}, u32[]{:S(2)}, u32[]{:S(2)}) collective-permute-start(bf16[128,2048]{1,0:T(8,128)(2,1)S(1)} %shard_map.125._.left_ref), channel_id=1, source_target_pairs={{0,1},{3,2},{4,5},{7,6},{8,9},{11,10},{12,13},{15,14},{16,17},{19,... | collective-permute-start | bytes 1572872 | tf_op jit(solution)/shard_map/ppermute | solution.py:578
  52.8 3.9 %collective-permute-done.4.right_ref = bf16[128,2048]{1,0:T(8,128)(2,1)} collective-permute-done((bf16[128,2048]{1,0:T(8,128)(2,1)S(1)}, bf16[128,2048]{1,0:T(8,128)(2,1)}, u32[]{:S(2)}, u32[]{:S(2)}) %collective-permute-start.4) | collective-permute-done | bytes 524320 | tf_op jit(solution)/shard_map/ppermute | solution.py:578
  59.2 4.7 %collective-permute-done.3.refs_1_ = bf16[144,2048]{1,0:T(8,128)(2,1)S(1)} collective-permute-done((bf16[144,2048]{1,0:T(8,128)(2,1)S(1)}, bf16[144,2048]{1,0:T(8,128)(2,1)S(1)}, u32[]{:S(2)}, u32[]{:S(2)}) %collective-permute-start.3) | collective-permute-done | bytes 589856 | tf_op jit(solution)/shard_map/ppermute | solution.py:578
  67.9 3.5 %collective-permute-done.10.refs_1_ = bf16[128,2048]{1,0:T(8,128)(2,1)S(1)} collective-permute-done((bf16[128,2048]{1,0:T(8,128)(2,1)S(1)}, bf16[128,2048]{1,0:T(8,128)(2,1)S(1)}, u32[]{:S(2)}, u32[]{:S(2)}) %collective-permute-start.10) | collective-permute-done | bytes 524320 | tf_op jit(solution)/shard_map/ppermute | solution.py:578
  81.5 4.0 %collective-permute-done.15.refs_1_ = bf16[128,2048]{1,0:T(8,128)(2,1)S(1)} collective-permute-done((bf16[128,2048]{1,0:T(8,128)(2,1)S(1)}, bf16[128,2048]{1,0:T(8,128)(2,1)S(1)}, u32[]{:S(2)}, u32[]{:S(2)}) %collective-permute-start.15) | collective-permute-done | bytes 524320 | tf_op jit(solution)/shard_map/ppermute | solution.py:578
  89.5 2.0 shard_map.138
  91.5 4.0 %collective-permute-done.20.refs_1_ = bf16[128,2048]{1,0:T(8,128)(2,1)S(1)} collective-permute-done((bf16[128,2048]{1,0:T(8,128)(2,1)S(1)}, bf16[128,2048]{1,0:T(8,128)(2,1)S(1)}, u32[]{:S(2)}, u32[]{:S(2)}) %collective-permute-start.20) | collective-permute-done | bytes 524320 | tf_op jit(solution)/shard_map/ppermute | solution.py:578
  100.7 3.5 %collective-permute-done.22.r2 = bf16[40,2176]{1,0:T(8,128)(2,1)S(1)} collective-permute-done((bf16[40,2176]{1,0:T(8,128)(2,1)S(1)}, bf16[40,2176]{1,0:T(8,128)(2,1)S(1)}, u32[]{:S(2)}, u32[]{:S(2)}) %collective-permute-start.22) | collective-permute-done | bytes 174112 | tf_op jit(solution)/shard_map/ppermute | solution.py:584
  104.2 2.8 %collective-permute-done.23.r3 = bf16[40,2176]{1,0:T(8,128)(2,1)S(1)} collective-permute-done((bf16[40,2176]{1,0:T(8,128)(2,1)S(1)}, bf16[40,2176]{1,0:T(8,128)(2,1)S(1)}, u32[]{:S(2)}, u32[]{:S(2)}) %collective-permute-start.23) | collective-permute-done | bytes 174112 | tf_op jit(solution)/shard_map/ppermute | solution.py:584
  112.2 2.3 %collective-permute-done.25.p2 = bf16[8,2048]{1,0:T(8,128)(2,1)S(1)} collective-permute-done((bf16[8,2048]{1,0:T(8,128)(2,1)S(1)}, bf16[8,2048]{1,0:T(8,128)(2,1)S(1)}, u32[]{:S(2)}, u32[]{:S(2)}) %collective-permute-start.25) | collective-permute-done | bytes 32800 | tf_op jit(solution)/shard_map/ppermute | solution.py:584
  118.1 2.6 %collective-permute-start.29 = (bf16[8,2048]{1,0:T(8,128)(2,1)S(1)}, bf16[8,2048]{1,0:T(8,128)(2,1)S(1)}, u32[]{:S(2)}, u32[]{:S(2)}) collective-permute-start(bf16[8,2048]{1,0:T(8,128)(2,1)S(1)} %shard_map.143.p0._), channel_id=1, source_target_pairs={{0,3},{1,2},{2,1},{3,0},{4,7},{5,6},{6,5},{7,4},{8,11},{9,10},{10,... | collective-permute-start | bytes 98312 | tf_op jit(solution)/shard_map/ppermute | solution.py:581
  121.8 2.0 %collective-permute-done.29.p3 = bf16[8,2048]{1,0:T(8,128)(2,1)S(1)} collective-permute-done((bf16[8,2048]{1,0:T(8,128)(2,1)S(1)}, bf16[8,2048]{1,0:T(8,128)(2,1)S(1)}, u32[]{:S(2)}, u32[]{:S(2)}) %collective-permute-start.29) | collective-permute-done | bytes 32800 | tf_op jit(solution)/shard_map/ppermute | solution.py:581
  126.4 2.3 %collective-permute-done.31.q2 = bf16[8,2048]{1,0:T(8,128)(2,1)S(1)} collective-permute-done((bf16[8,2048]{1,0:T(8,128)(2,1)S(1)}, bf16[8,2048]{1,0:T(8,128)(2,1)S(1)}, u32[]{:S(2)}, u32[]{:S(2)}) %collective-permute-start.31) | collective-permute-done | bytes 32800 | tf_op jit(solution)/shard_map/ppermute | solution.py:584
  128.9 2.3 %shard_map.145 = (f32[32,2048]{1,0:T(8,128)S(1)}, f32[32,768]{1,0:T(8,128)S(1)}, f32[1]{0:T(128)}) custom-call(s32[15]{0:T(128)S(1)} %concatenate.6.n, bf16[8,2048]{1,0:T(8,128)(2,1)S(1)} %shard_map.144.q0._, bf16[8,2048]{1,0:T(8,128)(2,1)S(1)} %collective-permute-done.30.q1, bf16[8,2048]{1,0:T(8,128)(2,1)S(1)} %collective-permute-done.31.q2, ...), custom_call_target="tpu_custom_call" | custom-call | flops 1 | bytes 1 | tf_op jit(solution)/shard_map/pallas_call | solution.py:524
  131.3 3.1 %shard_map.146 = (bf16[40,2048]{1,0:T(8,128)(2,1)S(1)}, bf16[40,2048]{1,0:T(8,128)(2,1)S(1)}, bf16[40,2048]{1,0:T(8,128)(2,1)S(1)}, bf16[40,2048]{1,0:T(8,128)(2,1)S(1)}) custom-call(s32[15]{0:T(128)S(1)} %concatenate.6.n, f32[4,160,768]{2,1,0:T(8,128)S(1)} %get-tuple-element.126.a_ref, f32[4,160,768]{2,1,0:T(8,128)S(1)} %get-tuple-element.127.b_ref, ...), custom_call_target="tpu_custom_call" | custom-call | flops 1 | bytes 1 | tf_op jit(solution)/shard_map/pallas_call | solution.py:524
  136.4 3.1 %shard_map.147 = (bf16[40,2048]{1,0:T(8,128)(2,1)S(1)}, bf16[40,2048]{1,0:T(8,128)(2,1)S(1)}, bf16[40,2048]{1,0:T(8,128)(2,1)S(1)}, bf16[40,2048]{1,0:T(8,128)(2,1)S(1)}) custom-call(s32[15]{0:T(128)S(1)} %concatenate.6.n, f32[4,160,768]{2,1,0:T(8,128)S(1)} %get-tuple-element.126.a_ref, f32[4,160,768]{2,1,0:T(8,128)S(1)} %get-tuple-element.127.b_ref, ...), custom_call_target="tpu_custom_call" | custom-call | flops 1 | bytes 1 | tf_op jit(solution)/shard_map/pallas_call | solution.py:524
  139.5 2.1 %collective-permute-done.37.r2 = bf16[40,2048]{1,0:T(8,128)(2,1)S(1)} collective-permute-done((bf16[40,2048]{1,0:T(8,128)(2,1)S(1)}, bf16[40,2048]{1,0:T(8,128)(2,1)S(1)}, u32[]{:S(2)}, u32[]{:S(2)}) %collective-permute-start.37) | collective-permute-done | bytes 163872 | tf_op jit(solution)/shard_map/ppermute | solution.py:584
  141.6 2.6 %collective-permute-done.38.r3 = bf16[40,2048]{1,0:T(8,128)(2,1)S(1)} collective-permute-done((bf16[40,2048]{1,0:T(8,128)(2,1)S(1)}, bf16[40,2048]{1,0:T(8,128)(2,1)S(1)}, u32[]{:S(2)}, u32[]{:S(2)}) %collective-permute-start.38) | collective-permute-done | bytes 163872 | tf_op jit(solution)/shard_map/ppermute | solution.py:584
  148.7 3.1 %shard_map.149 = (bf16[40,2048]{1,0:T(8,128)(2,1)S(1)}, bf16[40,2048]{1,0:T(8,128)(2,1)S(1)}, bf16[40,2048]{1,0:T(8,128)(2,1)S(1)}, bf16[40,2048]{1,0:T(8,128)(2,1)S(1)}) custom-call(s32[15]{0:T(128)S(1)} %concatenate.6.n, f32[4,160,768]{2,1,0:T(8,128)S(1)} %get-tuple-element.126.a_ref, f32[4,160,768]{2,1,0:T(8,128)S(1)} %get-tuple-element.127.b_ref, ...), custom_call_target="tpu_custom_call" | custom-call | flops 1 | bytes 1 | tf_op jit(solution)/shard_map/pallas_call | solution.py:524
  153.9 2.6 %collective-permute-done.35.r3 = bf16[40,2048]{1,0:T(8,128)(2,1)S(1)} collective-permute-done((bf16[40,2048]{1,0:T(8,128)(2,1)S(1)}, bf16[40,2048]{1,0:T(8,128)(2,1)S(1)}, u32[]{:S(2)}, u32[]{:S(2)}) %collective-permute-start.35) | collective-permute-done | bytes 163872 | tf_op jit(solution)/shard_map/ppermute | solution.py:584
  157.3 3.1 %shard_map.151 = (bf16[40,2048]{1,0:T(8,128)(2,1)S(1)}, bf16[40,2048]{1,0:T(8,128)(2,1)S(1)}, bf16[40,2048]{1,0:T(8,128)(2,1)S(1)}, bf16[40,2048]{1,0:T(8,128)(2,1)S(1)}) custom-call(s32[15]{0:T(128)S(1)} %concatenate.6.n, f32[4,160,768]{2,1,0:T(8,128)S(1)} %get-tuple-element.126.a_ref, f32[4,160,768]{2,1,0:T(8,128)S(1)} %get-tuple-element.127.b_ref, ...), custom_call_target="tpu_custom_call" | custom-call | flops 1 | bytes 1 | tf_op jit(solution)/shard_map/pallas_call | solution.py:524
  167.6 2.8 %collective-permute-start.48 = (bf16[128,2048]{1,0:T(8,128)(2,1)S(1)}, bf16[128,2048]{1,0:T(8,128)(2,1)S(1)}, u32[]{:S(2)}, u32[]{:S(2)}) collective-permute-start(bf16[128,2048]{1,0:T(8,128)(2,1)S(1)} %get-tuple-element.155), channel_id=1, source_target_pairs={{0,1},{3,2},{4,5},{7,6},{8,9},{11,10},{12,13},{15,14},{16,17},{19,... | collective-permute-start | bytes 1572872 | tf_op jit(solution)/shard_map/ppermute | solution.py:578
  170.4 2.6 %collective-permute-done.46.r2 = bf16[40,2048]{1,0:T(8,128)(2,1)S(1)} collective-permute-done((bf16[40,2048]{1,0:T(8,128)(2,1)S(1)}, bf16[40,2048]{1,0:T(8,128)(2,1)S(1)}, u32[]{:S(2)}, u32[]{:S(2)}) %collective-permute-start.46) | collective-permute-done | bytes 163872 | tf_op jit(solution)/shard_map/ppermute | solution.py:584
  173.1 2.1 %collective-permute-done.47.r3 = bf16[40,2048]{1,0:T(8,128)(2,1)S(1)} collective-permute-done((bf16[40,2048]{1,0:T(8,128)(2,1)S(1)}, bf16[40,2048]{1,0:T(8,128)(2,1)S(1)}, u32[]{:S(2)}, u32[]{:S(2)}) %collective-permute-start.47) | collective-permute-done | bytes 163872 | tf_op jit(solution)/shard_map/ppermute | solution.py:584
  181.2 3.8 %collective-permute-done.48.r4 = bf16[128,2048]{1,0:T(8,128)(2,1)S(1)} collective-permute-done((bf16[128,2048]{1,0:T(8,128)(2,1)S(1)}, bf16[128,2048]{1,0:T(8,128)(2,1)S(1)}, u32[]{:S(2)}, u32[]{:S(2)}) %collective-permute-start.48) | collective-permute-done | bytes 524320 | tf_op jit(solution)/shard_map/ppermute | solution.py:578
  185.0 11.3 %collective-permute-done.50.r6 = bf16[128,2048]{1,0:T(8,128)(2,1)S(1)} collective-permute-done((bf16[128,2048]{1,0:T(8,128)(2,1)S(1)}, bf16[128,2048]{1,0:T(8,128)(2,1)S(1)}, u32[]{:S(2)}, u32[]{:S(2)}) %collective-permute-start.50) | collective-permute-done | bytes 524320 | tf_op jit(solution)/shard_map/ppermute | solution.py:578
  196.2 2.0 %shard_map.158 = bf16[128,2048]{1,0:T(8,128)(2,1)} custom-call(s32[15]{0:T(128)S(1)} %concatenate.6.n, bf16[4,128,2048]{2,1,0:T(8,128)(2,1)S(1)} %get-tuple-element.118.t_ref, f32[1,2048]{1,0:T(1,128)S(1)} %bitcast.43, f32[128,2048]{1,0:T(8,128)S(1)} %get-tuple-element.153.dresid_ref._, f32[128,128]{1,0:T(8,128)S(1)} %get-tuple-element.154.scale_ref, ...), custom_call_target="tpu_custom_call" | custom-call | flops 1 | bytes 1 | tf_op jit(solution)/shard_map/pallas_call | solution.py:524
  (141 shorter events, 81.3 us)
Async XLA Ops:
  5.3 19.0 %collective-permute-start = (bf16[144,2048]{1,0:T(8,128)(2,1)}, bf16[144,2048]{1,0:T(8,128)(2,1)S(1)}, u32[]{:S(2)}, u32[]{:S(2)}) collective-permute-start(bf16[144,2048]{1,0:T(8,128)(2,1)} %shard_map.122.rest_0_.left_ref), channel_id=1, source_target_pairs={{0,1},{3,2},{4,5},{7,6},{8,9},{11,10},{12,13},{15,14},{16,17},{19,... | collective-permute-start | bytes 1769480 | tf_op jit(solution)/shard_map/ppermute | solution.py:578
  15.6 19.8 %collective-permute-start.2 = (bf16[128,2048]{1,0:T(8,128)(2,1)S(1)}, bf16[128,2048]{1,0:T(8,128)(2,1)S(1)}, u32[]{:S(2)}, u32[]{:S(2)}) collective-permute-start(bf16[128,2048]{1,0:T(8,128)(2,1)S(1)} %shard_map.123.rest_0_.left_ref), channel_id=1, source_target_pairs={{0,1},{3,2},{4,5},{7,6},{8,9},{11,10},{12,13},{15,14},{16,17},{19,... | collective-permute-start | bytes 1572872 | tf_op jit(solution)/shard_map/ppermute | solution.py:578
  24.9 20.1 %collective-permute-start.1 = (bf16[144,2048]{1,0:T(8,128)(2,1)S(1)}, bf16[144,2048]{1,0:T(8,128)(2,1)S(1)}, u32[]{:S(2)}, u32[]{:S(2)}) collective-permute-start(bf16[144,2048]{1,0:T(8,128)(2,1)S(1)} %shard_map.126._.left_ref), channel_id=1, source_target_pairs={{1,2},{2,1},{5,6},{6,5},{9,10},{10,9},{13,14},{14,13},{17,18},{18,... | collective-permute-start | bytes 1769480 | tf_op jit(solution)/shard_map/ppermute | solution.py:578
  25.6 21.5 %collective-permute-start.6 = (bf16[128,2048]{1,0:T(8,128)(2,1)S(1)}, bf16[128,2048]{1,0:T(8,128)(2,1)}, u32[]{:S(2)}, u32[]{:S(2)}) collective-permute-start(bf16[128,2048]{1,0:T(8,128)(2,1)S(1)} %shard_map.124.rest_0_.left_ref), channel_id=1, source_target_pairs={{0,1},{3,2},{4,5},{7,6},{8,9},{11,10},{12,13},{15,14},{16,17},{19,... | collective-permute-start | bytes 1572872 | tf_op jit(solution)/shard_map/ppermute | solution.py:578
  36.0 13.7 %collective-permute-start.5 = (bf16[128,2048]{1,0:T(8,128)(2,1)S(1)}, bf16[128,2048]{1,0:T(8,128)(2,1)}, u32[]{:S(2)}, u32[]{:S(2)}) collective-permute-start(bf16[128,2048]{1,0:T(8,128)(2,1)S(1)} %shard_map.127._.left_ref), channel_id=1, source_target_pairs={{1,2},{2,1},{5,6},{6,5},{9,10},{10,9},{13,14},{14,13},{17,18},{18,... | collective-permute-start | bytes 1572872 | tf_op jit(solution)/shard_map/ppermute | solution.py:578
  37.5 19.2 %collective-permute-start.4 = (bf16[128,2048]{1,0:T(8,128)(2,1)S(1)}, bf16[128,2048]{1,0:T(8,128)(2,1)}, u32[]{:S(2)}, u32[]{:S(2)}) collective-permute-start(bf16[128,2048]{1,0:T(8,128)(2,1)S(1)} %shard_map.125._.left_ref), channel_id=1, source_target_pairs={{0,1},{3,2},{4,5},{7,6},{8,9},{11,10},{12,13},{15,14},{16,17},{19,... | collective-permute-start | bytes 1572872 | tf_op jit(solution)/shard_map/ppermute | solution.py:578
  45.7 18.2 %collective-permute-start.3 = (bf16[144,2048]{1,0:T(8,128)(2,1)S(1)}, bf16[144,2048]{1,0:T(8,128)(2,1)S(1)}, u32[]{:S(2)}, u32[]{:S(2)}) collective-permute-start(bf16[144,2048]{1,0:T(8,128)(2,1)S(1)} %shard_map.128._.refs_0_), channel_id=1, source_target_pairs={{1,0},{2,3},{5,4},{6,7},{9,8},{10,11},{13,12},{14,15},{17,16},{18,... | collective-permute-start | bytes 1769480 | tf_op jit(solution)/shard_map/ppermute | solution.py:578
  48.8 18.0 %collective-permute-start.11 = (bf16[128,2048]{1,0:T(8,128)(2,1)S(1)}, bf16[128,2048]{1,0:T(8,128)(2,1)S(1)}, u32[]{:S(2)}, u32[]{:S(2)}) collective-permute-start(bf16[128,2048]{1,0:T(8,128)(2,1)S(1)} %shard_map.129._.left_ref), channel_id=1, source_target_pairs={{1,2},{2,1},{5,6},{6,5},{9,10},{10,9},{13,14},{14,13},{17,18},{18,... | collective-permute-start | bytes 1572872 | tf_op jit(solution)/shard_map/ppermute | solution.py:578
  51.4 20.0 %collective-permute-start.10 = (bf16[128,2048]{1,0:T(8,128)(2,1)S(1)}, bf16[128,2048]{1,0:T(8,128)(2,1)S(1)}, u32[]{:S(2)}, u32[]{:S(2)}) collective-permute-start(bf16[128,2048]{1,0:T(8,128)(2,1)S(1)} %shard_map.130._.refs_0_), channel_id=1, source_target_pairs={{1,0},{2,3},{5,4},{6,7},{9,8},{10,11},{13,12},{14,15},{17,16},{18,... | collective-permute-start | bytes 1572872 | tf_op jit(solution)/shard_map/ppermute | solution.py:578
  58.4 19.0 %collective-permute-start.16 = (bf16[128,2048]{1,0:T(8,128)(2,1)S(1)}, bf16[128,2048]{1,0:T(8,128)(2,1)S(1)}, u32[]{:S(2)}, u32[]{:S(2)}) collective-permute-start(bf16[128,2048]{1,0:T(8,128)(2,1)S(1)} %shard_map.131.refs_5_.left_ref), channel_id=1, source_target_pairs={{1,2},{2,1},{5,6},{6,5},{9,10},{10,9},{13,14},{14,13},{17,18},{18,... | collective-permute-start | bytes 1572872 | tf_op jit(solution)/shard_map/ppermute | solution.py:578
  65.2 8.8 %collective-permute-start.7 = (bf16[40,2176]{1,0:T(8,128)(2,1)S(1)}, bf16[40,2176]{1,0:T(8,128)(2,1)S(1)}, u32[]{:S(2)}, u32[]{:S(2)}) collective-permute-start(bf16[40,2176]{1,0:T(8,128)(2,1)S(1)} %get-tuple-element.80), channel_id=1, source_target_pairs={{0,4},{4,0},{8,12},{12,8},{1,5},{5,1},{9,13},{13,9},{2,6},{6,2},{1... | collective-permute-start | bytes 522248 | tf_op jit(solution)/shard_map/ppermute | solution.py:584
  65.3 8.7 %collective-permute-start.8 = (bf16[40,2176]{1,0:T(8,128)(2,1)S(1)}, bf16[40,2176]{1,0:T(8,128)(2,1)S(1)}, u32[]{:S(2)}, u32[]{:S(2)}) collective-permute-start(bf16[40,2176]{1,0:T(8,128)(2,1)S(1)} %get-tuple-element.81), channel_id=1, source_target_pairs={{0,8},{4,12},{8,0},{12,4},{1,9},{5,13},{9,1},{13,5},{2,10},{6,14},... | collective-permute-start | bytes 522248 | tf_op jit(solution)/shard_map/ppermute | solution.py:584
  66.9 8.6 %collective-permute-start.9 = (bf16[40,2176]{1,0:T(8,128)(2,1)S(1)}, bf16[40,2176]{1,0:T(8,128)(2,1)S(1)}, u32[]{:S(2)}, u32[]{:S(2)}) collective-permute-start(bf16[40,2176]{1,0:T(8,128)(2,1)S(1)} %get-tuple-element.82), channel_id=1, source_target_pairs={{0,12},{4,8},{8,4},{12,0},{1,13},{5,9},{9,5},{13,1},{2,14},{6,10},... | collective-permute-start | bytes 522248 | tf_op jit(solution)/shard_map/ppermute | solution.py:584
  71.3 14.2 %collective-permute-start.15 = (bf16[128,2048]{1,0:T(8,128)(2,1)S(1)}, bf16[128,2048]{1,0:T(8,128)(2,1)S(1)}, u32[]{:S(2)}, u32[]{:S(2)}) collective-permute-start(bf16[128,2048]{1,0:T(8,128)(2,1)S(1)} %shard_map.133.refs_8_.refs_0_), channel_id=1, source_target_pairs={{1,0},{2,3},{5,4},{6,7},{9,8},{10,11},{13,12},{14,15},{17,16},{18,... | collective-permute-start | bytes 1572872 | tf_op jit(solution)/shard_map/ppermute | solution.py:578
  78.1 17.4 %collective-permute-start.20 = (bf16[128,2048]{1,0:T(8,128)(2,1)S(1)}, bf16[128,2048]{1,0:T(8,128)(2,1)S(1)}, u32[]{:S(2)}, u32[]{:S(2)}) collective-permute-start(bf16[128,2048]{1,0:T(8,128)(2,1)S(1)} %shard_map.136.refs_8_.refs_0_), channel_id=1, source_target_pairs={{1,0},{2,3},{5,4},{6,7},{9,8},{10,11},{13,12},{14,15},{17,16},{18,... | collective-permute-start | bytes 1572872 | tf_op jit(solution)/shard_map/ppermute | solution.py:578
  79.9 8.6 %collective-permute-start.13 = (bf16[40,2176]{1,0:T(8,128)(2,1)S(1)}, bf16[40,2176]{1,0:T(8,128)(2,1)S(1)}, u32[]{:S(2)}, u32[]{:S(2)}) collective-permute-start(bf16[40,2176]{1,0:T(8,128)(2,1)S(1)} %get-tuple-element.89), channel_id=1, source_target_pairs={{0,8},{4,12},{8,0},{12,4},{1,9},{5,13},{9,1},{13,5},{2,10},{6,14},... | collective-permute-start | bytes 522248 | tf_op jit(solution)/shard_map/ppermute | solution.py:584
  81.4 8.1 %collective-permute-start.14 = (bf16[40,2176]{1,0:T(8,128)(2,1)S(1)}, bf16[40,2176]{1,0:T(8,128)(2,1)S(1)}, u32[]{:S(2)}, u32[]{:S(2)}) collective-permute-start(bf16[40,2176]{1,0:T(8,128)(2,1)S(1)} %get-tuple-element.90), channel_id=1, source_target_pairs={{0,12},{4,8},{8,4},{12,0},{1,13},{5,9},{9,5},{13,1},{2,14},{6,10},... | collective-permute-start | bytes 522248 | tf_op jit(solution)/shard_map/ppermute | solution.py:584
  86.9 11.6 %collective-permute-start.17 = (bf16[40,2176]{1,0:T(8,128)(2,1)S(1)}, bf16[40,2176]{1,0:T(8,128)(2,1)S(1)}, u32[]{:S(2)}, u32[]{:S(2)}) collective-permute-start(bf16[40,2176]{1,0:T(8,128)(2,1)S(1)} %get-tuple-element.99), channel_id=1, source_target_pairs={{0,4},{4,0},{8,12},{12,8},{1,5},{5,1},{9,13},{13,9},{2,6},{6,2},{1... | collective-permute-start | bytes 522248 | tf_op jit(solution)/shard_map/ppermute | solution.py:584
  87.0 11.8 %collective-permute-start.18 = (bf16[40,2176]{1,0:T(8,128)(2,1)S(1)}, bf16[40,2176]{1,0:T(8,128)(2,1)S(1)}, u32[]{:S(2)}, u32[]{:S(2)}) collective-permute-start(bf16[40,2176]{1,0:T(8,128)(2,1)S(1)} %get-tuple-element.100), channel_id=1, source_target_pairs={{0,8},{4,12},{8,0},{12,4},{1,9},{5,13},{9,1},{13,5},{2,10},{6,14},... | collective-permute-start | bytes 522248 | tf_op jit(solution)/shard_map/ppermute | solution.py:584
  88.5 10.2 %collective-permute-start.19 = (bf16[40,2176]{1,0:T(8,128)(2,1)S(1)}, bf16[40,2176]{1,0:T(8,128)(2,1)S(1)}, u32[]{:S(2)}, u32[]{:S(2)}) collective-permute-start(bf16[40,2176]{1,0:T(8,128)(2,1)S(1)} %get-tuple-element.101), channel_id=1, source_target_pairs={{0,12},{4,8},{8,4},{12,0},{1,13},{5,9},{9,5},{13,1},{2,14},{6,10},... | collective-permute-start | bytes 522248 | tf_op jit(solution)/shard_map/ppermute | solution.py:584
  98.5 8.6 %collective-permute-start.23 = (bf16[40,2176]{1,0:T(8,128)(2,1)S(1)}, bf16[40,2176]{1,0:T(8,128)(2,1)S(1)}, u32[]{:S(2)}, u32[]{:S(2)}) collective-permute-start(bf16[40,2176]{1,0:T(8,128)(2,1)S(1)} %get-tuple-element.112), channel_id=1, source_target_pairs={{0,12},{4,8},{8,4},{12,0},{1,13},{5,9},{9,5},{13,1},{2,14},{6,10},... | collective-permute-start | bytes 522248 | tf_op jit(solution)/shard_map/ppermute | solution.py:584
  135.6 8.5 %collective-permute-start.38 = (bf16[40,2048]{1,0:T(8,128)(2,1)S(1)}, bf16[40,2048]{1,0:T(8,128)(2,1)S(1)}, u32[]{:S(2)}, u32[]{:S(2)}) collective-permute-start(bf16[40,2048]{1,0:T(8,128)(2,1)S(1)} %get-tuple-element.138), channel_id=1, source_target_pairs={{0,12},{4,8},{8,4},{12,0},{1,13},{5,9},{9,5},{13,1},{2,14},{6,10},... | collective-permute-start | bytes 491528 | tf_op jit(solution)/shard_map/ppermute | solution.py:584
  145.0 19.4 %collective-permute-start.39 = (bf16[128,2048]{1,0:T(8,128)(2,1)S(1)}, bf16[128,2048]{1,0:T(8,128)(2,1)S(1)}, u32[]{:S(2)}, u32[]{:S(2)}) collective-permute-start(bf16[128,2048]{1,0:T(8,128)(2,1)S(1)} %get-tuple-element.142), channel_id=1, source_target_pairs={{0,1},{3,2},{4,5},{7,6},{8,9},{11,10},{12,13},{15,14},{16,17},{19,... | collective-permute-start | bytes 1572872 | tf_op jit(solution)/shard_map/ppermute | solution.py:578
  147.8 8.6 %collective-permute-start.35 = (bf16[40,2048]{1,0:T(8,128)(2,1)S(1)}, bf16[40,2048]{1,0:T(8,128)(2,1)S(1)}, u32[]{:S(2)}, u32[]{:S(2)}) collective-permute-start(bf16[40,2048]{1,0:T(8,128)(2,1)S(1)} %get-tuple-element.135), channel_id=1, source_target_pairs={{0,12},{4,8},{8,4},{12,0},{1,13},{5,9},{9,5},{13,1},{2,14},{6,10},... | collective-permute-start | bytes 491528 | tf_op jit(solution)/shard_map/ppermute | solution.py:584
  151.8 10.0 %collective-permute-start.40 = (bf16[40,2048]{1,0:T(8,128)(2,1)S(1)}, bf16[40,2048]{1,0:T(8,128)(2,1)S(1)}, u32[]{:S(2)}, u32[]{:S(2)}) collective-permute-start(bf16[40,2048]{1,0:T(8,128)(2,1)S(1)} %get-tuple-element.143), channel_id=1, source_target_pairs={{0,4},{4,0},{8,12},{12,8},{1,5},{5,1},{9,13},{13,9},{2,6},{6,2},{1... | collective-permute-start | bytes 491528 | tf_op jit(solution)/shard_map/ppermute | solution.py:584
  152.2 9.5 %collective-permute-start.41 = (bf16[40,2048]{1,0:T(8,128)(2,1)S(1)}, bf16[40,2048]{1,0:T(8,128)(2,1)S(1)}, u32[]{:S(2)}, u32[]{:S(2)}) collective-permute-start(bf16[40,2048]{1,0:T(8,128)(2,1)S(1)} %get-tuple-element.144), channel_id=1, source_target_pairs={{0,8},{4,12},{8,0},{12,4},{1,9},{5,13},{9,1},{13,5},{2,10},{6,14},... | collective-permute-start | bytes 491528 | tf_op jit(solution)/shard_map/ppermute | solution.py:584
  153.9 9.6 %collective-permute-start.42 = (bf16[40,2048]{1,0:T(8,128)(2,1)S(1)}, bf16[40,2048]{1,0:T(8,128)(2,1)S(1)}, u32[]{:S(2)}, u32[]{:S(2)}) collective-permute-start(bf16[40,2048]{1,0:T(8,128)(2,1)S(1)} %get-tuple-element.145), channel_id=1, source_target_pairs={{0,12},{4,8},{8,4},{12,0},{1,13},{5,9},{9,5},{13,1},{2,14},{6,10},... | collective-permute-start | bytes 491528 | tf_op jit(solution)/shard_map/ppermute | solution.py:584
  160.4 16.4 %collective-permute-start.44 = (bf16[128,2048]{1,0:T(8,128)(2,1)S(1)}, bf16[128,2048]{1,0:T(8,128)(2,1)S(1)}, u32[]{:S(2)}, u32[]{:S(2)}) collective-permute-start(bf16[128,2048]{1,0:T(8,128)(2,1)S(1)} %get-tuple-element.148), channel_id=1, source_target_pairs={{0,1},{3,2},{4,5},{7,6},{8,9},{11,10},{12,13},{15,14},{16,17},{19,... | collective-permute-start | bytes 1572872 | tf_op jit(solution)/shard_map/ppermute | solution.py:578
  165.0 13.2 %collective-permute-start.43 = (bf16[128,2048]{1,0:T(8,128)(2,1)S(1)}, bf16[128,2048]{1,0:T(8,128)(2,1)S(1)}, u32[]{:S(2)}, u32[]{:S(2)}) collective-permute-start(bf16[128,2048]{1,0:T(8,128)(2,1)S(1)} %shard_map.153._), channel_id=1, source_target_pairs={{1,2},{2,1},{5,6},{6,5},{9,10},{10,9},{13,14},{14,13},{17,18},{18,... | collective-permute-start | bytes 1572872 | tf_op jit(solution)/shard_map/ppermute | solution.py:578
  166.9 8.3 %collective-permute-start.47 = (bf16[40,2048]{1,0:T(8,128)(2,1)S(1)}, bf16[40,2048]{1,0:T(8,128)(2,1)S(1)}, u32[]{:S(2)}, u32[]{:S(2)}) collective-permute-start(bf16[40,2048]{1,0:T(8,128)(2,1)S(1)} %get-tuple-element.151), channel_id=1, source_target_pairs={{0,12},{4,8},{8,4},{12,0},{1,13},{5,9},{9,5},{13,1},{2,14},{6,10},... | collective-permute-start | bytes 491528 | tf_op jit(solution)/shard_map/ppermute | solution.py:584
  167.6 17.4 %collective-permute-start.48 = (bf16[128,2048]{1,0:T(8,128)(2,1)S(1)}, bf16[128,2048]{1,0:T(8,128)(2,1)S(1)}, u32[]{:S(2)}, u32[]{:S(2)}) collective-permute-start(bf16[128,2048]{1,0:T(8,128)(2,1)S(1)} %get-tuple-element.155), channel_id=1, source_target_pairs={{0,1},{3,2},{4,5},{7,6},{8,9},{11,10},{12,13},{15,14},{16,17},{19,... | collective-permute-start | bytes 1572872 | tf_op jit(solution)/shard_map/ppermute | solution.py:578
  178.8 17.5 %collective-permute-start.50 = (bf16[128,2048]{1,0:T(8,128)(2,1)S(1)}, bf16[128,2048]{1,0:T(8,128)(2,1)S(1)}, u32[]{:S(2)}, u32[]{:S(2)}) collective-permute-start(bf16[128,2048]{1,0:T(8,128)(2,1)S(1)} %shard_map.156._), channel_id=1, source_target_pairs={{1,0},{2,3},{5,4},{6,7},{9,8},{10,11},{13,12},{14,15},{17,16},{18,... | collective-permute-start | bytes 1572872 | tf_op jit(solution)/shard_map/ppermute | solution.py:578
  (30 other events, 200.8 us)

commit v6 on v5

--- a/solution.py
+++ b/solution.py
@@ -211,10 +211,10 @@
 LEAVES_OUT = ((1, 0), (2, 3))
 PIECES = (1, 1, 1, 1)
 FORWARD_ORDER = (
-    "p0", "p1", "p2", "p3", "s0", "s1", "t0", "s2", "t1", "s3", "d0", "t2", "d1", "x0", "t3", "d2", "x1", "d3", "x2", "x3",
+    "p0", "p1", "p2", "p3", "s0", "s1", "t0", "s2", "t1", "s3", "t2", "d0", "d1", "x0", "t3", "d2", "x1", "d3", "x2", "x3",
 )
 BACKWARD_ORDER = (
-    "b0", "b1", "c0", "b2", "c1", "b3", "c2", "i0", "c3", "i1", "l0",
+    "b0", "b1", "b2", "c0", "b3", "c1", "c2", "i0", "c3", "i1", "l0",
 )
 VMEM_LIMIT = 24 * 2**20
 FIRST_LIMIT = 54 * 2**20
@@ -470,12 +470,16 @@
         dlog_ref[...] = (moved * (jnp.where(lane == n[OWN_EXPERT], 1.0, 0.0) - gates)).astype(BF16)
 
     total = (
-        contract_last(dgate_ref[...], gate_ref[...])
-        + contract_last(dup_ref[...], up_ref[...])
+        dot_nn(dgate_ref[...], gate_ref[...])
+        + dot_nn(dup_ref[...], up_ref[...])
         + dot_nn(dlog_ref[...], router_ref[...])
     )
     for way, out in enumerate((o0, o1, o2, o3)):
         out[...] = total[way * capacity : (way + 1) * capacity].astype(BF16)
+
+
+def turn_kernel(n, weight_ref, _, out_ref):
+    out_ref[...] = jnp.transpose(weight_ref[...])
 
 
 def combine_kernel(n, place_ref, r0, r1, r2, r3, _, out_ref, narrow_ref):
@@ -703,6 +707,12 @@
         pools[c] = result[0]
         kept_acts.update({i: result[i] for i in (1, 2, 3, 4)})
 
+    turned = [None, None]
+
+    def turn(k):
+        size = (hidden_width, width)
+        (turned[k],) = chain(turn_kernel, [whole((gate_w, up_w)[k])], [(shape(size, BF16), fixed(size))])
+
     calls = {"p": first_hop, "s": second_hop, "t": third_hop, "d": dispatch, "x": expert}
     for step in FORWARD_ORDER:
         calls[step[0]](int(step[1:]))
@@ -723,8 +733,12 @@
     def add_four(values):
         return chain(sum_kernel, [whole(v) for v in values], [(shape(seq_size, BF16), fixed(seq_size))])[0]
 
-    mine = add_four([quarters[0]] + [swap_e(quarters[way], way) for way in (1, 2, 3)])
-    mine = add_four([mine] + [swap_z(mine, way) for way in (1, 2, 3)])
+    parts_e = [quarters[0]] + [swap_e(quarters[way], way) for way in (1, 2, 3)]
+    turn(0)
+    mine = add_four(parts_e)
+    parts_z = [mine] + [swap_z(mine, way) for way in (1, 2, 3)]
+    turn(1)
+    mine = add_four(parts_z)
     gathered = [mine] + [swap_e(mine, way) for way in (1, 2, 3)]
     sizes = ((sequences, width), (sequences, hidden_width))
     dembedded, hidden_grad, loss = chain(
@@ -740,7 +754,6 @@
     def backward(k):
         tile = width
         block = lambda size: pl.BlockSpec((1, slots, size), lambda j, n: (n[ORDER + k], 0, 0))
-        weight_spec = pl.BlockSpec(memory_space=pltpu.VMEM)
         grads = chain(
             functools.partial(backward_kernel, capacity),
             [
@@ -749,8 +762,8 @@
                 (hidden_all, block(hidden_width)),
                 (info_all, block(ROW_EXTRA)),
                 whole(hidden_grad),
-                (gate_w, weight_spec),
-                (up_w, weight_spec),
+                whole(turned[0]),
+                whole(turned[1]),
                 (router_rows, pl.BlockSpec((ROW_EXTRA, tile), lambda j, n: (0, j))),
             ],
             [(shape((capacity, width), BF16), pl.BlockSpec((capacity, tile), lambda j, n: (0, j)))] * 4,

time: 199 us -> 198 us (level)
    ppermute x30, waiting for transfers between devices: 28.7 us -> 31.9 us  [swap_e(): return lax.ppermute(value, 'expert', [(i, i ^ bits) for i in range(4)])]
    ppermute x18, waiting for transfers between devices: 41.8 us -> 39.1 us  [along_z(): return lax.ppermute(value, 'tensor', pairs)]
    pallas_call x36 -> x38, Pallas kernels: 51.9 us -> 51.3 us  [__call__(): pl.pallas_call(kernel, out_shape=list(shapes), grid_spec=pltpu.PrefetchSc...]
  transfers between devices with their start and end apart: 51 -> 51, of which waited for: 26 -> 28; matrix products, arithmetic and copies ran while one was open for 1% -> 1% of each run, Pallas kernels for 20% -> 20%
where the time goes in v6:
time: 198 us; the launch traced here: 197 us
  waiting for transfers between devices  72.2 us (36%)
  starting transfers between devices  63.2 us (32%)
  Pallas kernels  55.9 us (28%)
  local copies, waits for them, and re-layouts  4.18 us (2%)
    pallas_call x38, Pallas kernels, __call__(): pl.pallas_call(kernel, out_shape=list(shapes), grid_spec=pltpu.PrefetchSc...  51.3 us
    ppermute x18, starting transfers between devices, along_z(): return lax.ppermute(value, 'tensor', pairs)  40.8 us
    ppermute x18, waiting for transfers between devices, along_z(): return lax.ppermute(value, 'tensor', pairs)  39.1 us
    ppermute x30, waiting for transfers between devices, swap_e(): return lax.ppermute(value, 'expert', [(i, i ^ bits) for i in range(4)])  31.9 us
    ppermute x30, starting transfers between devices, swap_e(): return lax.ppermute(value, 'expert', [(i, i ^ bits) for i in range(4)])  17.9 us
    pallas_call x1, Pallas kernels, first_hop(): pl.pallas_call(functools.partial(first_kernel, experts), out_shape=shape(...  4.6 us
    ppermute x3, starting transfers between devices, swap_z(): return lax.ppermute(value, 'tensor', [(i, i ^ bits) for i in range(4)])  4.45 us
  transfers between devices with their start and end apart: 51, of which 28 were waited for; matrix products, arithmetic and copies ran while one was open for 1% of the time, Pallas kernels for 20%

profile of v6, /device:TPU:0, one launch (start us, length us, event | category | flops | bytes accessed | tf_op | source)
XLA Modules:
  0.0 197.1 jit_solution(10195057649301806268)
XLA Ops:
  0.6 4.6 %shard_map.122.rest_0_.left_ref = bf16[144,2048]{1,0:T(8,128)(2,1)} custom-call(s32[4,128]{1,0:T(4,128)} %bitcast.40, bf16[512,1024]{1,0:T(8,128)(2,1)} %context_ref.5, bf16[1024,2048]{1,0:T(8,128)(2,1)} %weight_ref.5, bf16[128,2048]{1,0:T(8,128)(2,1)} %resid_ref.5), custom_call_target="tpu_custom_call" | custom-call | tf_op jit(solution)/shard_map/pallas_call | solution.py:622
  5.3 5.0 %collective-permute-start = (bf16[144,2048]{1,0:T(8,128)(2,1)}, bf16[144,2048]{1,0:T(8,128)(2,1)S(1)}, u32[]{:S(2)}, u32[]{:S(2)}) collective-permute-start(bf16[144,2048]{1,0:T(8,128)(2,1)} %shard_map.122.rest_0_.left_ref), channel_id=1, source_target_pairs={{0,1},{3,2},{4,5},{7,6},{8,9},{11,10},{12,13},{15,14},{16,17},{19,... | collective-permute-start | bytes 1769480 | tf_op jit(solution)/shard_map/ppermute | solution.py:582
  11.0 2.2 %copy-done.2 = bf16[1024,2048]{1,0:T(8,128)(2,1)S(1)} copy-done((bf16[1024,2048]{1,0:T(8,128)(2,1)S(1)}, bf16[1024,2048]{1,0:T(8,128)(2,1)}, u32[]{:S(2)}) %copy-start.2) | copy-done | bytes 4194328
  19.5 4.7 %collective-permute-done.right_ref = bf16[144,2048]{1,0:T(8,128)(2,1)S(1)} collective-permute-done((bf16[144,2048]{1,0:T(8,128)(2,1)}, bf16[144,2048]{1,0:T(8,128)(2,1)S(1)}, u32[]{:S(2)}, u32[]{:S(2)}) %collective-permute-start) | collective-permute-done | bytes 589856 | tf_op jit(solution)/shard_map/ppermute | solution.py:582
  25.6 7.9 %collective-permute-start.4 = (bf16[128,2048]{1,0:T(8,128)(2,1)S(1)}, bf16[128,2048]{1,0:T(8,128)(2,1)}, u32[]{:S(2)}, u32[]{:S(2)}) collective-permute-start(bf16[128,2048]{1,0:T(8,128)(2,1)S(1)} %shard_map.124.rest_0_.left_ref), channel_id=1, source_target_pairs={{0,1},{3,2},{4,5},{7,6},{8,9},{11,10},{12,13},{15,14},{16,17},{19,... | collective-permute-start | bytes 1572872 | tf_op jit(solution)/shard_map/ppermute | solution.py:582
  37.5 7.2 %collective-permute-start.6 = (bf16[128,2048]{1,0:T(8,128)(2,1)S(1)}, bf16[128,2048]{1,0:T(8,128)(2,1)}, u32[]{:S(2)}, u32[]{:S(2)}) collective-permute-start(bf16[128,2048]{1,0:T(8,128)(2,1)S(1)} %shard_map.125._.left_ref), channel_id=1, source_target_pairs={{0,1},{3,2},{4,5},{7,6},{8,9},{11,10},{12,13},{15,14},{16,17},{19,... | collective-permute-start | bytes 1572872 | tf_op jit(solution)/shard_map/ppermute | solution.py:582
  52.6 4.1 %collective-permute-done.6.right_ref = bf16[128,2048]{1,0:T(8,128)(2,1)} collective-permute-done((bf16[128,2048]{1,0:T(8,128)(2,1)S(1)}, bf16[128,2048]{1,0:T(8,128)(2,1)}, u32[]{:S(2)}, u32[]{:S(2)}) %collective-permute-start.6) | collective-permute-done | bytes 524320 | tf_op jit(solution)/shard_map/ppermute | solution.py:582
  59.8 4.0 %collective-permute-done.3.refs_1_ = bf16[144,2048]{1,0:T(8,128)(2,1)S(1)} collective-permute-done((bf16[144,2048]{1,0:T(8,128)(2,1)S(1)}, bf16[144,2048]{1,0:T(8,128)(2,1)S(1)}, u32[]{:S(2)}, u32[]{:S(2)}) %collective-permute-start.3) | collective-permute-done | bytes 589856 | tf_op jit(solution)/shard_map/ppermute | solution.py:582
  67.2 4.1 %collective-permute-done.11.refs_1_ = bf16[128,2048]{1,0:T(8,128)(2,1)S(1)} collective-permute-done((bf16[128,2048]{1,0:T(8,128)(2,1)S(1)}, bf16[128,2048]{1,0:T(8,128)(2,1)S(1)}, u32[]{:S(2)}, u32[]{:S(2)}) %collective-permute-start.11) | collective-permute-done | bytes 524320 | tf_op jit(solution)/shard_map/ppermute | solution.py:582
  75.4 2.0 shard_map.135
  81.5 2.4 %collective-permute-done.15.refs_1_ = bf16[128,2048]{1,0:T(8,128)(2,1)S(1)} collective-permute-done((bf16[128,2048]{1,0:T(8,128)(2,1)S(1)}, bf16[128,2048]{1,0:T(8,128)(2,1)S(1)}, u32[]{:S(2)}, u32[]{:S(2)}) %collective-permute-start.15) | collective-permute-done | bytes 524320 | tf_op jit(solution)/shard_map/ppermute | solution.py:582
  87.2 2.7 %collective-permute-done.14.r3 = bf16[40,2176]{1,0:T(8,128)(2,1)S(1)} collective-permute-done((bf16[40,2176]{1,0:T(8,128)(2,1)S(1)}, bf16[40,2176]{1,0:T(8,128)(2,1)S(1)}, u32[]{:S(2)}, u32[]{:S(2)}) %collective-permute-start.14) | collective-permute-done | bytes 174112 | tf_op jit(solution)/shard_map/ppermute | solution.py:588
  89.9 2.0 shard_map.138
  91.8 2.8 %collective-permute-done.20.refs_1_ = bf16[128,2048]{1,0:T(8,128)(2,1)S(1)} collective-permute-done((bf16[128,2048]{1,0:T(8,128)(2,1)S(1)}, bf16[128,2048]{1,0:T(8,128)(2,1)S(1)}, u32[]{:S(2)}, u32[]{:S(2)}) %collective-permute-start.20) | collective-permute-done | bytes 524320 | tf_op jit(solution)/shard_map/ppermute | solution.py:582
  99.9 3.5 %collective-permute-done.22.r2 = bf16[40,2176]{1,0:T(8,128)(2,1)S(1)} collective-permute-done((bf16[40,2176]{1,0:T(8,128)(2,1)S(1)}, bf16[40,2176]{1,0:T(8,128)(2,1)S(1)}, u32[]{:S(2)}, u32[]{:S(2)}) %collective-permute-start.22) | collective-permute-done | bytes 174112 | tf_op jit(solution)/shard_map/ppermute | solution.py:588
  103.3 2.8 %collective-permute-done.23.r3 = bf16[40,2176]{1,0:T(8,128)(2,1)S(1)} collective-permute-done((bf16[40,2176]{1,0:T(8,128)(2,1)S(1)}, bf16[40,2176]{1,0:T(8,128)(2,1)S(1)}, u32[]{:S(2)}, u32[]{:S(2)}) %collective-permute-start.23) | collective-permute-done | bytes 174112 | tf_op jit(solution)/shard_map/ppermute | solution.py:588
  115.4 2.1 %collective-permute-start.29 = (bf16[8,2048]{1,0:T(8,128)(2,1)S(1)}, bf16[8,2048]{1,0:T(8,128)(2,1)S(1)}, u32[]{:S(2)}, u32[]{:S(2)}) collective-permute-start(bf16[8,2048]{1,0:T(8,128)(2,1)S(1)} %shard_map.144._.p0), channel_id=1, source_target_pairs={{0,3},{1,2},{2,1},{3,0},{4,7},{5,6},{6,5},{7,4},{8,11},{9,10},{10,... | collective-permute-start | bytes 98312 | tf_op jit(solution)/shard_map/ppermute | solution.py:585
  127.3 2.3 %shard_map.147 = (f32[32,2048]{1,0:T(8,128)S(1)}, f32[32,768]{1,0:T(8,128)S(1)}, f32[1]{0:T(128)}) custom-call(s32[15]{0:T(128)S(1)} %concatenate.6.n, bf16[8,2048]{1,0:T(8,128)(2,1)S(1)} %shard_map.146.q0._, bf16[8,2048]{1,0:T(8,128)(2,1)S(1)} %collective-permute-done.30.q1, bf16[8,2048]{1,0:T(8,128)(2,1)S(1)} %collective-permute-done.31.q2, ...), custom_call_target="tpu_custom_call" | custom-call | flops 1 | bytes 1 | tf_op jit(solution)/shard_map/pallas_call | solution.py:528
  129.6 2.2 %shard_map.148 = (bf16[40,2048]{1,0:T(8,128)(2,1)S(1)}, bf16[40,2048]{1,0:T(8,128)(2,1)S(1)}, bf16[40,2048]{1,0:T(8,128)(2,1)S(1)}, bf16[40,2048]{1,0:T(8,128)(2,1)S(1)}) custom-call(s32[15]{0:T(128)S(1)} %concatenate.6.n, f32[4,160,768]{2,1,0:T(8,128)S(1)} %get-tuple-element.126.a_ref, f32[4,160,768]{2,1,0:T(8,128)S(1)} %get-tuple-element.127.b_ref, ...), custom_call_target="tpu_custom_call" | custom-call | flops 1 | bytes 1 | tf_op jit(solution)/shard_map/pallas_call | solution.py:528
  133.8 2.4 %shard_map.149 = (bf16[40,2048]{1,0:T(8,128)(2,1)S(1)}, bf16[40,2048]{1,0:T(8,128)(2,1)S(1)}, bf16[40,2048]{1,0:T(8,128)(2,1)S(1)}, bf16[40,2048]{1,0:T(8,128)(2,1)S(1)}) custom-call(s32[15]{0:T(128)S(1)} %concatenate.6.n, f32[4,160,768]{2,1,0:T(8,128)S(1)} %get-tuple-element.126.a_ref, f32[4,160,768]{2,1,0:T(8,128)S(1)} %get-tuple-element.127.b_ref, ...), custom_call_target="tpu_custom_call" | custom-call | flops 1 | bytes 1 | tf_op jit(solution)/shard_map/pallas_call | solution.py:528
  136.2 2.2 %shard_map.150 = (bf16[40,2048]{1,0:T(8,128)(2,1)S(1)}, bf16[40,2048]{1,0:T(8,128)(2,1)S(1)}, bf16[40,2048]{1,0:T(8,128)(2,1)S(1)}, bf16[40,2048]{1,0:T(8,128)(2,1)S(1)}) custom-call(s32[15]{0:T(128)S(1)} %concatenate.6.n, f32[4,160,768]{2,1,0:T(8,128)S(1)} %get-tuple-element.126.a_ref, f32[4,160,768]{2,1,0:T(8,128)S(1)} %get-tuple-element.127.b_ref, ...), custom_call_target="tpu_custom_call" | custom-call | flops 1 | bytes 1 | tf_op jit(solution)/shard_map/pallas_call | solution.py:528
  139.0 2.6 %collective-permute-done.38.r3 = bf16[40,2048]{1,0:T(8,128)(2,1)S(1)} collective-permute-done((bf16[40,2048]{1,0:T(8,128)(2,1)S(1)}, bf16[40,2048]{1,0:T(8,128)(2,1)S(1)}, u32[]{:S(2)}, u32[]{:S(2)}) %collective-permute-start.38) | collective-permute-done | bytes 163872 | tf_op jit(solution)/shard_map/ppermute | solution.py:588
  142.4 3.1 %collective-permute-start.39 = (bf16[128,2048]{1,0:T(8,128)(2,1)S(1)}, bf16[128,2048]{1,0:T(8,128)(2,1)S(1)}, u32[]{:S(2)}, u32[]{:S(2)}) collective-permute-start(bf16[128,2048]{1,0:T(8,128)(2,1)S(1)} %get-tuple-element.143), channel_id=1, source_target_pairs={{0,1},{3,2},{4,5},{7,6},{8,9},{11,10},{12,13},{15,14},{16,17},{19,... | collective-permute-start | bytes 1572872 | tf_op jit(solution)/shard_map/ppermute | solution.py:582
  148.3 4.4 %collective-permute-done.34.r2 = bf16[40,2048]{1,0:T(8,128)(2,1)S(1)} collective-permute-done((bf16[40,2048]{1,0:T(8,128)(2,1)S(1)}, bf16[40,2048]{1,0:T(8,128)(2,1)S(1)}, u32[]{:S(2)}, u32[]{:S(2)}) %collective-permute-start.34) | collective-permute-done | bytes 163872 | tf_op jit(solution)/shard_map/ppermute | solution.py:588
  152.7 2.2 %shard_map.152 = (bf16[40,2048]{1,0:T(8,128)(2,1)S(1)}, bf16[40,2048]{1,0:T(8,128)(2,1)S(1)}, bf16[40,2048]{1,0:T(8,128)(2,1)S(1)}, bf16[40,2048]{1,0:T(8,128)(2,1)S(1)}) custom-call(s32[15]{0:T(128)S(1)} %concatenate.6.n, f32[4,160,768]{2,1,0:T(8,128)S(1)} %get-tuple-element.126.a_ref, f32[4,160,768]{2,1,0:T(8,128)S(1)} %get-tuple-element.127.b_ref, ...), custom_call_target="tpu_custom_call" | custom-call | flops 1 | bytes 1 | tf_op jit(solution)/shard_map/pallas_call | solution.py:528
  157.5 2.2 %collective-permute-done.41.r2 = bf16[40,2048]{1,0:T(8,128)(2,1)S(1)} collective-permute-done((bf16[40,2048]{1,0:T(8,128)(2,1)S(1)}, bf16[40,2048]{1,0:T(8,128)(2,1)S(1)}, u32[]{:S(2)}, u32[]{:S(2)}) %collective-permute-start.41) | collective-permute-done | bytes 163872 | tf_op jit(solution)/shard_map/ppermute | solution.py:588
  159.7 2.6 %collective-permute-done.42.r3 = bf16[40,2048]{1,0:T(8,128)(2,1)S(1)} collective-permute-done((bf16[40,2048]{1,0:T(8,128)(2,1)S(1)}, bf16[40,2048]{1,0:T(8,128)(2,1)S(1)}, u32[]{:S(2)}, u32[]{:S(2)}) %collective-permute-start.42) | collective-permute-done | bytes 163872 | tf_op jit(solution)/shard_map/ppermute | solution.py:588
  166.4 3.4 %collective-permute-start.48 = (bf16[128,2048]{1,0:T(8,128)(2,1)S(1)}, bf16[128,2048]{1,0:T(8,128)(2,1)S(1)}, u32[]{:S(2)}, u32[]{:S(2)}) collective-permute-start(bf16[128,2048]{1,0:T(8,128)(2,1)S(1)} %get-tuple-element.155), channel_id=1, source_target_pairs={{0,1},{3,2},{4,5},{7,6},{8,9},{11,10},{12,13},{15,14},{16,17},{19,... | collective-permute-start | bytes 1572872 | tf_op jit(solution)/shard_map/ppermute | solution.py:582
  169.9 2.0 %collective-permute-done.46.r2 = bf16[40,2048]{1,0:T(8,128)(2,1)S(1)} collective-permute-done((bf16[40,2048]{1,0:T(8,128)(2,1)S(1)}, bf16[40,2048]{1,0:T(8,128)(2,1)S(1)}, u32[]{:S(2)}, u32[]{:S(2)}) %collective-permute-start.46) | collective-permute-done | bytes 163872 | tf_op jit(solution)/shard_map/ppermute | solution.py:588
  171.9 2.1 %collective-permute-done.47.r3 = bf16[40,2048]{1,0:T(8,128)(2,1)S(1)} collective-permute-done((bf16[40,2048]{1,0:T(8,128)(2,1)S(1)}, bf16[40,2048]{1,0:T(8,128)(2,1)S(1)}, u32[]{:S(2)}, u32[]{:S(2)}) %collective-permute-start.47) | collective-permute-done | bytes 163872 | tf_op jit(solution)/shard_map/ppermute | solution.py:588
  181.9 13.3 %collective-permute-done.50.r6 = bf16[128,2048]{1,0:T(8,128)(2,1)S(1)} collective-permute-done((bf16[128,2048]{1,0:T(8,128)(2,1)S(1)}, bf16[128,2048]{1,0:T(8,128)(2,1)S(1)}, u32[]{:S(2)}, u32[]{:S(2)}) %collective-permute-start.50) | collective-permute-done | bytes 524320 | tf_op jit(solution)/shard_map/ppermute | solution.py:582
  195.1 2.0 %shard_map.160 = bf16[128,2048]{1,0:T(8,128)(2,1)} custom-call(s32[15]{0:T(128)S(1)} %concatenate.6.n, bf16[4,128,2048]{2,1,0:T(8,128)(2,1)S(1)} %get-tuple-element.118.t_ref, f32[1,2048]{1,0:T(1,128)S(1)} %bitcast.37, f32[128,2048]{1,0:T(8,128)S(1)} %get-tuple-element.153.dresid_ref._, f32[128,128]{1,0:T(8,128)S(1)} %get-tuple-element.154.scale_ref, ...), custom_call_target="tpu_custom_call" | custom-call | flops 1 | bytes 1 | tf_op jit(solution)/shard_map/pallas_call | solution.py:528
  (143 shorter events, 83.0 us)
Async XLA Ops:
  5.3 19.0 %collective-permute-start = (bf16[144,2048]{1,0:T(8,128)(2,1)}, bf16[144,2048]{1,0:T(8,128)(2,1)S(1)}, u32[]{:S(2)}, u32[]{:S(2)}) collective-permute-start(bf16[144,2048]{1,0:T(8,128)(2,1)} %shard_map.122.rest_0_.left_ref), channel_id=1, source_target_pairs={{0,1},{3,2},{4,5},{7,6},{8,9},{11,10},{12,13},{15,14},{16,17},{19,... | collective-permute-start | bytes 1769480 | tf_op jit(solution)/shard_map/ppermute | solution.py:582
  15.6 19.8 %collective-permute-start.2 = (bf16[128,2048]{1,0:T(8,128)(2,1)S(1)}, bf16[128,2048]{1,0:T(8,128)(2,1)S(1)}, u32[]{:S(2)}, u32[]{:S(2)}) collective-permute-start(bf16[128,2048]{1,0:T(8,128)(2,1)S(1)} %shard_map.123.rest_0_.left_ref), channel_id=1, source_target_pairs={{0,1},{3,2},{4,5},{7,6},{8,9},{11,10},{12,13},{15,14},{16,17},{19,... | collective-permute-start | bytes 1572872 | tf_op jit(solution)/shard_map/ppermute | solution.py:582
  24.9 20.1 %collective-permute-start.1 = (bf16[144,2048]{1,0:T(8,128)(2,1)S(1)}, bf16[144,2048]{1,0:T(8,128)(2,1)S(1)}, u32[]{:S(2)}, u32[]{:S(2)}) collective-permute-start(bf16[144,2048]{1,0:T(8,128)(2,1)S(1)} %shard_map.126._.left_ref), channel_id=1, source_target_pairs={{1,2},{2,1},{5,6},{6,5},{9,10},{10,9},{13,14},{14,13},{17,18},{18,... | collective-permute-start | bytes 1769480 | tf_op jit(solution)/shard_map/ppermute | solution.py:582
  25.6 21.5 %collective-permute-start.4 = (bf16[128,2048]{1,0:T(8,128)(2,1)S(1)}, bf16[128,2048]{1,0:T(8,128)(2,1)}, u32[]{:S(2)}, u32[]{:S(2)}) collective-permute-start(bf16[128,2048]{1,0:T(8,128)(2,1)S(1)} %shard_map.124.rest_0_.left_ref), channel_id=1, source_target_pairs={{0,1},{3,2},{4,5},{7,6},{8,9},{11,10},{12,13},{15,14},{16,17},{19,... | collective-permute-start | bytes 1572872 | tf_op jit(solution)/shard_map/ppermute | solution.py:582
  36.0 13.5 %collective-permute-start.7 = (bf16[128,2048]{1,0:T(8,128)(2,1)S(1)}, bf16[128,2048]{1,0:T(8,128)(2,1)}, u32[]{:S(2)}, u32[]{:S(2)}) collective-permute-start(bf16[128,2048]{1,0:T(8,128)(2,1)S(1)} %shard_map.127._.left_ref), channel_id=1, source_target_pairs={{1,2},{2,1},{5,6},{6,5},{9,10},{10,9},{13,14},{14,13},{17,18},{18,... | collective-permute-start | bytes 1572872 | tf_op jit(solution)/shard_map/ppermute | solution.py:582
  37.5 19.2 %collective-permute-start.6 = (bf16[128,2048]{1,0:T(8,128)(2,1)S(1)}, bf16[128,2048]{1,0:T(8,128)(2,1)}, u32[]{:S(2)}, u32[]{:S(2)}) collective-permute-start(bf16[128,2048]{1,0:T(8,128)(2,1)S(1)} %shard_map.125._.left_ref), channel_id=1, source_target_pairs={{0,1},{3,2},{4,5},{7,6},{8,9},{11,10},{12,13},{15,14},{16,17},{19,... | collective-permute-start | bytes 1572872 | tf_op jit(solution)/shard_map/ppermute | solution.py:582
  45.7 18.2 %collective-permute-start.3 = (bf16[144,2048]{1,0:T(8,128)(2,1)S(1)}, bf16[144,2048]{1,0:T(8,128)(2,1)S(1)}, u32[]{:S(2)}, u32[]{:S(2)}) collective-permute-start(bf16[144,2048]{1,0:T(8,128)(2,1)S(1)} %shard_map.128._.refs_0_), channel_id=1, source_target_pairs={{1,0},{2,3},{5,4},{6,7},{9,8},{10,11},{13,12},{14,15},{17,16},{18,... | collective-permute-start | bytes 1769480 | tf_op jit(solution)/shard_map/ppermute | solution.py:582
  48.8 10.4 %collective-permute-start.5 = (bf16[128,2048]{1,0:T(8,128)(2,1)S(1)}, bf16[128,2048]{1,0:T(8,128)(2,1)S(1)}, u32[]{:S(2)}, u32[]{:S(2)}) collective-permute-start(bf16[128,2048]{1,0:T(8,128)(2,1)S(1)} %shard_map.129._.left_ref), channel_id=1, source_target_pairs={{1,2},{2,1},{5,6},{6,5},{9,10},{10,9},{13,14},{14,13},{17,18},{18,... | collective-permute-start | bytes 1572872 | tf_op jit(solution)/shard_map/ppermute | solution.py:582
  51.2 20.1 %collective-permute-start.11 = (bf16[128,2048]{1,0:T(8,128)(2,1)S(1)}, bf16[128,2048]{1,0:T(8,128)(2,1)S(1)}, u32[]{:S(2)}, u32[]{:S(2)}) collective-permute-start(bf16[128,2048]{1,0:T(8,128)(2,1)S(1)} %shard_map.130._.refs_0_), channel_id=1, source_target_pairs={{1,0},{2,3},{5,4},{6,7},{9,8},{10,11},{13,12},{14,15},{17,16},{18,... | collective-permute-start | bytes 1572872 | tf_op jit(solution)/shard_map/ppermute | solution.py:582
  58.4 19.0 %collective-permute-start.16 = (bf16[128,2048]{1,0:T(8,128)(2,1)S(1)}, bf16[128,2048]{1,0:T(8,128)(2,1)S(1)}, u32[]{:S(2)}, u32[]{:S(2)}) collective-permute-start(bf16[128,2048]{1,0:T(8,128)(2,1)S(1)} %shard_map.131._.left_ref), channel_id=1, source_target_pairs={{1,2},{2,1},{5,6},{6,5},{9,10},{10,9},{13,14},{14,13},{17,18},{18,... | collective-permute-start | bytes 1572872 | tf_op jit(solution)/shard_map/ppermute | solution.py:582
  65.2 8.8 %collective-permute-start.8 = (bf16[40,2176]{1,0:T(8,128)(2,1)S(1)}, bf16[40,2176]{1,0:T(8,128)(2,1)S(1)}, u32[]{:S(2)}, u32[]{:S(2)}) collective-permute-start(bf16[40,2176]{1,0:T(8,128)(2,1)S(1)} %get-tuple-element.80), channel_id=1, source_target_pairs={{0,4},{4,0},{8,12},{12,8},{1,5},{5,1},{9,13},{13,9},{2,6},{6,2},{1... | collective-permute-start | bytes 522248 | tf_op jit(solution)/shard_map/ppermute | solution.py:588
  65.3 8.7 %collective-permute-start.9 = (bf16[40,2176]{1,0:T(8,128)(2,1)S(1)}, bf16[40,2176]{1,0:T(8,128)(2,1)S(1)}, u32[]{:S(2)}, u32[]{:S(2)}) collective-permute-start(bf16[40,2176]{1,0:T(8,128)(2,1)S(1)} %get-tuple-element.81), channel_id=1, source_target_pairs={{0,8},{4,12},{8,0},{12,4},{1,9},{5,13},{9,1},{13,5},{2,10},{6,14},... | collective-permute-start | bytes 522248 | tf_op jit(solution)/shard_map/ppermute | solution.py:588
  66.8 8.6 %collective-permute-start.10 = (bf16[40,2176]{1,0:T(8,128)(2,1)S(1)}, bf16[40,2176]{1,0:T(8,128)(2,1)S(1)}, u32[]{:S(2)}, u32[]{:S(2)}) collective-permute-start(bf16[40,2176]{1,0:T(8,128)(2,1)S(1)} %get-tuple-element.82), channel_id=1, source_target_pairs={{0,12},{4,8},{8,4},{12,0},{1,13},{5,9},{9,5},{13,1},{2,14},{6,10},... | collective-permute-start | bytes 522248 | tf_op jit(solution)/shard_map/ppermute | solution.py:588
  71.3 12.6 %collective-permute-start.15 = (bf16[128,2048]{1,0:T(8,128)(2,1)S(1)}, bf16[128,2048]{1,0:T(8,128)(2,1)S(1)}, u32[]{:S(2)}, u32[]{:S(2)}) collective-permute-start(bf16[128,2048]{1,0:T(8,128)(2,1)S(1)} %shard_map.132.refs_5_.refs_0_), channel_id=1, source_target_pairs={{1,0},{2,3},{5,4},{6,7},{9,8},{10,11},{13,12},{14,15},{17,16},{18,... | collective-permute-start | bytes 1572872 | tf_op jit(solution)/shard_map/ppermute | solution.py:582
  78.1 16.6 %collective-permute-start.20 = (bf16[128,2048]{1,0:T(8,128)(2,1)S(1)}, bf16[128,2048]{1,0:T(8,128)(2,1)S(1)}, u32[]{:S(2)}, u32[]{:S(2)}) collective-permute-start(bf16[128,2048]{1,0:T(8,128)(2,1)S(1)} %shard_map.136.refs_8_.refs_0_), channel_id=1, source_target_pairs={{1,0},{2,3},{5,4},{6,7},{9,8},{10,11},{13,12},{14,15},{17,16},{18,... | collective-permute-start | bytes 1572872 | tf_op jit(solution)/shard_map/ppermute | solution.py:582
  81.4 8.5 %collective-permute-start.14 = (bf16[40,2176]{1,0:T(8,128)(2,1)S(1)}, bf16[40,2176]{1,0:T(8,128)(2,1)S(1)}, u32[]{:S(2)}, u32[]{:S(2)}) collective-permute-start(bf16[40,2176]{1,0:T(8,128)(2,1)S(1)} %get-tuple-element.90), channel_id=1, source_target_pairs={{0,12},{4,8},{8,4},{12,0},{1,13},{5,9},{9,5},{13,1},{2,14},{6,10},... | collective-permute-start | bytes 522248 | tf_op jit(solution)/shard_map/ppermute | solution.py:588
  85.2 12.3 %collective-permute-start.17 = (bf16[40,2176]{1,0:T(8,128)(2,1)S(1)}, bf16[40,2176]{1,0:T(8,128)(2,1)S(1)}, u32[]{:S(2)}, u32[]{:S(2)}) collective-permute-start(bf16[40,2176]{1,0:T(8,128)(2,1)S(1)} %get-tuple-element.99), channel_id=1, source_target_pairs={{0,4},{4,0},{8,12},{12,8},{1,5},{5,1},{9,13},{13,9},{2,6},{6,2},{1... | collective-permute-start | bytes 522248 | tf_op jit(solution)/shard_map/ppermute | solution.py:588
  85.3 12.6 %collective-permute-start.18 = (bf16[40,2176]{1,0:T(8,128)(2,1)S(1)}, bf16[40,2176]{1,0:T(8,128)(2,1)S(1)}, u32[]{:S(2)}, u32[]{:S(2)}) collective-permute-start(bf16[40,2176]{1,0:T(8,128)(2,1)S(1)} %get-tuple-element.100), channel_id=1, source_target_pairs={{0,8},{4,12},{8,0},{12,4},{1,9},{5,13},{9,1},{13,5},{2,10},{6,14},... | collective-permute-start | bytes 522248 | tf_op jit(solution)/shard_map/ppermute | solution.py:588
  87.1 10.8 %collective-permute-start.19 = (bf16[40,2176]{1,0:T(8,128)(2,1)S(1)}, bf16[40,2176]{1,0:T(8,128)(2,1)S(1)}, u32[]{:S(2)}, u32[]{:S(2)}) collective-permute-start(bf16[40,2176]{1,0:T(8,128)(2,1)S(1)} %get-tuple-element.101), channel_id=1, source_target_pairs={{0,12},{4,8},{8,4},{12,0},{1,13},{5,9},{9,5},{13,1},{2,14},{6,10},... | collective-permute-start | bytes 522248 | tf_op jit(solution)/shard_map/ppermute | solution.py:588
  96.1 7.3 %collective-permute-start.22 = (bf16[40,2176]{1,0:T(8,128)(2,1)S(1)}, bf16[40,2176]{1,0:T(8,128)(2,1)S(1)}, u32[]{:S(2)}, u32[]{:S(2)}) collective-permute-start(bf16[40,2176]{1,0:T(8,128)(2,1)S(1)} %get-tuple-element.111), channel_id=1, source_target_pairs={{0,8},{4,12},{8,0},{12,4},{1,9},{5,13},{9,1},{13,5},{2,10},{6,14},... | collective-permute-start | bytes 522248 | tf_op jit(solution)/shard_map/ppermute | solution.py:588
  97.6 8.6 %collective-permute-start.23 = (bf16[40,2176]{1,0:T(8,128)(2,1)S(1)}, bf16[40,2176]{1,0:T(8,128)(2,1)S(1)}, u32[]{:S(2)}, u32[]{:S(2)}) collective-permute-start(bf16[40,2176]{1,0:T(8,128)(2,1)S(1)} %get-tuple-element.112), channel_id=1, source_target_pairs={{0,12},{4,8},{8,4},{12,0},{1,13},{5,9},{9,5},{13,1},{2,14},{6,10},... | collective-permute-start | bytes 522248 | tf_op jit(solution)/shard_map/ppermute | solution.py:588
  132.7 8.9 %collective-permute-start.38 = (bf16[40,2048]{1,0:T(8,128)(2,1)S(1)}, bf16[40,2048]{1,0:T(8,128)(2,1)S(1)}, u32[]{:S(2)}, u32[]{:S(2)}) collective-permute-start(bf16[40,2048]{1,0:T(8,128)(2,1)S(1)} %get-tuple-element.138), channel_id=1, source_target_pairs={{0,12},{4,8},{8,4},{12,0},{1,13},{5,9},{9,5},{13,1},{2,14},{6,10},... | collective-permute-start | bytes 491528 | tf_op jit(solution)/shard_map/ppermute | solution.py:588
  142.4 20.7 %collective-permute-start.39 = (bf16[128,2048]{1,0:T(8,128)(2,1)S(1)}, bf16[128,2048]{1,0:T(8,128)(2,1)S(1)}, u32[]{:S(2)}, u32[]{:S(2)}) collective-permute-start(bf16[128,2048]{1,0:T(8,128)(2,1)S(1)} %get-tuple-element.143), channel_id=1, source_target_pairs={{0,1},{3,2},{4,5},{7,6},{8,9},{11,10},{12,13},{15,14},{16,17},{19,... | collective-permute-start | bytes 1572872 | tf_op jit(solution)/shard_map/ppermute | solution.py:582
  146.2 9.1 %collective-permute-start.35 = (bf16[40,2048]{1,0:T(8,128)(2,1)S(1)}, bf16[40,2048]{1,0:T(8,128)(2,1)S(1)}, u32[]{:S(2)}, u32[]{:S(2)}) collective-permute-start(bf16[40,2048]{1,0:T(8,128)(2,1)S(1)} %get-tuple-element.135), channel_id=1, source_target_pairs={{0,12},{4,8},{8,4},{12,0},{1,13},{5,9},{9,5},{13,1},{2,14},{6,10},... | collective-permute-start | bytes 491528 | tf_op jit(solution)/shard_map/ppermute | solution.py:588
  147.5 10.0 %collective-permute-start.40 = (bf16[40,2048]{1,0:T(8,128)(2,1)S(1)}, bf16[40,2048]{1,0:T(8,128)(2,1)S(1)}, u32[]{:S(2)}, u32[]{:S(2)}) collective-permute-start(bf16[40,2048]{1,0:T(8,128)(2,1)S(1)} %get-tuple-element.144), channel_id=1, source_target_pairs={{0,4},{4,0},{8,12},{12,8},{1,5},{5,1},{9,13},{13,9},{2,6},{6,2},{1... | collective-permute-start | bytes 491528 | tf_op jit(solution)/shard_map/ppermute | solution.py:588
  147.8 11.9 %collective-permute-start.41 = (bf16[40,2048]{1,0:T(8,128)(2,1)S(1)}, bf16[40,2048]{1,0:T(8,128)(2,1)S(1)}, u32[]{:S(2)}, u32[]{:S(2)}) collective-permute-start(bf16[40,2048]{1,0:T(8,128)(2,1)S(1)} %get-tuple-element.145), channel_id=1, source_target_pairs={{0,8},{4,12},{8,0},{12,4},{1,9},{5,13},{9,1},{13,5},{2,10},{6,14},... | collective-permute-start | bytes 491528 | tf_op jit(solution)/shard_map/ppermute | solution.py:588
  152.7 9.6 %collective-permute-start.42 = (bf16[40,2048]{1,0:T(8,128)(2,1)S(1)}, bf16[40,2048]{1,0:T(8,128)(2,1)S(1)}, u32[]{:S(2)}, u32[]{:S(2)}) collective-permute-start(bf16[40,2048]{1,0:T(8,128)(2,1)S(1)} %get-tuple-element.146), channel_id=1, source_target_pairs={{0,12},{4,8},{8,4},{12,0},{1,13},{5,9},{9,5},{13,1},{2,14},{6,10},... | collective-permute-start | bytes 491528 | tf_op jit(solution)/shard_map/ppermute | solution.py:588
  156.1 19.5 %collective-permute-start.44 = (bf16[128,2048]{1,0:T(8,128)(2,1)S(1)}, bf16[128,2048]{1,0:T(8,128)(2,1)S(1)}, u32[]{:S(2)}, u32[]{:S(2)}) collective-permute-start(bf16[128,2048]{1,0:T(8,128)(2,1)S(1)} %get-tuple-element.148), channel_id=1, source_target_pairs={{0,1},{3,2},{4,5},{7,6},{8,9},{11,10},{12,13},{15,14},{16,17},{19,... | collective-permute-start | bytes 1572872 | tf_op jit(solution)/shard_map/ppermute | solution.py:582
  163.8 13.2 %collective-permute-start.43 = (bf16[128,2048]{1,0:T(8,128)(2,1)S(1)}, bf16[128,2048]{1,0:T(8,128)(2,1)S(1)}, u32[]{:S(2)}, u32[]{:S(2)}) collective-permute-start(bf16[128,2048]{1,0:T(8,128)(2,1)S(1)} %shard_map.155._), channel_id=1, source_target_pairs={{1,2},{2,1},{5,6},{6,5},{9,10},{10,9},{13,14},{14,13},{17,18},{18,... | collective-permute-start | bytes 1572872 | tf_op jit(solution)/shard_map/ppermute | solution.py:582
  165.3 8.7 %collective-permute-start.47 = (bf16[40,2048]{1,0:T(8,128)(2,1)S(1)}, bf16[40,2048]{1,0:T(8,128)(2,1)S(1)}, u32[]{:S(2)}, u32[]{:S(2)}) collective-permute-start(bf16[40,2048]{1,0:T(8,128)(2,1)S(1)} %get-tuple-element.151), channel_id=1, source_target_pairs={{0,12},{4,8},{8,4},{12,0},{1,13},{5,9},{9,5},{13,1},{2,14},{6,10},... | collective-permute-start | bytes 491528 | tf_op jit(solution)/shard_map/ppermute | solution.py:588
  166.4 15.4 %collective-permute-start.48 = (bf16[128,2048]{1,0:T(8,128)(2,1)S(1)}, bf16[128,2048]{1,0:T(8,128)(2,1)S(1)}, u32[]{:S(2)}, u32[]{:S(2)}) collective-permute-start(bf16[128,2048]{1,0:T(8,128)(2,1)S(1)} %get-tuple-element.155), channel_id=1, source_target_pairs={{0,1},{3,2},{4,5},{7,6},{8,9},{11,10},{12,13},{15,14},{16,17},{19,... | collective-permute-start | bytes 1572872 | tf_op jit(solution)/shard_map/ppermute | solution.py:582
  177.6 17.5 %collective-permute-start.50 = (bf16[128,2048]{1,0:T(8,128)(2,1)S(1)}, bf16[128,2048]{1,0:T(8,128)(2,1)S(1)}, u32[]{:S(2)}, u32[]{:S(2)}) collective-permute-start(bf16[128,2048]{1,0:T(8,128)(2,1)S(1)} %shard_map.158._), channel_id=1, source_target_pairs={{1,0},{2,3},{5,4},{6,7},{9,8},{10,11},{13,12},{14,15},{17,16},{18,... | collective-permute-start | bytes 1572872 | tf_op jit(solution)/shard_map/ppermute | solution.py:582
  (30 other events, 197.6 us)

commit v7 on v6

--- a/solution.py
+++ b/solution.py
@@ -218,7 +218,7 @@
 )
 VMEM_LIMIT = 24 * 2**20
 FIRST_LIMIT = 54 * 2**20
-FIRST_CUTS = 8
+FIRST_CUTS = 4
 BLOCK_ORDER = ((3, 2, 1, 0), (3, 0, 2, 1), (0, 3, 1, 2), (0, 1, 2, 3))
 OWN_EXPERT, LEAF, Z, PEER, PEER_EXPERT, ORDER = 0, 1, 2, 3, 7, 11
 BF16 = jnp.bfloat16

time: 198 us -> 198 us (level)
  no operation moved by 1% of the time
where the time goes in v7:
time: 198 us; the launch traced here: 197 us
  waiting for transfers between devices  72.2 us (36%)
  starting transfers between devices  63.1 us (32%)
  Pallas kernels  55.7 us (28%)
  local copies, waits for them, and re-layouts  4.18 us (2%)
    pallas_call x38, Pallas kernels, __call__(): pl.pallas_call(kernel, out_shape=list(shapes), grid_spec=pltpu.PrefetchSc...  51.3 us
    ppermute x18, starting transfers between devices, along_z(): return lax.ppermute(value, 'tensor', pairs)  40.8 us
    ppermute x18, waiting for transfers between devices, along_z(): return lax.ppermute(value, 'tensor', pairs)  39.1 us
    ppermute x30, waiting for transfers between devices, swap_e(): return lax.ppermute(value, 'expert', [(i, i ^ bits) for i in range(4)])  32 us
    ppermute x30, starting transfers between devices, swap_e(): return lax.ppermute(value, 'expert', [(i, i ^ bits) for i in range(4)])  17.9 us
    ppermute x3, starting transfers between devices, swap_z(): return lax.ppermute(value, 'tensor', [(i, i ^ bits) for i in range(4)])  4.45 us
    pallas_call x1, Pallas kernels, first_hop(): pl.pallas_call(functools.partial(first_kernel, experts), out_shape=shape(...  4.4 us
  transfers between devices with their start and end apart: 51, of which 28 were waited for; matrix products, arithmetic and copies ran while one was open for 1% of the time, Pallas kernels for 20%

profile of v7, /device:TPU:0, one launch (start us, length us, event | category | flops | bytes accessed | tf_op | source)
XLA Modules:
  0.0 196.9 jit_solution(3369413966377577411)
XLA Ops:
  0.6 4.4 %shard_map.122.rest_0_.left_ref = bf16[144,2048]{1,0:T(8,128)(2,1)} custom-call(s32[4,128]{1,0:T(4,128)} %bitcast.40, bf16[512,1024]{1,0:T(8,128)(2,1)} %context_ref.5, bf16[1024,2048]{1,0:T(8,128)(2,1)} %weight_ref.5, bf16[128,2048]{1,0:T(8,128)(2,1)} %resid_ref.5), custom_call_target="tpu_custom_call" | custom-call | tf_op jit(solution)/shard_map/pallas_call | solution.py:622
  5.1 5.0 %collective-permute-start = (bf16[144,2048]{1,0:T(8,128)(2,1)}, bf16[144,2048]{1,0:T(8,128)(2,1)S(1)}, u32[]{:S(2)}, u32[]{:S(2)}) collective-permute-start(bf16[144,2048]{1,0:T(8,128)(2,1)} %shard_map.122.rest_0_.left_ref), channel_id=1, source_target_pairs={{0,1},{3,2},{4,5},{7,6},{8,9},{11,10},{12,13},{15,14},{16,17},{19,... | collective-permute-start | bytes 1769480 | tf_op jit(solution)/shard_map/ppermute | solution.py:582
  10.9 2.2 %copy-done.2 = bf16[1024,2048]{1,0:T(8,128)(2,1)S(1)} copy-done((bf16[1024,2048]{1,0:T(8,128)(2,1)S(1)}, bf16[1024,2048]{1,0:T(8,128)(2,1)}, u32[]{:S(2)}) %copy-start.2) | copy-done | bytes 4194328
  19.3 4.8 %collective-permute-done.right_ref = bf16[144,2048]{1,0:T(8,128)(2,1)S(1)} collective-permute-done((bf16[144,2048]{1,0:T(8,128)(2,1)}, bf16[144,2048]{1,0:T(8,128)(2,1)S(1)}, u32[]{:S(2)}, u32[]{:S(2)}) %collective-permute-start) | collective-permute-done | bytes 589856 | tf_op jit(solution)/shard_map/ppermute | solution.py:582
  25.4 7.9 %collective-permute-start.4 = (bf16[128,2048]{1,0:T(8,128)(2,1)S(1)}, bf16[128,2048]{1,0:T(8,128)(2,1)}, u32[]{:S(2)}, u32[]{:S(2)}) collective-permute-start(bf16[128,2048]{1,0:T(8,128)(2,1)S(1)} %shard_map.124.rest_0_.left_ref), channel_id=1, source_target_pairs={{0,1},{3,2},{4,5},{7,6},{8,9},{11,10},{12,13},{15,14},{16,17},{19,... | collective-permute-start | bytes 1572872 | tf_op jit(solution)/shard_map/ppermute | solution.py:582
  37.3 7.2 %collective-permute-start.6 = (bf16[128,2048]{1,0:T(8,128)(2,1)S(1)}, bf16[128,2048]{1,0:T(8,128)(2,1)}, u32[]{:S(2)}, u32[]{:S(2)}) collective-permute-start(bf16[128,2048]{1,0:T(8,128)(2,1)S(1)} %shard_map.125._.left_ref), channel_id=1, source_target_pairs={{0,1},{3,2},{4,5},{7,6},{8,9},{11,10},{12,13},{15,14},{16,17},{19,... | collective-permute-start | bytes 1572872 | tf_op jit(solution)/shard_map/ppermute | solution.py:582
  52.4 4.1 %collective-permute-done.6.right_ref = bf16[128,2048]{1,0:T(8,128)(2,1)} collective-permute-done((bf16[128,2048]{1,0:T(8,128)(2,1)S(1)}, bf16[128,2048]{1,0:T(8,128)(2,1)}, u32[]{:S(2)}, u32[]{:S(2)}) %collective-permute-start.6) | collective-permute-done | bytes 524320 | tf_op jit(solution)/shard_map/ppermute | solution.py:582
  59.6 4.0 %collective-permute-done.3.refs_1_ = bf16[144,2048]{1,0:T(8,128)(2,1)S(1)} collective-permute-done((bf16[144,2048]{1,0:T(8,128)(2,1)S(1)}, bf16[144,2048]{1,0:T(8,128)(2,1)S(1)}, u32[]{:S(2)}, u32[]{:S(2)}) %collective-permute-start.3) | collective-permute-done | bytes 589856 | tf_op jit(solution)/shard_map/ppermute | solution.py:582
  67.0 4.1 %collective-permute-done.11.refs_1_ = bf16[128,2048]{1,0:T(8,128)(2,1)S(1)} collective-permute-done((bf16[128,2048]{1,0:T(8,128)(2,1)S(1)}, bf16[128,2048]{1,0:T(8,128)(2,1)S(1)}, u32[]{:S(2)}, u32[]{:S(2)}) %collective-permute-start.11) | collective-permute-done | bytes 524320 | tf_op jit(solution)/shard_map/ppermute | solution.py:582
  75.2 2.0 shard_map.135
  81.3 2.4 %collective-permute-done.15.refs_1_ = bf16[128,2048]{1,0:T(8,128)(2,1)S(1)} collective-permute-done((bf16[128,2048]{1,0:T(8,128)(2,1)S(1)}, bf16[128,2048]{1,0:T(8,128)(2,1)S(1)}, u32[]{:S(2)}, u32[]{:S(2)}) %collective-permute-start.15) | collective-permute-done | bytes 524320 | tf_op jit(solution)/shard_map/ppermute | solution.py:582
  86.9 2.7 %collective-permute-done.14.r3 = bf16[40,2176]{1,0:T(8,128)(2,1)S(1)} collective-permute-done((bf16[40,2176]{1,0:T(8,128)(2,1)S(1)}, bf16[40,2176]{1,0:T(8,128)(2,1)S(1)}, u32[]{:S(2)}, u32[]{:S(2)}) %collective-permute-start.14) | collective-permute-done | bytes 174112 | tf_op jit(solution)/shard_map/ppermute | solution.py:588
  89.7 2.0 shard_map.138
  91.6 2.7 %collective-permute-done.20.refs_1_ = bf16[128,2048]{1,0:T(8,128)(2,1)S(1)} collective-permute-done((bf16[128,2048]{1,0:T(8,128)(2,1)S(1)}, bf16[128,2048]{1,0:T(8,128)(2,1)S(1)}, u32[]{:S(2)}, u32[]{:S(2)}) %collective-permute-start.20) | collective-permute-done | bytes 524320 | tf_op jit(solution)/shard_map/ppermute | solution.py:582
  99.7 3.5 %collective-permute-done.22.r2 = bf16[40,2176]{1,0:T(8,128)(2,1)S(1)} collective-permute-done((bf16[40,2176]{1,0:T(8,128)(2,1)S(1)}, bf16[40,2176]{1,0:T(8,128)(2,1)S(1)}, u32[]{:S(2)}, u32[]{:S(2)}) %collective-permute-start.22) | collective-permute-done | bytes 174112 | tf_op jit(solution)/shard_map/ppermute | solution.py:588
  103.1 2.8 %collective-permute-done.23.r3 = bf16[40,2176]{1,0:T(8,128)(2,1)S(1)} collective-permute-done((bf16[40,2176]{1,0:T(8,128)(2,1)S(1)}, bf16[40,2176]{1,0:T(8,128)(2,1)S(1)}, u32[]{:S(2)}, u32[]{:S(2)}) %collective-permute-start.23) | collective-permute-done | bytes 174112 | tf_op jit(solution)/shard_map/ppermute | solution.py:588
  115.2 2.0 %collective-permute-start.29 = (bf16[8,2048]{1,0:T(8,128)(2,1)S(1)}, bf16[8,2048]{1,0:T(8,128)(2,1)S(1)}, u32[]{:S(2)}, u32[]{:S(2)}) collective-permute-start(bf16[8,2048]{1,0:T(8,128)(2,1)S(1)} %shard_map.144._.p0), channel_id=1, source_target_pairs={{0,3},{1,2},{2,1},{3,0},{4,7},{5,6},{6,5},{7,4},{8,11},{9,10},{10,... | collective-permute-start | bytes 98312 | tf_op jit(solution)/shard_map/ppermute | solution.py:585
  127.1 2.3 %shard_map.147 = (f32[32,2048]{1,0:T(8,128)S(1)}, f32[32,768]{1,0:T(8,128)S(1)}, f32[1]{0:T(128)}) custom-call(s32[15]{0:T(128)S(1)} %concatenate.6.n, bf16[8,2048]{1,0:T(8,128)(2,1)S(1)} %shard_map.146.q0._, bf16[8,2048]{1,0:T(8,128)(2,1)S(1)} %collective-permute-done.30.q1, bf16[8,2048]{1,0:T(8,128)(2,1)S(1)} %collective-permute-done.31.q2, ...), custom_call_target="tpu_custom_call" | custom-call | flops 1 | bytes 1 | tf_op jit(solution)/shard_map/pallas_call | solution.py:528
  129.4 2.2 %shard_map.148 = (bf16[40,2048]{1,0:T(8,128)(2,1)S(1)}, bf16[40,2048]{1,0:T(8,128)(2,1)S(1)}, bf16[40,2048]{1,0:T(8,128)(2,1)S(1)}, bf16[40,2048]{1,0:T(8,128)(2,1)S(1)}) custom-call(s32[15]{0:T(128)S(1)} %concatenate.6.n, f32[4,160,768]{2,1,0:T(8,128)S(1)} %get-tuple-element.126.a_ref, f32[4,160,768]{2,1,0:T(8,128)S(1)} %get-tuple-element.127.b_ref, ...), custom_call_target="tpu_custom_call" | custom-call | flops 1 | bytes 1 | tf_op jit(solution)/shard_map/pallas_call | solution.py:528
  133.6 2.4 %shard_map.149 = (bf16[40,2048]{1,0:T(8,128)(2,1)S(1)}, bf16[40,2048]{1,0:T(8,128)(2,1)S(1)}, bf16[40,2048]{1,0:T(8,128)(2,1)S(1)}, bf16[40,2048]{1,0:T(8,128)(2,1)S(1)}) custom-call(s32[15]{0:T(128)S(1)} %concatenate.6.n, f32[4,160,768]{2,1,0:T(8,128)S(1)} %get-tuple-element.126.a_ref, f32[4,160,768]{2,1,0:T(8,128)S(1)} %get-tuple-element.127.b_ref, ...), custom_call_target="tpu_custom_call" | custom-call | flops 1 | bytes 1 | tf_op jit(solution)/shard_map/pallas_call | solution.py:528
  136.0 2.2 %shard_map.150 = (bf16[40,2048]{1,0:T(8,128)(2,1)S(1)}, bf16[40,2048]{1,0:T(8,128)(2,1)S(1)}, bf16[40,2048]{1,0:T(8,128)(2,1)S(1)}, bf16[40,2048]{1,0:T(8,128)(2,1)S(1)}) custom-call(s32[15]{0:T(128)S(1)} %concatenate.6.n, f32[4,160,768]{2,1,0:T(8,128)S(1)} %get-tuple-element.126.a_ref, f32[4,160,768]{2,1,0:T(8,128)S(1)} %get-tuple-element.127.b_ref, ...), custom_call_target="tpu_custom_call" | custom-call | flops 1 | bytes 1 | tf_op jit(solution)/shard_map/pallas_call | solution.py:528
  138.8 2.6 %collective-permute-done.38.r3 = bf16[40,2048]{1,0:T(8,128)(2,1)S(1)} collective-permute-done((bf16[40,2048]{1,0:T(8,128)(2,1)S(1)}, bf16[40,2048]{1,0:T(8,128)(2,1)S(1)}, u32[]{:S(2)}, u32[]{:S(2)}) %collective-permute-start.38) | collective-permute-done | bytes 163872 | tf_op jit(solution)/shard_map/ppermute | solution.py:588
  142.2 3.1 %collective-permute-start.39 = (bf16[128,2048]{1,0:T(8,128)(2,1)S(1)}, bf16[128,2048]{1,0:T(8,128)(2,1)S(1)}, u32[]{:S(2)}, u32[]{:S(2)}) collective-permute-start(bf16[128,2048]{1,0:T(8,128)(2,1)S(1)} %get-tuple-element.143), channel_id=1, source_target_pairs={{0,1},{3,2},{4,5},{7,6},{8,9},{11,10},{12,13},{15,14},{16,17},{19,... | collective-permute-start | bytes 1572872 | tf_op jit(solution)/shard_map/ppermute | solution.py:582
  148.1 4.4 %collective-permute-done.34.r2 = bf16[40,2048]{1,0:T(8,128)(2,1)S(1)} collective-permute-done((bf16[40,2048]{1,0:T(8,128)(2,1)S(1)}, bf16[40,2048]{1,0:T(8,128)(2,1)S(1)}, u32[]{:S(2)}, u32[]{:S(2)}) %collective-permute-start.34) | collective-permute-done | bytes 163872 | tf_op jit(solution)/shard_map/ppermute | solution.py:588
  152.5 2.2 %shard_map.152 = (bf16[40,2048]{1,0:T(8,128)(2,1)S(1)}, bf16[40,2048]{1,0:T(8,128)(2,1)S(1)}, bf16[40,2048]{1,0:T(8,128)(2,1)S(1)}, bf16[40,2048]{1,0:T(8,128)(2,1)S(1)}) custom-call(s32[15]{0:T(128)S(1)} %concatenate.6.n, f32[4,160,768]{2,1,0:T(8,128)S(1)} %get-tuple-element.126.a_ref, f32[4,160,768]{2,1,0:T(8,128)S(1)} %get-tuple-element.127.b_ref, ...), custom_call_target="tpu_custom_call" | custom-call | flops 1 | bytes 1 | tf_op jit(solution)/shard_map/pallas_call | solution.py:528
  157.3 2.2 %collective-permute-done.41.r2 = bf16[40,2048]{1,0:T(8,128)(2,1)S(1)} collective-permute-done((bf16[40,2048]{1,0:T(8,128)(2,1)S(1)}, bf16[40,2048]{1,0:T(8,128)(2,1)S(1)}, u32[]{:S(2)}, u32[]{:S(2)}) %collective-permute-start.41) | collective-permute-done | bytes 163872 | tf_op jit(solution)/shard_map/ppermute | solution.py:588
  159.5 2.6 %collective-permute-done.42.r3 = bf16[40,2048]{1,0:T(8,128)(2,1)S(1)} collective-permute-done((bf16[40,2048]{1,0:T(8,128)(2,1)S(1)}, bf16[40,2048]{1,0:T(8,128)(2,1)S(1)}, u32[]{:S(2)}, u32[]{:S(2)}) %collective-permute-start.42) | collective-permute-done | bytes 163872 | tf_op jit(solution)/shard_map/ppermute | solution.py:588
  166.2 3.4 %collective-permute-start.48 = (bf16[128,2048]{1,0:T(8,128)(2,1)S(1)}, bf16[128,2048]{1,0:T(8,128)(2,1)S(1)}, u32[]{:S(2)}, u32[]{:S(2)}) collective-permute-start(bf16[128,2048]{1,0:T(8,128)(2,1)S(1)} %get-tuple-element.155), channel_id=1, source_target_pairs={{0,1},{3,2},{4,5},{7,6},{8,9},{11,10},{12,13},{15,14},{16,17},{19,... | collective-permute-start | bytes 1572872 | tf_op jit(solution)/shard_map/ppermute | solution.py:582
  169.7 2.0 %collective-permute-done.46.r2 = bf16[40,2048]{1,0:T(8,128)(2,1)S(1)} collective-permute-done((bf16[40,2048]{1,0:T(8,128)(2,1)S(1)}, bf16[40,2048]{1,0:T(8,128)(2,1)S(1)}, u32[]{:S(2)}, u32[]{:S(2)}) %collective-permute-start.46) | collective-permute-done | bytes 163872 | tf_op jit(solution)/shard_map/ppermute | solution.py:588
  171.7 2.1 %collective-permute-done.47.r3 = bf16[40,2048]{1,0:T(8,128)(2,1)S(1)} collective-permute-done((bf16[40,2048]{1,0:T(8,128)(2,1)S(1)}, bf16[40,2048]{1,0:T(8,128)(2,1)S(1)}, u32[]{:S(2)}, u32[]{:S(2)}) %collective-permute-start.47) | collective-permute-done | bytes 163872 | tf_op jit(solution)/shard_map/ppermute | solution.py:588
  181.7 13.3 %collective-permute-done.50.r6 = bf16[128,2048]{1,0:T(8,128)(2,1)S(1)} collective-permute-done((bf16[128,2048]{1,0:T(8,128)(2,1)S(1)}, bf16[128,2048]{1,0:T(8,128)(2,1)S(1)}, u32[]{:S(2)}, u32[]{:S(2)}) %collective-permute-start.50) | collective-permute-done | bytes 524320 | tf_op jit(solution)/shard_map/ppermute | solution.py:582
  194.9 2.0 %shard_map.160 = bf16[128,2048]{1,0:T(8,128)(2,1)} custom-call(s32[15]{0:T(128)S(1)} %concatenate.6.n, bf16[4,128,2048]{2,1,0:T(8,128)(2,1)S(1)} %get-tuple-element.118.t_ref, f32[1,2048]{1,0:T(1,128)S(1)} %bitcast.37, f32[128,2048]{1,0:T(8,128)S(1)} %get-tuple-element.153.dresid_ref._, f32[128,128]{1,0:T(8,128)S(1)} %get-tuple-element.154.scale_ref, ...), custom_call_target="tpu_custom_call" | custom-call | flops 1 | bytes 1 | tf_op jit(solution)/shard_map/pallas_call | solution.py:528
  (143 shorter events, 83.0 us)
Async XLA Ops:
  5.1 19.0 %collective-permute-start = (bf16[144,2048]{1,0:T(8,128)(2,1)}, bf16[144,2048]{1,0:T(8,128)(2,1)S(1)}, u32[]{:S(2)}, u32[]{:S(2)}) collective-permute-start(bf16[144,2048]{1,0:T(8,128)(2,1)} %shard_map.122.rest_0_.left_ref), channel_id=1, source_target_pairs={{0,1},{3,2},{4,5},{7,6},{8,9},{11,10},{12,13},{15,14},{16,17},{19,... | collective-permute-start | bytes 1769480 | tf_op jit(solution)/shard_map/ppermute | solution.py:582
  15.4 19.8 %collective-permute-start.2 = (bf16[128,2048]{1,0:T(8,128)(2,1)S(1)}, bf16[128,2048]{1,0:T(8,128)(2,1)S(1)}, u32[]{:S(2)}, u32[]{:S(2)}) collective-permute-start(bf16[128,2048]{1,0:T(8,128)(2,1)S(1)} %shard_map.123.rest_0_.left_ref), channel_id=1, source_target_pairs={{0,1},{3,2},{4,5},{7,6},{8,9},{11,10},{12,13},{15,14},{16,17},{19,... | collective-permute-start | bytes 1572872 | tf_op jit(solution)/shard_map/ppermute | solution.py:582
  24.7 20.1 %collective-permute-start.1 = (bf16[144,2048]{1,0:T(8,128)(2,1)S(1)}, bf16[144,2048]{1,0:T(8,128)(2,1)S(1)}, u32[]{:S(2)}, u32[]{:S(2)}) collective-permute-start(bf16[144,2048]{1,0:T(8,128)(2,1)S(1)} %shard_map.126._.left_ref), channel_id=1, source_target_pairs={{1,2},{2,1},{5,6},{6,5},{9,10},{10,9},{13,14},{14,13},{17,18},{18,... | collective-permute-start | bytes 1769480 | tf_op jit(solution)/shard_map/ppermute | solution.py:582
  25.4 21.4 %collective-permute-start.4 = (bf16[128,2048]{1,0:T(8,128)(2,1)S(1)}, bf16[128,2048]{1,0:T(8,128)(2,1)}, u32[]{:S(2)}, u32[]{:S(2)}) collective-permute-start(bf16[128,2048]{1,0:T(8,128)(2,1)S(1)} %shard_map.124.rest_0_.left_ref), channel_id=1, source_target_pairs={{0,1},{3,2},{4,5},{7,6},{8,9},{11,10},{12,13},{15,14},{16,17},{19,... | collective-permute-start | bytes 1572872 | tf_op jit(solution)/shard_map/ppermute | solution.py:582
  35.8 13.5 %collective-permute-start.7 = (bf16[128,2048]{1,0:T(8,128)(2,1)S(1)}, bf16[128,2048]{1,0:T(8,128)(2,1)}, u32[]{:S(2)}, u32[]{:S(2)}) collective-permute-start(bf16[128,2048]{1,0:T(8,128)(2,1)S(1)} %shard_map.127._.left_ref), channel_id=1, source_target_pairs={{1,2},{2,1},{5,6},{6,5},{9,10},{10,9},{13,14},{14,13},{17,18},{18,... | collective-permute-start | bytes 1572872 | tf_op jit(solution)/shard_map/ppermute | solution.py:582
  37.3 19.2 %collective-permute-start.6 = (bf16[128,2048]{1,0:T(8,128)(2,1)S(1)}, bf16[128,2048]{1,0:T(8,128)(2,1)}, u32[]{:S(2)}, u32[]{:S(2)}) collective-permute-start(bf16[128,2048]{1,0:T(8,128)(2,1)S(1)} %shard_map.125._.left_ref), channel_id=1, source_target_pairs={{0,1},{3,2},{4,5},{7,6},{8,9},{11,10},{12,13},{15,14},{16,17},{19,... | collective-permute-start | bytes 1572872 | tf_op jit(solution)/shard_map/ppermute | solution.py:582
  45.5 18.2 %collective-permute-start.3 = (bf16[144,2048]{1,0:T(8,128)(2,1)S(1)}, bf16[144,2048]{1,0:T(8,128)(2,1)S(1)}, u32[]{:S(2)}, u32[]{:S(2)}) collective-permute-start(bf16[144,2048]{1,0:T(8,128)(2,1)S(1)} %shard_map.128._.refs_0_), channel_id=1, source_target_pairs={{1,0},{2,3},{5,4},{6,7},{9,8},{10,11},{13,12},{14,15},{17,16},{18,... | collective-permute-start | bytes 1769480 | tf_op jit(solution)/shard_map/ppermute | solution.py:582
  48.6 10.4 %collective-permute-start.5 = (bf16[128,2048]{1,0:T(8,128)(2,1)S(1)}, bf16[128,2048]{1,0:T(8,128)(2,1)S(1)}, u32[]{:S(2)}, u32[]{:S(2)}) collective-permute-start(bf16[128,2048]{1,0:T(8,128)(2,1)S(1)} %shard_map.129._.left_ref), channel_id=1, source_target_pairs={{1,2},{2,1},{5,6},{6,5},{9,10},{10,9},{13,14},{14,13},{17,18},{18,... | collective-permute-start | bytes 1572872 | tf_op jit(solution)/shard_map/ppermute | solution.py:582
  51.0 20.1 %collective-permute-start.11 = (bf16[128,2048]{1,0:T(8,128)(2,1)S(1)}, bf16[128,2048]{1,0:T(8,128)(2,1)S(1)}, u32[]{:S(2)}, u32[]{:S(2)}) collective-permute-start(bf16[128,2048]{1,0:T(8,128)(2,1)S(1)} %shard_map.130._.refs_0_), channel_id=1, source_target_pairs={{1,0},{2,3},{5,4},{6,7},{9,8},{10,11},{13,12},{14,15},{17,16},{18,... | collective-permute-start | bytes 1572872 | tf_op jit(solution)/shard_map/ppermute | solution.py:582
  58.2 19.0 %collective-permute-start.16 = (bf16[128,2048]{1,0:T(8,128)(2,1)S(1)}, bf16[128,2048]{1,0:T(8,128)(2,1)S(1)}, u32[]{:S(2)}, u32[]{:S(2)}) collective-permute-start(bf16[128,2048]{1,0:T(8,128)(2,1)S(1)} %shard_map.131._.left_ref), channel_id=1, source_target_pairs={{1,2},{2,1},{5,6},{6,5},{9,10},{10,9},{13,14},{14,13},{17,18},{18,... | collective-permute-start | bytes 1572872 | tf_op jit(solution)/shard_map/ppermute | solution.py:582
  65.0 8.7 %collective-permute-start.8 = (bf16[40,2176]{1,0:T(8,128)(2,1)S(1)}, bf16[40,2176]{1,0:T(8,128)(2,1)S(1)}, u32[]{:S(2)}, u32[]{:S(2)}) collective-permute-start(bf16[40,2176]{1,0:T(8,128)(2,1)S(1)} %get-tuple-element.80), channel_id=1, source_target_pairs={{0,4},{4,0},{8,12},{12,8},{1,5},{5,1},{9,13},{13,9},{2,6},{6,2},{1... | collective-permute-start | bytes 522248 | tf_op jit(solution)/shard_map/ppermute | solution.py:588
  65.1 8.7 %collective-permute-start.9 = (bf16[40,2176]{1,0:T(8,128)(2,1)S(1)}, bf16[40,2176]{1,0:T(8,128)(2,1)S(1)}, u32[]{:S(2)}, u32[]{:S(2)}) collective-permute-start(bf16[40,2176]{1,0:T(8,128)(2,1)S(1)} %get-tuple-element.81), channel_id=1, source_target_pairs={{0,8},{4,12},{8,0},{12,4},{1,9},{5,13},{9,1},{13,5},{2,10},{6,14},... | collective-permute-start | bytes 522248 | tf_op jit(solution)/shard_map/ppermute | solution.py:588
  66.7 8.5 %collective-permute-start.10 = (bf16[40,2176]{1,0:T(8,128)(2,1)S(1)}, bf16[40,2176]{1,0:T(8,128)(2,1)S(1)}, u32[]{:S(2)}, u32[]{:S(2)}) collective-permute-start(bf16[40,2176]{1,0:T(8,128)(2,1)S(1)} %get-tuple-element.82), channel_id=1, source_target_pairs={{0,12},{4,8},{8,4},{12,0},{1,13},{5,9},{9,5},{13,1},{2,14},{6,10},... | collective-permute-start | bytes 522248 | tf_op jit(solution)/shard_map/ppermute | solution.py:588
  71.1 12.5 %collective-permute-start.15 = (bf16[128,2048]{1,0:T(8,128)(2,1)S(1)}, bf16[128,2048]{1,0:T(8,128)(2,1)S(1)}, u32[]{:S(2)}, u32[]{:S(2)}) collective-permute-start(bf16[128,2048]{1,0:T(8,128)(2,1)S(1)} %shard_map.132.refs_5_.refs_0_), channel_id=1, source_target_pairs={{1,0},{2,3},{5,4},{6,7},{9,8},{10,11},{13,12},{14,15},{17,16},{18,... | collective-permute-start | bytes 1572872 | tf_op jit(solution)/shard_map/ppermute | solution.py:582
  77.9 16.5 %collective-permute-start.20 = (bf16[128,2048]{1,0:T(8,128)(2,1)S(1)}, bf16[128,2048]{1,0:T(8,128)(2,1)S(1)}, u32[]{:S(2)}, u32[]{:S(2)}) collective-permute-start(bf16[128,2048]{1,0:T(8,128)(2,1)S(1)} %shard_map.136.refs_8_.refs_0_), channel_id=1, source_target_pairs={{1,0},{2,3},{5,4},{6,7},{9,8},{10,11},{13,12},{14,15},{17,16},{18,... | collective-permute-start | bytes 1572872 | tf_op jit(solution)/shard_map/ppermute | solution.py:582
  81.2 8.5 %collective-permute-start.14 = (bf16[40,2176]{1,0:T(8,128)(2,1)S(1)}, bf16[40,2176]{1,0:T(8,128)(2,1)S(1)}, u32[]{:S(2)}, u32[]{:S(2)}) collective-permute-start(bf16[40,2176]{1,0:T(8,128)(2,1)S(1)} %get-tuple-element.90), channel_id=1, source_target_pairs={{0,12},{4,8},{8,4},{12,0},{1,13},{5,9},{9,5},{13,1},{2,14},{6,10},... | collective-permute-start | bytes 522248 | tf_op jit(solution)/shard_map/ppermute | solution.py:588
  85.0 12.4 %collective-permute-start.17 = (bf16[40,2176]{1,0:T(8,128)(2,1)S(1)}, bf16[40,2176]{1,0:T(8,128)(2,1)S(1)}, u32[]{:S(2)}, u32[]{:S(2)}) collective-permute-start(bf16[40,2176]{1,0:T(8,128)(2,1)S(1)} %get-tuple-element.99), channel_id=1, source_target_pairs={{0,4},{4,0},{8,12},{12,8},{1,5},{5,1},{9,13},{13,9},{2,6},{6,2},{1... | collective-permute-start | bytes 522248 | tf_op jit(solution)/shard_map/ppermute | solution.py:588
  85.1 12.6 %collective-permute-start.18 = (bf16[40,2176]{1,0:T(8,128)(2,1)S(1)}, bf16[40,2176]{1,0:T(8,128)(2,1)S(1)}, u32[]{:S(2)}, u32[]{:S(2)}) collective-permute-start(bf16[40,2176]{1,0:T(8,128)(2,1)S(1)} %get-tuple-element.100), channel_id=1, source_target_pairs={{0,8},{4,12},{8,0},{12,4},{1,9},{5,13},{9,1},{13,5},{2,10},{6,14},... | collective-permute-start | bytes 522248 | tf_op jit(solution)/shard_map/ppermute | solution.py:588
  86.9 10.8 %collective-permute-start.19 = (bf16[40,2176]{1,0:T(8,128)(2,1)S(1)}, bf16[40,2176]{1,0:T(8,128)(2,1)S(1)}, u32[]{:S(2)}, u32[]{:S(2)}) collective-permute-start(bf16[40,2176]{1,0:T(8,128)(2,1)S(1)} %get-tuple-element.101), channel_id=1, source_target_pairs={{0,12},{4,8},{8,4},{12,0},{1,13},{5,9},{9,5},{13,1},{2,14},{6,10},... | collective-permute-start | bytes 522248 | tf_op jit(solution)/shard_map/ppermute | solution.py:588
  95.8 7.3 %collective-permute-start.22 = (bf16[40,2176]{1,0:T(8,128)(2,1)S(1)}, bf16[40,2176]{1,0:T(8,128)(2,1)S(1)}, u32[]{:S(2)}, u32[]{:S(2)}) collective-permute-start(bf16[40,2176]{1,0:T(8,128)(2,1)S(1)} %get-tuple-element.111), channel_id=1, source_target_pairs={{0,8},{4,12},{8,0},{12,4},{1,9},{5,13},{9,1},{13,5},{2,10},{6,14},... | collective-permute-start | bytes 522248 | tf_op jit(solution)/shard_map/ppermute | solution.py:588
  97.4 8.6 %collective-permute-start.23 = (bf16[40,2176]{1,0:T(8,128)(2,1)S(1)}, bf16[40,2176]{1,0:T(8,128)(2,1)S(1)}, u32[]{:S(2)}, u32[]{:S(2)}) collective-permute-start(bf16[40,2176]{1,0:T(8,128)(2,1)S(1)} %get-tuple-element.112), channel_id=1, source_target_pairs={{0,12},{4,8},{8,4},{12,0},{1,13},{5,9},{9,5},{13,1},{2,14},{6,10},... | collective-permute-start | bytes 522248 | tf_op jit(solution)/shard_map/ppermute | solution.py:588
  132.4 8.9 %collective-permute-start.38 = (bf16[40,2048]{1,0:T(8,128)(2,1)S(1)}, bf16[40,2048]{1,0:T(8,128)(2,1)S(1)}, u32[]{:S(2)}, u32[]{:S(2)}) collective-permute-start(bf16[40,2048]{1,0:T(8,128)(2,1)S(1)} %get-tuple-element.138), channel_id=1, source_target_pairs={{0,12},{4,8},{8,4},{12,0},{1,13},{5,9},{9,5},{13,1},{2,14},{6,10},... | collective-permute-start | bytes 491528 | tf_op jit(solution)/shard_map/ppermute | solution.py:588
  142.2 20.7 %collective-permute-start.39 = (bf16[128,2048]{1,0:T(8,128)(2,1)S(1)}, bf16[128,2048]{1,0:T(8,128)(2,1)S(1)}, u32[]{:S(2)}, u32[]{:S(2)}) collective-permute-start(bf16[128,2048]{1,0:T(8,128)(2,1)S(1)} %get-tuple-element.143), channel_id=1, source_target_pairs={{0,1},{3,2},{4,5},{7,6},{8,9},{11,10},{12,13},{15,14},{16,17},{19,... | collective-permute-start | bytes 1572872 | tf_op jit(solution)/shard_map/ppermute | solution.py:582
  146.0 9.1 %collective-permute-start.35 = (bf16[40,2048]{1,0:T(8,128)(2,1)S(1)}, bf16[40,2048]{1,0:T(8,128)(2,1)S(1)}, u32[]{:S(2)}, u32[]{:S(2)}) collective-permute-start(bf16[40,2048]{1,0:T(8,128)(2,1)S(1)} %get-tuple-element.135), channel_id=1, source_target_pairs={{0,12},{4,8},{8,4},{12,0},{1,13},{5,9},{9,5},{13,1},{2,14},{6,10},... | collective-permute-start | bytes 491528 | tf_op jit(solution)/shard_map/ppermute | solution.py:588
  147.3 10.0 %collective-permute-start.40 = (bf16[40,2048]{1,0:T(8,128)(2,1)S(1)}, bf16[40,2048]{1,0:T(8,128)(2,1)S(1)}, u32[]{:S(2)}, u32[]{:S(2)}) collective-permute-start(bf16[40,2048]{1,0:T(8,128)(2,1)S(1)} %get-tuple-element.144), channel_id=1, source_target_pairs={{0,4},{4,0},{8,12},{12,8},{1,5},{5,1},{9,13},{13,9},{2,6},{6,2},{1... | collective-permute-start | bytes 491528 | tf_op jit(solution)/shard_map/ppermute | solution.py:588
  147.6 11.9 %collective-permute-start.41 = (bf16[40,2048]{1,0:T(8,128)(2,1)S(1)}, bf16[40,2048]{1,0:T(8,128)(2,1)S(1)}, u32[]{:S(2)}, u32[]{:S(2)}) collective-permute-start(bf16[40,2048]{1,0:T(8,128)(2,1)S(1)} %get-tuple-element.145), channel_id=1, source_target_pairs={{0,8},{4,12},{8,0},{12,4},{1,9},{5,13},{9,1},{13,5},{2,10},{6,14},... | collective-permute-start | bytes 491528 | tf_op jit(solution)/shard_map/ppermute | solution.py:588
  152.5 9.6 %collective-permute-start.42 = (bf16[40,2048]{1,0:T(8,128)(2,1)S(1)}, bf16[40,2048]{1,0:T(8,128)(2,1)S(1)}, u32[]{:S(2)}, u32[]{:S(2)}) collective-permute-start(bf16[40,2048]{1,0:T(8,128)(2,1)S(1)} %get-tuple-element.146), channel_id=1, source_target_pairs={{0,12},{4,8},{8,4},{12,0},{1,13},{5,9},{9,5},{13,1},{2,14},{6,10},... | collective-permute-start | bytes 491528 | tf_op jit(solution)/shard_map/ppermute | solution.py:588
  155.9 19.5 %collective-permute-start.44 = (bf16[128,2048]{1,0:T(8,128)(2,1)S(1)}, bf16[128,2048]{1,0:T(8,128)(2,1)S(1)}, u32[]{:S(2)}, u32[]{:S(2)}) collective-permute-start(bf16[128,2048]{1,0:T(8,128)(2,1)S(1)} %get-tuple-element.148), channel_id=1, source_target_pairs={{0,1},{3,2},{4,5},{7,6},{8,9},{11,10},{12,13},{15,14},{16,17},{19,... | collective-permute-start | bytes 1572872 | tf_op jit(solution)/shard_map/ppermute | solution.py:582
  163.6 13.2 %collective-permute-start.43 = (bf16[128,2048]{1,0:T(8,128)(2,1)S(1)}, bf16[128,2048]{1,0:T(8,128)(2,1)S(1)}, u32[]{:S(2)}, u32[]{:S(2)}) collective-permute-start(bf16[128,2048]{1,0:T(8,128)(2,1)S(1)} %shard_map.155._), channel_id=1, source_target_pairs={{1,2},{2,1},{5,6},{6,5},{9,10},{10,9},{13,14},{14,13},{17,18},{18,... | collective-permute-start | bytes 1572872 | tf_op jit(solution)/shard_map/ppermute | solution.py:582
  165.0 8.8 %collective-permute-start.47 = (bf16[40,2048]{1,0:T(8,128)(2,1)S(1)}, bf16[40,2048]{1,0:T(8,128)(2,1)S(1)}, u32[]{:S(2)}, u32[]{:S(2)}) collective-permute-start(bf16[40,2048]{1,0:T(8,128)(2,1)S(1)} %get-tuple-element.151), channel_id=1, source_target_pairs={{0,12},{4,8},{8,4},{12,0},{1,13},{5,9},{9,5},{13,1},{2,14},{6,10},... | collective-permute-start | bytes 491528 | tf_op jit(solution)/shard_map/ppermute | solution.py:588
  166.2 15.4 %collective-permute-start.48 = (bf16[128,2048]{1,0:T(8,128)(2,1)S(1)}, bf16[128,2048]{1,0:T(8,128)(2,1)S(1)}, u32[]{:S(2)}, u32[]{:S(2)}) collective-permute-start(bf16[128,2048]{1,0:T(8,128)(2,1)S(1)} %get-tuple-element.155), channel_id=1, source_target_pairs={{0,1},{3,2},{4,5},{7,6},{8,9},{11,10},{12,13},{15,14},{16,17},{19,... | collective-permute-start | bytes 1572872 | tf_op jit(solution)/shard_map/ppermute | solution.py:582
  177.4 17.5 %collective-permute-start.50 = (bf16[128,2048]{1,0:T(8,128)(2,1)S(1)}, bf16[128,2048]{1,0:T(8,128)(2,1)S(1)}, u32[]{:S(2)}, u32[]{:S(2)}) collective-permute-start(bf16[128,2048]{1,0:T(8,128)(2,1)S(1)} %shard_map.158._), channel_id=1, source_target_pairs={{1,0},{2,3},{5,4},{6,7},{9,8},{10,11},{13,12},{14,15},{17,16},{18,... | collective-permute-start | bytes 1572872 | tf_op jit(solution)/shard_map/ppermute | solution.py:582
  (30 other events, 197.2 us)
